TPU v7x, 256 devices: a whole 4x4x8 slice. The times are simulated.
256 devices in a mesh: ctx: 32 (over x, y, core), tp: 8 (over z).
Axes of the slice: x: 4, y: 4, z: 8, core: 2. Of those that a mesh axis runs over, the one named last changes fastest.
Arguments:
- queries: bfloat16 [2, 8, 64, 128], P(None, None, 'tp'), may hold values from -128 to 128
- new_kv: bfloat16 [2, 2, 8, 8, 128], P(None, None, None, 'tp'), may hold values from -16 to 16
- long_cache: bfloat16 [2, 8, 16384, 8, 128], P(None, None, 'ctx', 'tp'), may hold values from -6 to 6
- short_cache: bfloat16 [2, 8, 256, 8, 128], P(None, None, None, 'tp'), may hold values from -6 to 6
- lengths: int32 [8], replicated, may hold values from 4096 to 16384, as said below
- residual: bfloat16 [2, 8, 8192], P(None, None, 'ctx'), may hold values from -12 to 12
- out_weight: bfloat16 [8192, 8192], P('tp', 'ctx'), may hold values from -0.0625 to 0.0625
- final_gain: float32 [8192], P('ctx'), may hold values from 1 to 96
- head_weight: bfloat16 [8192, 128256], P('ctx', 'tp'), may hold values from -0.0625 to 0.0625
- targets: int32 [8], replicated, may hold values from 0 to 128255
Outputs:
- scores: float32 [8, 128256], P(None, ('tp', 'ctx'))
- chosen: float32 [8], replicated
Inputs may be any that keep to these rules, and one draw needn't show every extreme that they name: Row b's cached context is its first lengths[b] positions; in every draw some row holds 16384 positions.
All inputs are finite; a program needn't handle non-finite values.
Results may differ from a plain program's by a relative error of at most 0.00098.
Values sent between devices are 32-bit elements; how exact they have to be, the bound alone decides.
No kernel may reach another device: no remote copies, remote signals or barrier semaphores. Data moves between devices by JAX's collectives and lax.ppermute only.
A program may use at most 64 MiB of HBM per device.

v0:
```python
import jax
import jax.numpy as jnp
from jax import lax
from jax.sharding import PartitionSpec as P

D = 8192
HEAD_DIM = 128


NEG_FILL = -1e30
NORM_EPS = 1e-05
CONTRAST_WEIGHT = 0.5
LOG_FLOOR = -2.302585092994046


def combined_all(value, axis, combine):
    everything = jax.tree.map(lambda part: lax.all_gather(part, axis), value)
    initial = jax.tree.map(lambda part: part[0], everything)

    def step(k, so_far):
        return combine(so_far, jax.tree.map(lambda part: part[k], everything))

    return lax.fori_loop(1, lax.axis_size(axis), step, initial)


def local_block(query_matrix_rows, key_matrix_rows, value_rows, usable):
    score_scale = HEAD_DIM ** (-0.5)
    scores = (
        jnp.einsum(
            "bkgd,btkd->bkgt",
            query_matrix_rows,
            key_matrix_rows,
            preferred_element_type=jnp.float32,
        )
        * score_scale
    )
    mask = usable[:, None, None, :]
    masked = jnp.where(mask, scores, NEG_FILL)
    peak_local = jnp.max(masked, axis=-1)
    weights = jnp.where(mask, jnp.exp(masked - peak_local[..., None]), 0.0)
    totals = jnp.sum(weights, axis=-1)
    output = jnp.einsum(
        "bkgt,btkd->bkgd",
        weights.astype(jnp.bfloat16),
        value_rows,
        preferred_element_type=jnp.float32,
    )
    return (peak_local, totals, output)


def finish_branch(peak_all, totals, output, query_matrix_rows, incoming_key, value_new):
    score_scale = HEAD_DIM ** (-0.5)
    own = (
        jnp.einsum(
            "faew,faw->fae", query_matrix_rows, incoming_key, preferred_element_type=jnp.float32
        )
        * score_scale
    )
    final = jnp.maximum(peak_all, own)
    older = jnp.exp(peak_all - final)
    newer = jnp.exp(own - final)
    mixed = (
        output * older[..., None] + newer[..., None] * value_new.astype(jnp.float32)[:, :, None, :]
    )
    return (mixed / (totals * older + newer)[..., None]).astype(jnp.bfloat16)


def vocab_local(branch_logits, column_start, targets):
    peak_local = jnp.max(branch_logits, axis=-1)
    totals = jnp.sum(jnp.exp(branch_logits - peak_local[..., None]), axis=-1)
    columns = column_start + jnp.arange(branch_logits.shape[-1], dtype=jnp.int32)
    target_hit = columns[None, :] == targets[:, None]
    picks = jnp.sum(jnp.where(target_hit[None], branch_logits, 0.0), axis=-1)
    return (peak_local, totals, picks)


def join_stats(first_part, second_part):
    peak_both = jnp.maximum(first_part[0], second_part[0])
    totals = first_part[1] * jnp.exp(first_part[0] - peak_both) + second_part[1] * jnp.exp(
        second_part[0] - peak_both
    )
    return (peak_both, totals, first_part[2] + second_part[2])


def per_device(
    queries,
    new_kv,
    long_cache,
    short_cache,
    lengths,
    residual,
    out_weight,
    final_gain,
    head_weight,
    targets,
):
    row_count = queries.shape[1]
    heads_here = queries.shape[2]
    kv_here = long_cache.shape[3]
    block_len = long_cache.shape[2]
    group_size = heads_here // kv_here
    width_here = residual.shape[2]
    vocab_here = head_weight.shape[1]
    grouped_query_heads = queries.reshape(2, row_count, kv_here, group_size, HEAD_DIM)
    position = lax.axis_index("ctx") * block_len + jnp.arange(block_len, dtype=jnp.int32)
    long_usable = position[None, :] < lengths[:, None]
    peak_local, totals, output = local_block(
        grouped_query_heads[0], long_cache[0], long_cache[1], long_usable
    )
    peak_all = lax.pmax(peak_local, "ctx")
    factor = jnp.exp(peak_local - peak_all)
    totals, output = lax.psum((totals * factor, output * factor[..., None]), "ctx")
    with_context = finish_branch(
        peak_all, totals, output, grouped_query_heads[0], new_kv[0, 0], new_kv[0, 1]
    )
    short_usable = jnp.ones((row_count, short_cache.shape[2]), dtype=bool)
    short_peak, short_totals, short_output = local_block(
        grouped_query_heads[1], short_cache[0], short_cache[1], short_usable
    )
    context_free = finish_branch(
        short_peak, short_totals, short_output, grouped_query_heads[1], new_kv[1, 0], new_kv[1, 1]
    )
    attended = jnp.stack([with_context, context_free]).reshape(2 * row_count, heads_here * HEAD_DIM)
    projected = jnp.dot(attended, out_weight, preferred_element_type=jnp.float32)
    projected = lax.psum(projected, "tp")
    stream = residual.reshape(2 * row_count, width_here).astype(jnp.float32) + projected
    squares = jnp.sum(stream * stream, axis=-1)
    scaled = (stream * final_gain).astype(jnp.bfloat16)
    partial_value = jnp.dot(scaled, head_weight, preferred_element_type=jnp.float32)
    total_squares = lax.psum(squares, "ctx")
    local_logits = lax.psum_scatter(partial_value, "ctx", scatter_dimension=1, tiled=True)
    share_width = local_logits.shape[1]
    inverse = lax.rsqrt(total_squares / D + NORM_EPS)
    local_logits = (local_logits * inverse[:, None]).reshape(2, row_count, share_width)
    column_start = lax.axis_index("tp") * vocab_here + lax.axis_index("ctx") * share_width
    stats = vocab_local(local_logits, column_start, targets)
    vocab_peak, vocab_totals, picks = combined_all(stats, ("ctx", "tp"), join_stats)
    lse = vocab_peak + jnp.log(vocab_totals)
    logp = local_logits - lse[..., None]
    scores = (
        (1.0 + CONTRAST_WEIGHT) * logp[0]
        - CONTRAST_WEIGHT * logp[1]
        + jnp.minimum(0.0, local_logits[0] - vocab_peak[0][:, None] - LOG_FLOOR)
    )
    picked_logp = picks - lse
    chosen = (
        (1.0 + CONTRAST_WEIGHT) * picked_logp[0]
        - CONTRAST_WEIGHT * picked_logp[1]
        + jnp.minimum(0.0, picks[0] - vocab_peak[0] - LOG_FLOOR)
    )
    return (scores, chosen)


def solution(mesh):
    placed = (
        P(None, None, "tp", None),
        P(None, None, None, "tp", None),
        P(None, None, "ctx", "tp", None),
        P(None, None, None, "tp", None),
        P(),
        P(None, None, "ctx"),
        P("tp", "ctx"),
        P("ctx"),
        P("ctx", "tp"),
        P(),
    )
    return jax.shard_map(
        per_device,
        mesh=mesh,
        in_specs=placed,
        out_specs=(P(None, ("tp", "ctx")), P()),
        check_vma=False,
    )
```

profile of v0, /device:TPU:1, one launch (start us, length us, event | category | flops | bytes accessed | tf_op | source)
XLA Modules:
  0.0 563.5 jit_solution(15784351988773118303)
XLA Ops:
  7.2 0.9 bitcast_convert_fusion.1
  8.1 1.4 fusion.57
  9.5 0.9 fusion.26
  10.4 0.7 broadcast_compare_fusion.1
  11.1 1.7 fusion.58
  12.8 65.3 %pmax.7 = f32[8,1,8]{2,0,1:T(8,128)S(1)} all-reduce(f32[8,1,8]{2,0,1:T(8,128)S(1)} %bitcast.149), channel_id=1, replica_groups=mesh['ctx'=32,'tp'=8] {'ctx'}, use_global_device_ids=true, to_apply=%region_1.2 | all-reduce | flops 64 | bytes 512 | tf_op jit(solution)/shard_map/pmax | solution.py:110
  78.1 0.8 fusion.29
  78.9 0.2 fusion.8
  79.1 0.3 fusion.3
  79.4 0.2 fusion.14
  79.6 121.7 %all-reduce.1 = (f32[8,1,8]{2,0,1:T(8,128)S(1)}, f32[8,1,8,128]{3,2,0,1:T(8,128)S(1)}) all-reduce(f32[8,1,8]{2,0,1:T(8,128)S(1)} %get-tuple-element.219, f32[8,1,8,128]{3,2,0,1:T(8,128)S(1)} %fusion.3), channel_id=1, replica_groups=mesh['ctx'=32,'tp'=8] {'ctx'}, use_global_device_ids=true, to_apply=%region_4.5 | all-reduce | flops 8256 | bytes 66048 | tf_op jit(solution)/shard_map/psum | solution.py:112
  201.3 1.3 fusion.7
  202.6 0.1 fusion.32
  202.7 0.2 fusion.17
  202.9 25.5 %psum.30 = f32[16,256]{1,0:T(8,128)S(1)} all-reduce(f32[16,256]{1,0:T(8,128)S(1)} %fusion.17), channel_id=1, replica_groups=mesh['ctx'=32,'tp'=8] {'tp'}, use_global_device_ids=true, to_apply=%region_7.8 | all-reduce | flops 4096 | bytes 32768 | tf_op jit(solution)/shard_map/psum | solution.py:125
  228.4 6.6 %fusion.37 = f32[16,16032]{1,0:T(8,128)} fusion(bf16[256,16032]{0,1:T(8,128)(2,1)} %param.20, f32[16,256]{1,0:T(8,128)S(1)} %psum.30, bf16[2,8,256]{2,1,0:T(8,128)(2,1)S(1)} %copy-done.2, f32[256]{0:T(256)S(1)} %copy-done.3), kind=kOutput, calls=%fused_computation.62 | convolution fusion | flops 131350528 | bytes 9260032 | tf_op jit(solution)/shard_map/dot_general | solution.py:129
  235.1 0.1 multiply_reduce_fusion
  235.2 74.9 %psum.31 = f32[16]{0:T(128)S(1)} all-reduce(f32[16]{0:T(128)S(1)} %multiply_reduce_fusion), channel_id=1, replica_groups=mesh['ctx'=32,'tp'=8] {'ctx'}, use_global_device_ids=true, to_apply=%region_10.11 | all-reduce | flops 16 | bytes 128 | tf_op jit(solution)/shard_map/psum | solution.py:130
  310.2 0.6 dynamic-slice
  311.4 0.1 broadcast_compare_fusion
  311.5 43.9 %all-reduce.4.cloned.1.call-done = f32[16,16032]{1,0:T(8,128)} async-done(((f32[16,16032]{1,0:T(8,128)}), f32[16,16032]{1,0:T(8,128)}) %all-reduce.4.cloned.1.call-update) | async-done | bytes 1026064
  355.4 1.0 fusion.54
  356.4 0.1 all_gather.18
  356.4 62.9 %all_gather.19 = f32[256,2,8]{2,1,0:T(2,128)S(1)} all-gather(f32[1,2,8]{2,1,0:T(2,128)S(1)} %all_gather.18), channel_id=1, replica_groups=mesh['ctx'=32,'tp'=8] {'ctx','tp'}, dimensions={0}, use_global_device_ids=true | all-gather | bytes 16448 | tf_op jit(solution)/shard_map/all_gather | solution.py:17
  419.3 0.2 select_reduce_fusion
  419.5 0.1 all_gather.20
  419.6 61.2 %all_gather.21 = f32[256,2,8]{2,1,0:T(2,128)S(1)} all-gather(f32[1,2,8]{2,1,0:T(2,128)S(1)} %all_gather.20), channel_id=1, replica_groups=mesh['ctx'=32,'tp'=8] {'ctx','tp'}, dimensions={0}, use_global_device_ids=true | all-gather | bytes 16448 | tf_op jit(solution)/shard_map/all_gather | solution.py:17
  480.8 0.1 all_gather.22
  480.9 63.0 %all_gather.23 = f32[256,2,8]{2,1,0:T(2,128)S(1)} all-gather(f32[1,2,8]{2,1,0:T(2,128)S(1)} %all_gather.22), channel_id=1, replica_groups=mesh['ctx'=32,'tp'=8] {'ctx','tp'}, dimensions={0}, use_global_device_ids=true | all-gather | bytes 16448 | tf_op jit(solution)/shard_map/all_gather | solution.py:17
  543.9 11.5 %while.19 = (s32[]{:T(128)}, f32[2,8]{1,0:T(2,128)S(1)}, f32[2,8]{1,0:T(2,128)S(1)}, f32[2,8]{1,0:T(2,128)S(1)}, f32[256,2,8]{2,1,0:T(2,128)S(1)}, /*index=5*/f3...) while((s32[]{:T(128)}, f32[2,8]{1,0:T(2,128)S(1)}, ...), condition=%wide.region_15.16_spmd, body=%wide.region_14.15_spmd.sunk | while | flops 117 | bytes 723 | solution.py:23
  555.5 0.5 fusion.51
  556.0 0.7 fusion.23
  (282 shorter events, 6.9 us)
Async XLA Ops:
  7.2 195.6 %copy-start = (bf16[1024,256]{1,0:T(8,128)(2,1)S(1)}, bf16[1024,256]{1,0:T(8,128)(2,1)}, u32[]{:S(2)}) copy-start(bf16[1024,256]{1,0:T(8,128)(2,1)} %param.18) | copy-start | bytes 1572868
  7.2 71.9 %copy-start.1 = (bf16[2,8,512,1,128]{4,2,3,1,0:T(8,128)(2,1)S(1)}, bf16[2,8,512,1,128]{4,2,3,1,0:T(8,128)(2,1)}, u32[]{:S(2)}) copy-start(bf16[2,8,512,1,128]{4,2,3,1,0:T(8,128)(2,1)} %param.14) | copy-start | bytes 6291460
  7.2 348.2 %all-reduce.4.cloned.1.call-start = ((), (), s32[]{:S(2)}) async-start(), calls=%async_computation | async-start | bytes 2064384
  11.1 217.3 %copy-start.2 = (bf16[2,8,256]{2,1,0:T(8,128)(2,1)S(1)}, bf16[2,8,256]{2,1,0:T(8,128)(2,1)}, u32[]{:S(2)}) copy-start(bf16[2,8,256]{2,1,0:T(8,128)(2,1)} %param.17) | copy-start | bytes 24580
  11.1 217.3 %copy-start.3 = (f32[256]{0:T(256)S(1)}, f32[256]{0:T(256)}, u32[]{:S(2)}) copy-start(f32[256]{0:T(256)} %param.19) | copy-start | bytes 3076
  228.4 81.7 %copy-start.5 = (u32[256]{0:T(256)S(1)}, u32[256]{0:T(256)}, u32[]{:S(2)}) copy-start(u32[256]{0:T(256)} %constant.87) | copy-start | bytes 3076
  228.4 83.0 %copy-start.4 = (s32[8]{0:T(128)S(1)}, s32[8]{0:T(128)}, u32[]{:S(2)}) copy-start(s32[8]{0:T(128)} %param.21) | copy-start | bytes 100
Sparse Core Ops, SparseCore 0:
  235.2 120.1 all-reduce.3
where the time goes:
time: 565 us; the launch traced here: 564 us
  blocking collectives  474 us (84%)
  waiting for transfers between devices  43.9 us (8%)
  between operations  14.8 us (3%)
  matrix products  13.2 us (2%)
  other arithmetic  11.4 us (2%)
    all_gather x3, blocking collectives, combined_all(): everything = jax.tree.map(lambda part: lax.all_gather(part, axis), value)  187 us
    psum x1, blocking collectives, per_device(): lax.psum((totals * factor, output * factor[..., None]), 'ctx')  122 us
    psum x1, blocking collectives, per_device(): total_squares = lax.psum(squares, 'ctx')  74.9 us
    pmax x1, blocking collectives, per_device(): peak_all = lax.pmax(peak_local, 'ctx')  65.3 us
    unnamed x2, waiting for transfers between devices  43.9 us
    psum x1, blocking collectives, per_device(): projected = lax.psum(projected, 'tp')  25.5 us
  transfers between devices with their start and end apart: 1, of which 1 were waited for; matrix products, arithmetic and copies ran while one was open for 0% of the time, Pallas kernels for 0%

commit v1 on v0

--- a/solution.py
+++ b/solution.py
@@ -13,14 +13,20 @@
 LOG_FLOOR = -2.302585092994046
 
 
-def combined_all(value, axis, combine):
-    everything = jax.tree.map(lambda part: lax.all_gather(part, axis), value)
-    initial = jax.tree.map(lambda part: part[0], everything)
-
-    def step(k, so_far):
-        return combine(so_far, jax.tree.map(lambda part: part[k], everything))
-
-    return lax.fori_loop(1, lax.axis_size(axis), step, initial)
+CTX_STEPS = (1, 2, 6, 8, 24)
+
+
+def swap(value, mask):
+    size = lax.axis_size("ctx")
+    return lax.ppermute(value, "ctx", [(i, i ^ mask) for i in range(size)])
+
+
+def merge_blocks(state, other):
+    peak_one, peak_two = state[:, 128:129], other[:, 128:129]
+    peak = jnp.maximum(peak_one, peak_two)
+    summed = state * jnp.exp(peak_one - peak) + other * jnp.exp(peak_two - peak)
+    lane = lax.broadcasted_iota(jnp.int32, state.shape, 1)
+    return jnp.where(lane == 128, peak, summed)
 
 
 def local_block(query_matrix_rows, key_matrix_rows, value_rows, usable):
@@ -72,14 +78,6 @@
     target_hit = columns[None, :] == targets[:, None]
     picks = jnp.sum(jnp.where(target_hit[None], branch_logits, 0.0), axis=-1)
     return (peak_local, totals, picks)
-
-
-def join_stats(first_part, second_part):
-    peak_both = jnp.maximum(first_part[0], second_part[0])
-    totals = first_part[1] * jnp.exp(first_part[0] - peak_both) + second_part[1] * jnp.exp(
-        second_part[0] - peak_both
-    )
-    return (peak_both, totals, first_part[2] + second_part[2])
 
 
 def per_device(
@@ -107,9 +105,20 @@
     peak_local, totals, output = local_block(
         grouped_query_heads[0], long_cache[0], long_cache[1], long_usable
     )
-    peak_all = lax.pmax(peak_local, "ctx")
-    factor = jnp.exp(peak_local - peak_all)
-    totals, output = lax.psum((totals * factor, output * factor[..., None]), "ctx")
+    state = jnp.concatenate(
+        [
+            output.reshape(-1, HEAD_DIM),
+            peak_local.reshape(-1, 1),
+            totals.reshape(-1, 1),
+            jnp.zeros((row_count * heads_here, HEAD_DIM - 2), jnp.float32),
+        ],
+        axis=1,
+    )
+    for mask in CTX_STEPS:
+        state = merge_blocks(state, swap(state, mask))
+    output = state[:, :HEAD_DIM].reshape(output.shape)
+    peak_all = state[:, HEAD_DIM].reshape(peak_local.shape)
+    totals = state[:, HEAD_DIM + 1].reshape(totals.shape)
     with_context = finish_branch(
         peak_all, totals, output, grouped_query_heads[0], new_kv[0, 0], new_kv[0, 1]
     )
@@ -122,19 +131,47 @@
     )
     attended = jnp.stack([with_context, context_free]).reshape(2 * row_count, heads_here * HEAD_DIM)
     projected = jnp.dot(attended, out_weight, preferred_element_type=jnp.float32)
-    projected = lax.psum(projected, "tp")
+    tp_size = lax.axis_size("tp")
+    spread = jnp.broadcast_to(projected[None], (tp_size,) + projected.shape)
+    projected = jnp.sum(lax.all_to_all(spread, "tp", 0, 0, tiled=True), axis=0)
     stream = residual.reshape(2 * row_count, width_here).astype(jnp.float32) + projected
     squares = jnp.sum(stream * stream, axis=-1)
     scaled = (stream * final_gain).astype(jnp.bfloat16)
     partial_value = jnp.dot(scaled, head_weight, preferred_element_type=jnp.float32)
-    total_squares = lax.psum(squares, "ctx")
-    local_logits = lax.psum_scatter(partial_value, "ctx", scatter_dimension=1, tiled=True)
-    share_width = local_logits.shape[1]
+    ctx_size = lax.axis_size("ctx")
+    share_width = vocab_here // ctx_size
+    padded_width = -(-(share_width + 1) // 128) * 128
+    rows = 2 * row_count
+    blocks = partial_value.reshape(rows, ctx_size, share_width).transpose(1, 0, 2)
+    extra = jnp.broadcast_to(
+        squares[None, :, None], (ctx_size, rows, padded_width - share_width)
+    )
+    blocks = jnp.concatenate([blocks, extra], axis=2)
+    blocks = blocks.reshape(ctx_size // 2, 2, rows, padded_width)
+    core = lax.axis_index("ctx") % 2
+    mine = lax.dynamic_index_in_dim(blocks, core, 1, keepdims=False)
+    theirs = lax.dynamic_index_in_dim(blocks, 1 - core, 1, keepdims=False)
+    mine = mine + swap(theirs, 1)
+    chips = [list(range(which, ctx_size, 2)) for which in range(2)]
+    received = lax.all_to_all(mine, "ctx", 0, 0, tiled=True, axis_index_groups=chips)
+    summed = jnp.sum(received, axis=0)
+    total_squares = summed[:, share_width]
+    local_logits = summed[:, :share_width]
     inverse = lax.rsqrt(total_squares / D + NORM_EPS)
     local_logits = (local_logits * inverse[:, None]).reshape(2, row_count, share_width)
     column_start = lax.axis_index("tp") * vocab_here + lax.axis_index("ctx") * share_width
     stats = vocab_local(local_logits, column_start, targets)
-    vocab_peak, vocab_totals, picks = combined_all(stats, ("ctx", "tp"), join_stats)
+    packed = jnp.stack([part.reshape(-1) for part in stats])
+    devices = ctx_size * tp_size
+    everyone = lax.all_to_all(
+        jnp.broadcast_to(packed[None], (devices,) + packed.shape), ("ctx", "tp"), 0, 0, tiled=True
+    )
+    vocab_peak = jnp.max(everyone[:, 0], axis=0)
+    vocab_totals = jnp.sum(everyone[:, 1] * jnp.exp(everyone[:, 0] - vocab_peak), axis=0)
+    picks = jnp.sum(everyone[:, 2], axis=0)
+    vocab_peak, vocab_totals, picks = (
+        part.reshape(2, row_count) for part in (vocab_peak, vocab_totals, picks)
+    )
     lse = vocab_peak + jnp.log(vocab_totals)
     logp = local_logits - lse[..., None]
     scores = (

time: 565 us -> 113 us (0.20)
  blocking collectives: 474 us -> 31.1 us
  starting transfers between devices: 0.04 us -> 23.8 us
  waiting for transfers between devices: 43.9 us -> 27.1 us
  between operations: 14.8 us -> 0.9 us
  local copies, waits for them, and re-layouts: 0.87 us -> 9.57 us
    psum x3 -> x0, blocking collectives: 222 us -> none  [the longest x1 122 us: per_device(): lax.psum((totals * factor, output * factor[..., None]), 'ctx')]
    all_gather x3 -> x0, blocking collectives: 187 us -> none  [combined_all(): everything = jax.tree.map(lambda part: lax.all_gather(part, axis), value)]
    pmax x1 -> x0, blocking collectives: 65.3 us -> none  [per_device(): peak_all = lax.pmax(peak_local, 'ctx')]
    unnamed x2 -> x0, waiting for transfers between devices: 43.9 us -> none
    all_to_all x0 -> x1, blocking collectives: none -> 31.1 us  [per_device(): lax.all_to_all(jnp.broadcast_to(packed[None], (devices,) + packed.shape),...]
    ppermute x0 -> x6, waiting for transfers between devices: none -> 16.8 us  [swap(): return lax.ppermute(value, 'ctx', [(i, i ^ mask) for i in range(size)])]
    all_to_all x0 -> x2, starting transfers between devices: none -> 12.8 us  [the longest x1 6.58 us: per_device(): projected = jnp.sum(lax.all_to_all(spread, 'tp', 0, 0, tiled=True), axis=0)]
    ppermute x0 -> x6, starting transfers between devices: none -> 11 us  [swap(): return lax.ppermute(value, 'ctx', [(i, i ^ mask) for i in range(size)])]
  transfers between devices with their start and end apart: 1 -> 8, of which waited for: 1 -> 7; matrix products, arithmetic and copies ran while one was open for 0% -> 12% of each run, Pallas kernels for 0% -> 0%
where the time goes in v1:
time: 113 us; the launch traced here: 112 us
  blocking collectives  31.1 us (28%)
  waiting for transfers between devices  27.1 us (24%)
  starting transfers between devices  23.8 us (21%)
  matrix products  13.3 us (12%)
  local copies, waits for them, and re-layouts  9.57 us (8%)
  other arithmetic  6.27 us (6%)
    all_to_all x1, blocking collectives, per_device(): lax.all_to_all(jnp.broadcast_to(packed[None], (devices,) + packed.shape),...  31.1 us
    ppermute x6, waiting for transfers between devices, swap(): return lax.ppermute(value, 'ctx', [(i, i ^ mask) for i in range(size)])  16.8 us
    ppermute x6, starting transfers between devices, swap(): return lax.ppermute(value, 'ctx', [(i, i ^ mask) for i in range(size)])  11 us
    all_to_all x1, waiting for transfers between devices, per_device(): lax.all_to_all(mine, 'ctx', 0, 0, tiled=True, axis_index_groups=chips)  10.3 us
    dot_general x1, local copies, waits for them, and re-layouts, per_device(): jnp.dot(scaled, head_weight, preferred_element_type=jnp.float32)  7.81 us
    all_to_all x1, starting transfers between devices, per_device(): projected = jnp.sum(lax.all_to_all(spread, 'tp', 0, 0, tiled=True), axis=0)  6.58 us
    all_to_all x1, starting transfers between devices, per_device(): lax.all_to_all(mine, 'ctx', 0, 0, tiled=True, axis_index_groups=chips)  6.25 us
    dot_general x1, matrix products, per_device(): jnp.dot(scaled, head_weight, preferred_element_type=jnp.float32)  5.59 us
  transfers between devices with their start and end apart: 8, of which 7 were waited for; matrix products, arithmetic and copies ran while one was open for 12% of the time, Pallas kernels for 0%

profile of v1, /device:TPU:1, one launch (start us, length us, event | category | flops | bytes accessed | tf_op | source)
XLA Modules:
  0.0 112.1 jit_solution(10629389210624865009)
XLA Ops:
  0.7 0.8 broadcast_compare_fusion.1
  1.4 1.7 %fusion.60 = (f32[8,8]{1,0:T(8,128)S(1)}, f32[8,8,512]{2,1,0:T(8,128)S(1)}) fusion(bf16[2,8,512,1,128]{4,2,1,3,0:T(8,128)(2,1)} %bitcast.145, bf16[2,8,8,128]{3,2,1,0:T(8,128)(2,1)} %param.10, pred[8,512]{1,0:T(8,128)(4,1)S(1)} %broadcast_compare_fusion.1), kind=kOutput, calls=%fused_computation.123 | convolution fusion | flops 8486848 | bytes 1200384 | tf_op jit(solution)/shard_map/bkgd,btkd->bkgt/dot_general | solution.py:35
  3.1 1.5 %convolution_bitcast_fusion.1 = f32[64,128]{1,0:T(8,128)S(1)} fusion(bf16[2,8,512,1,128]{4,2,1,3,0:T(8,128)(2,1)} %bitcast.146, f32[8,8,512]{2,1,0:T(8,128)S(1)} %get-tuple-element.41, f32[8,8]{1,0:T(8,128)S(1)} %get-tuple-element.40, pred[8,512]{1,0:T(8,128)(4,1)S(1)} %broadcast_compare_fusion.1), kind=kOutput, calls=%fused_computation.4 | convolution fusion | flops 8486912 | bytes 1216768 | tf_op jit(solution)/shard_map/bkgt,btkd->bkgd/dot_general | solution.py:48
  5.3 3.3 %collective-permute-start = (f32[64,256]{0,1:T(8,128)S(1)}, f32[64,256]{0,1:T(8,128)S(1)}, u32[]{:S(2)}, u32[]{:S(2)}) collective-permute-start(f32[64,256]{0,1:T(8,128)S(1)} %maximum_maximum_fusion), channel_id=1, source_target_pairs={{0,8},{8,0},{16,24},{24,16},{32,40},{40,32},{48,56},{56,48},{64,72... | collective-permute-start | bytes 196616 | tf_op jit(solution)/shard_map/ppermute | solution.py:21
  8.6 0.7 bitcast_convert_fusion.1
  9.4 0.8 fusion.29
  10.2 1.4 %fusion.59 = (f32[8,8]{1,0:T(8,128)S(1)}, f32[8,8,256]{2,1,0:T(8,128)S(1)}) fusion(bf16[2,8,256,1,128]{4,2,1,3,0:T(8,128)(2,1)} %bitcast.150, bf16[2,8,8,128]{3,2,1,0:T(8,128)(2,1)} %param.10), kind=kOutput, calls=%fused_computation.122 | convolution fusion | flops 4227008 | bytes 606464 | tf_op jit(solution)/shard_map/bkgd,btkd->bkgt/dot_general | solution.py:35
  11.9 0.8 fusion.26
  12.7 4.3 %collective-permute-done.1 = f32[64,256]{0,1:T(8,128)S(1)} collective-permute-done((f32[64,256]{0,1:T(8,128)S(1)}, f32[64,256]{0,1:T(8,128)S(1)}, u32[]{:S(2)}, u32[]{:S(2)}) %collective-permute-start.1) | collective-permute-done | bytes 65568 | tf_op jit(solution)/shard_map/ppermute | solution.py:21
  17.1 1.1 collective-permute-start.2
  18.3 4.3 %collective-permute-done.2 = f32[64,256]{0,1:T(8,128)S(1)} collective-permute-done((f32[64,256]{0,1:T(8,128)S(1)}, f32[64,256]{0,1:T(8,128)S(1)}, u32[]{:S(2)}, u32[]{:S(2)}) %collective-permute-start.2) | collective-permute-done | bytes 65568 | tf_op jit(solution)/shard_map/ppermute | solution.py:21
  22.8 3.8 %collective-permute-done.3 = f32[64,256]{0,1:T(8,128)S(1)} collective-permute-done((f32[64,256]{0,1:T(8,128)S(1)}, f32[64,256]{0,1:T(8,128)S(1)}, u32[]{:S(2)}, u32[]{:S(2)}) %collective-permute-start.3) | collective-permute-done | bytes 65568 | tf_op jit(solution)/shard_map/ppermute | solution.py:21
  26.8 1.0 collective-permute-start.4
  27.7 1.3 %fusion.4 = bf16[1,8,1,8,128]{4,3,1,2,0:T(8,128)(2,1)S(1)} fusion(bf16[2,8,256,1,128]{4,2,1,3,0:T(8,128)(2,1)} %bitcast.151, f32[8,8,256]{2,1,0:T(8,128)S(1)} %get-tuple-element.39, f32[8,8]{1,0:T(8,128)S(1)} %get-tuple-element.38, f32[8,8]{1,0:T(8,128)S(1)} %get-tuple-element.11, f32[8,128]{1,0:T(8,128)S(1)} %get-tuple-element.34, ...), kind=kOutput, calls=%fused_computation.9 | convolution fusion | flops 4268032 | bytes 611328 | tf_op jit(solution)/shard_map/bkgt,btkd->bkgd/dot_general | solution.py:48
  29.0 2.9 %collective-permute-done.4 = f32[64,256]{0,1:T(8,128)S(1)} collective-permute-done((f32[64,256]{0,1:T(8,128)S(1)}, f32[64,256]{0,1:T(8,128)S(1)}, u32[]{:S(2)}, u32[]{:S(2)}) %collective-permute-start.4) | collective-permute-done | bytes 65568 | tf_op jit(solution)/shard_map/ppermute | solution.py:21
  32.4 0.2 fusion.14
  32.6 0.7 broadcast_in_dim.140
  33.3 6.6 %all-to-all-start = ((f32[8,16,256]{2,1,0:T(8,128)}), f32[8,16,256]{2,1,0:T(8,128)S(1)}, u32[]{:S(2)}, u32[]{:S(2)}) async-start(f32[8,16,256]{2,1,0:T(8,128)} %broadcast_in_dim.140), calls=%async_computation | async-start | bytes 262144 | tf_op jit(solution)/shard_map/all_to_all | solution.py:136
  39.9 7.8 %dot_general.36 = bf16[32,501,256]{2,1,0:T(8,128)(2,1)} reshape(bf16[16032,256]{1,0:T(8,128)(2,1)} %bitcast.142) | data formatting | bytes 16416768 | tf_op jit(solution)/shard_map/dot_general | solution.py:140
  48.0 5.6 %convolution_bitcast_fusion = f32[32,16,501]{2,1,0:T(8,128)S(1)} fusion(bf16[32,501,256]{2,1,0:T(8,128)(2,1)} %dot_general.36, f32[16,256]{1,0:T(8,128)S(1)} %reduce_sum.85, bf16[2,8,256]{2,1,0:T(8,128)(2,1)S(1)} %copy-done.1, f32[256]{0:T(256)S(1)} %copy-done.2), kind=kOutput, calls=%fused_computation | convolution fusion | flops 131350528 | bytes 9260032 | tf_op jit(solution)/shard_map/dot_general | solution.py:140
  53.9 5.4 %collective-permute-start.5 = (f32[16,16,512]{2,1,0:T(8,128)S(1)}, f32[16,16,512]{2,1,0:T(8,128)S(1)}, u32[]{:S(2)}, u32[]{:S(2)}) collective-permute-start(f32[16,16,512]{2,1,0:T(8,128)S(1)} %dynamic-slice_bitcast_fusion), channel_id=1, source_target_pairs={{0,8},{8,0},{16,24},{24,16},{32,40},{40,32},{48,56},{56,48},{64,72... | collective-permute-start | bytes 1572872 | tf_op jit(solution)/shard_map/ppermute | solution.py:21
  59.3 1.5 %collective-permute-done.5 = f32[16,16,512]{2,1,0:T(8,128)S(1)} collective-permute-done((f32[16,16,512]{2,1,0:T(8,128)S(1)}, f32[16,16,512]{2,1,0:T(8,128)S(1)}, u32[]{:S(2)}, u32[]{:S(2)}) %collective-permute-start.5) | collective-permute-done | bytes 524320 | tf_op jit(solution)/shard_map/ppermute | solution.py:21
  60.9 0.9 bitcast_add_fusion
  61.8 6.2 %all-to-all-start.1 = ((f32[16,16,512]{2,1,0:T(8,128)}), f32[16,16,512]{2,1,0:T(8,128)S(1)}, u32[]{:S(2)}, u32[]{:S(2)}) async-start(f32[16,16,512]{2,1,0:T(8,128)} %bitcast_add_fusion), calls=%async_computation.1 | async-start | bytes 1048576 | tf_op jit(solution)/shard_map/all_to_all | solution.py:156
  68.1 10.3 %all-to-all-done.1 = f32[16,16,512]{2,1,0:T(8,128)S(1)} async-done(((f32[16,16,512]{2,1,0:T(8,128)}), f32[16,16,512]{2,1,0:T(8,128)S(1)}, u32[]{:S(2)}, u32[]{:S(2)}) %all-to-all-start.1) | async-done | bytes 524320 | tf_op jit(solution)/shard_map/all_to_all | solution.py:156
  78.4 0.2 fusion.40
  78.6 0.2 fusion.54
  78.8 0.2 exponential_reduce_fusion
  79.1 31.1 %all_to_all.15 = f32[256,3,16]{2,1,0:T(4,128)S(1)} all-to-all(f32[256,3,16]{2,1,0:T(4,128)S(1)} %broadcast_in_dim.146), channel_id=1, replica_groups=mesh['ctx'=32,'tp'=8] {'ctx','tp'}, dimensions={0} | all-to-all | bytes 98304 | tf_op jit(solution)/shard_map/all_to_all | solution.py:166
  110.2 0.3 slice_reduce_fusion
  110.9 0.5 bitcast_add_fusion.2
  111.4 0.7 fusion.23
  (59 shorter events, 3.1 us)
Async XLA Ops:
  0.6 31.8 %copy-start = (bf16[1024,256]{1,0:T(8,128)(2,1)S(1)}, bf16[1024,256]{1,0:T(8,128)(2,1)}, u32[]{:S(2)}) copy-start(bf16[1024,256]{1,0:T(8,128)(2,1)} %param.16) | copy-start | bytes 1572868
  5.3 6.3 %collective-permute-start = (f32[64,256]{0,1:T(8,128)S(1)}, f32[64,256]{0,1:T(8,128)S(1)}, u32[]{:S(2)}, u32[]{:S(2)}) collective-permute-start(f32[64,256]{0,1:T(8,128)S(1)} %maximum_maximum_fusion), channel_id=1, source_target_pairs={{0,8},{8,0},{16,24},{24,16},{32,40},{40,32},{48,56},{56,48},{64,72... | collective-permute-start | bytes 196616 | tf_op jit(solution)/shard_map/ppermute | solution.py:21
  11.8 5.2 %collective-permute-start.1 = (f32[64,256]{0,1:T(8,128)S(1)}, f32[64,256]{0,1:T(8,128)S(1)}, u32[]{:S(2)}, u32[]{:S(2)}) collective-permute-start(f32[64,256]{0,1:T(8,128)S(1)} %add_select_fusion.4), channel_id=1, source_target_pairs={{0,16},{8,24},{16,0},{24,8},{32,48},{40,56},{48,32},{56,40},{64,80... | collective-permute-start | bytes 196616 | tf_op jit(solution)/shard_map/ppermute | solution.py:21
  17.1 5.5 %collective-permute-start.2 = (f32[64,256]{0,1:T(8,128)S(1)}, f32[64,256]{0,1:T(8,128)S(1)}, u32[]{:S(2)}, u32[]{:S(2)}) collective-permute-start(f32[64,256]{0,1:T(8,128)S(1)} %add_select_fusion.3), channel_id=1, source_target_pairs={{0,48},{8,56},{16,32},{24,40},{32,16},{40,24},{48,0},{56,8},{64,11... | collective-permute-start | bytes 196616 | tf_op jit(solution)/shard_map/ppermute | solution.py:21
  22.7 3.9 %collective-permute-start.3 = (f32[64,256]{0,1:T(8,128)S(1)}, f32[64,256]{0,1:T(8,128)S(1)}, u32[]{:S(2)}, u32[]{:S(2)}) collective-permute-start(f32[64,256]{0,1:T(8,128)S(1)} %add_select_fusion.2), channel_id=1, source_target_pairs={{0,64},{8,72},{16,80},{24,88},{32,96},{40,104},{48,112},{56,120},{... | collective-permute-start | bytes 196616 | tf_op jit(solution)/shard_map/ppermute | solution.py:21
  26.8 5.1 %collective-permute-start.4 = (f32[64,256]{0,1:T(8,128)S(1)}, f32[64,256]{0,1:T(8,128)S(1)}, u32[]{:S(2)}, u32[]{:S(2)}) collective-permute-start(f32[64,256]{0,1:T(8,128)S(1)} %add_select_fusion.1), channel_id=1, source_target_pairs={{0,192},{8,200},{16,208},{24,216},{32,224},{40,232},{48,240},{56,2... | collective-permute-start | bytes 196616 | tf_op jit(solution)/shard_map/ppermute | solution.py:21
  33.3 14.5 %all-to-all-start = ((f32[8,16,256]{2,1,0:T(8,128)}), f32[8,16,256]{2,1,0:T(8,128)S(1)}, u32[]{:S(2)}, u32[]{:S(2)}) async-start(f32[8,16,256]{2,1,0:T(8,128)} %broadcast_in_dim.140), calls=%async_computation | async-start | bytes 262144 | tf_op jit(solution)/shard_map/all_to_all | solution.py:136
  39.9 7.9 %copy-start.1 = (bf16[2,8,256]{2,1,0:T(8,128)(2,1)S(1)}, bf16[2,8,256]{2,1,0:T(8,128)(2,1)}, u32[]{:S(2)}) copy-start(bf16[2,8,256]{2,1,0:T(8,128)(2,1)} %param.15) | copy-start | bytes 24580
  39.9 8.1 %copy-start.2 = (f32[256]{0:T(256)S(1)}, f32[256]{0:T(256)}, u32[]{:S(2)}) copy-start(f32[256]{0:T(256)} %param.17) | copy-start | bytes 3076
  47.7 20.3 %copy-start.3 = (s32[8]{0:T(128)S(1)}, s32[8]{0:T(128)}, u32[]{:S(2)}) copy-start(s32[8]{0:T(128)} %param.19) | copy-start | bytes 100
  53.9 7.0 %collective-permute-start.5 = (f32[16,16,512]{2,1,0:T(8,128)S(1)}, f32[16,16,512]{2,1,0:T(8,128)S(1)}, u32[]{:S(2)}, u32[]{:S(2)}) collective-permute-start(f32[16,16,512]{2,1,0:T(8,128)S(1)} %dynamic-slice_bitcast_fusion), channel_id=1, source_target_pairs={{0,8},{8,0},{16,24},{24,16},{32,40},{40,32},{48,56},{56,48},{64,72... | collective-permute-start | bytes 1572872 | tf_op jit(solution)/shard_map/ppermute | solution.py:21
  61.8 16.6 %all-to-all-start.1 = ((f32[16,16,512]{2,1,0:T(8,128)}), f32[16,16,512]{2,1,0:T(8,128)S(1)}, u32[]{:S(2)}, u32[]{:S(2)}) async-start(f32[16,16,512]{2,1,0:T(8,128)} %bitcast_add_fusion), calls=%async_computation.1 | async-start | bytes 1048576 | tf_op jit(solution)/shard_map/all_to_all | solution.py:156

commit v2 on v0

v2 whole, which is shorter than its diff:
```python
import functools

import jax
import jax.numpy as jnp
from jax import lax
from jax.experimental import pallas as pl
from jax.experimental.pallas import tpu as pltpu
from jax.sharding import PartitionSpec as P

D = 8192
HEAD_DIM = 128
SCORE_SCALE = HEAD_DIM ** (-0.5)

NEG_FILL = -1e30
NORM_EPS = 1e-05
CONTRAST_WEIGHT = 0.5
LOG_FLOOR = -2.302585092994046

F32 = jnp.float32
BF16 = jnp.bfloat16
VMEM = pl.BlockSpec(memory_space=pltpu.VMEM)
SMEM = pl.BlockSpec(memory_space=pltpu.SMEM)
ANY = pl.BlockSpec(memory_space=pl.ANY)


def dot_rows(left, right):
    return lax.dot_general(left, right, (((1,), (1,)), ((), ())), preferred_element_type=F32)


def iota(shape, axis):
    return lax.broadcasted_iota(jnp.int32, shape, axis)


def long_kernel(chunks, lengths, queries, cache, state, held, wide, stat, sems):
    rows, block_len = cache.shape[1], cache.shape[2]
    per = rows // chunks
    copies = [
        pltpu.make_async_copy(
            cache.at[part, pl.ds(c * per, per)],
            held.at[part, pl.ds(c * per, per)],
            sems.at[part * chunks + c],
        )
        for part in range(2)
        for c in range(chunks)
    ]
    for copy in copies:
        copy.start()
    start = lax.axis_index("ctx") * block_len
    query = queries[0].astype(F32)
    heads = query.shape[0] // rows
    position = start + iota((heads, block_len), 1)
    lane = iota((heads, HEAD_DIM), 1)
    kept = []
    for b in range(rows):
        if b % per == 0:
            copies[b // per].wait()
        mine = query[b * heads : (b + 1) * heads].astype(BF16)
        mask = position < lengths[b]
        scores = jnp.where(mask, dot_rows(mine, held[0, b]) * SCORE_SCALE, NEG_FILL)
        top = jnp.max(scores, axis=1, keepdims=True)
        weights = jnp.where(mask, jnp.exp(scores - top), 0.0)
        total = jnp.sum(weights, axis=1, keepdims=True)
        stat[pl.ds(b, heads, stride=rows), :] = jnp.where(lane == 0, top, total)
        kept.append(weights.astype(BF16))
    for b in range(rows):
        if b % per == 0:
            copies[chunks + b // per].wait()
        wide[pl.ds(b, heads, stride=rows), :] = jnp.dot(
            kept[b], held[1, b], preferred_element_type=F32
        )
    half = HEAD_DIM // 2
    turned = wide[...].T
    state[0:half, :] = jnp.concatenate([turned[:half], turned[half:]], axis=1)
    turned = stat[...].T[:8]
    state[half : half + 8, :] = jnp.concatenate([turned, turned], axis=1)


def short_kernel(queries, cache, fresh, aux):
    rows = cache.shape[1]
    query = [queries[0].astype(F32), queries[1].astype(F32)]
    heads = query[0].shape[0] // rows
    key = [fresh[0, 0].astype(F32), fresh[1, 0].astype(F32)]
    value = [fresh[0, 1].astype(F32), fresh[1, 1].astype(F32)]
    for b in range(rows):
        part = [q[b * heads : (b + 1) * heads] for q in query]
        own = [
            jnp.sum(part[n] * key[n][b : b + 1], axis=1, keepdims=True) * SCORE_SCALE
            for n in range(2)
        ]
        scores = dot_rows(part[1].astype(BF16), cache[0, b]) * SCORE_SCALE
        top = jnp.max(scores, axis=1, keepdims=True)
        weights = jnp.exp(scores - top)
        total = jnp.sum(weights, axis=1, keepdims=True)
        output = jnp.dot(weights.astype(BF16), cache[1, b], preferred_element_type=F32)
        final = jnp.maximum(top, own[1])
        older = jnp.exp(top - final)
        newer = jnp.exp(own[1] - final)
        mixed = output * older + newer * value[1][b : b + 1]
        where = pl.ds(b, heads, stride=rows)
        aux[0, where, :] = mixed / (total * older + newer)
        aux[1, where, :] = jnp.broadcast_to(own[0], (heads, HEAD_DIM))
        aux[2, where, :] = jnp.broadcast_to(value[0][b : b + 1], (heads, HEAD_DIM))


def merge_states(parts):
    half = HEAD_DIM // 2
    tops = [part[half : half + 1, :] for part in parts]
    peak = functools.reduce(jnp.maximum, tops)
    factors = [jnp.exp(top - peak) for top in tops]
    total = sum(part[half + 1 : half + 2, :] * f for part, f in zip(parts, factors))
    values = sum(part[0:half, :] * f for part, f in zip(parts, factors))
    return values, peak, total


def packed_stats(peak, total):
    return jnp.where(iota((8, HEAD_DIM), 0) == 0, peak, total)


def pair_kernel(one, two, spread):
    half = HEAD_DIM // 2
    values, peak, total = merge_states([one, two])
    stats = packed_stats(peak, total)
    for k in range(spread.shape[0]):
        spread[k, 0:half, :] = values
        spread[k, half : half + 8, :] = stats


def project_kernel(states, aux, weight, spread):
    half = HEAD_DIM // 2
    values, peak, total = merge_states([states.at[k] for k in range(states.shape[0])])
    blank = jnp.zeros((half - 8, HEAD_DIM), F32)
    turned = jnp.concatenate([values, packed_stats(peak, total), blank], axis=0).T
    left, right = turned[:half], turned[half:]
    lane = iota((half, HEAD_DIM), 1)
    output = jnp.where(lane < half, left, pltpu.roll(right, half, 1))
    peak, total = left[:, half : half + 1], left[:, half + 1 : half + 2]
    own = aux[1][:, 0:1]
    final = jnp.maximum(peak, own)
    older = jnp.exp(peak - final)
    newer = jnp.exp(own - final)
    attended = [(output * older + newer * aux[2]) / (total * older + newer), aux[0]]
    rows = 8
    heads = half // rows
    rows_wide = jnp.concatenate(
        [
            jnp.concatenate([part[h * rows : (h + 1) * rows] for part in attended], axis=0)
            for h in range(heads)
        ],
        axis=1,
    )
    projected = jnp.dot(rows_wide.astype(BF16), weight[...], preferred_element_type=F32)
    for k in range(spread.shape[0]):
        spread[k] = projected


def head_blocks(other, share, scaled, squares, weight, blocks, held, sems):
    count, vocab = blocks.shape[0], weight.shape[0]
    padded, reach = blocks.shape[2], held.shape[1]
    fetched = sems_rows(share)
    core = lax.rem(lax.axis_index("ctx"), 2)
    which = 1 - core if other else core

    def place(k):
        offset = (2 * k + which) * share
        base = jnp.minimum(offset // 16 * 16, vocab - fetched)
        return pl.multiple_of(base, 16), offset - base

    def copy(k):
        return pltpu.make_async_copy(
            weight.at[pl.ds(place(k)[0], fetched)], held.at[k, pl.ds(0, fetched)], sems.at[k]
        )

    for k in range(count):
        copy(k).start()
    lane = iota((blocks.shape[1], padded), 1)
    left, fill = scaled(), squares()

    def block(k, carry):
        copy(k).wait()
        product = dot_rows(left, held[k])
        moved = pltpu.roll(product, lax.rem(reach - place(k)[1], reach), 1)[:, :padded]
        blocks[k] = jnp.where(lane < share, moved, fill)
        return carry

    lax.fori_loop(0, count, block, 0, unroll=True)


def sems_rows(share):
    return -(-(share + 15) // 16) * 16


def other_kernel(share, parts, residual, gain, weight, blocks, scaled, squares, held, sems):
    def first():
        projected = sum(parts[k] for k in range(parts.shape[0]))
        stream = residual[...].astype(F32) + projected
        squares[...] = jnp.broadcast_to(
            jnp.sum(stream * stream, axis=1, keepdims=True), squares.shape
        )
        scaled[...] = (stream * gain[...]).astype(BF16)
        return scaled[...]

    head_blocks(True, share, first, lambda: squares[:, 0:1], weight, blocks, held, sems)


def same_kernel(share, scaled, squares, weight, blocks, held, sems):
    head_blocks(
        False, share, lambda: scaled[...], lambda: squares[:, 0:1], weight, blocks, held, sems
    )


def add_kernel(one, two, out):
    out[...] = one[...] + two[...]


def column_of(values, rows):
    shape = (rows, values.shape[1])
    return jnp.sum(jnp.where(iota(shape, 0) == iota(shape, 1), values, 0.0), axis=1, keepdims=True)


def stats_kernel(share, vocab, targets, parts, logits, spread):
    rows, padded = logits.shape
    summed = sum(parts[k] for k in range(parts.shape[0]))
    inverse = lax.rsqrt(summed[:, share : share + 1] * (1.0 / D) + NORM_EPS)
    lane = iota((rows, padded), 1)
    valid = lane < share
    local = summed * inverse
    logits[...] = local
    peak = jnp.max(jnp.where(valid, local, -jnp.inf), axis=1, keepdims=True)
    total = jnp.sum(jnp.where(valid, jnp.exp(local - peak), 0.0), axis=1, keepdims=True)
    row = iota((rows, 1), 0)
    wanted = jnp.zeros((rows, 1), jnp.int32)
    for b in range(rows // 2):
        wanted = jnp.where(lax.rem(row, rows // 2) == b, targets[b], wanted)
    start = lax.axis_index("tp") * vocab + lax.axis_index("ctx") * share
    hit = jnp.logical_and(valid, lane + start == wanted)
    picks = jnp.sum(jnp.where(hit, local, 0.0), axis=1, keepdims=True)
    place = iota((rows, 128), 1)
    mixed = jnp.where(place < rows, peak, jnp.where(place < 2 * rows, total, picks))
    keep = jnp.logical_and(lax.rem(place, rows) == iota((rows, 128), 0), place < 3 * rows)
    line = jnp.sum(jnp.where(keep, mixed, 0.0), axis=0, keepdims=True)
    spread[...] = jnp.broadcast_to(line, spread.shape)


def scores_kernel(share, everyone, logits, scores, chosen):
    rows = logits.shape[0]
    half = rows // 2
    data = everyone[...]
    peak = jnp.max(data, axis=0, keepdims=True)
    scale = jnp.exp(data - peak)
    lane = iota(peak.shape, 1)
    total = jnp.sum(pltpu.roll(scale, rows, 1) * data, axis=0, keepdims=True)
    total = jnp.where(lane < rows, pltpu.roll(total, 128 - rows, 1), 1.0)
    picks = pltpu.roll(jnp.sum(data, axis=0, keepdims=True), 128 - 2 * rows, 1)
    lse = peak + jnp.log(total)
    picked = picks - lse
    line = (
        (1.0 + CONTRAST_WEIGHT) * picked
        - CONTRAST_WEIGHT * pltpu.roll(picked, 128 - half, 1)
        + jnp.minimum(0.0, picks - peak - LOG_FLOOR)
    )
    chosen[...] = line[:, :half]
    logp = logits[...] - column_of(lse, rows)
    top = column_of(peak, rows)
    result = (
        (1.0 + CONTRAST_WEIGHT) * logp[:half]
        - CONTRAST_WEIGHT * logp[half:]
        + jnp.minimum(0.0, logits[:half] - top[:half] - LOG_FLOOR)
    )
    scores[...] = result[:, :share]


def call(kernel, out, in_specs, name, scratch=(), flops=0, moved=0):
    outs = [jax.ShapeDtypeStruct(shape, kind) for shape, kind in out]
    specs = [VMEM] * len(outs)
    return pl.pallas_call(
        kernel,
        out_shape=outs if len(outs) > 1 else outs[0],
        in_specs=in_specs,
        out_specs=specs if len(outs) > 1 else specs[0],
        scratch_shapes=list(scratch),
        name=name,
        cost_estimate=pl.CostEstimate(flops=flops, bytes_accessed=moved, transcendentals=0),
        compiler_params=pltpu.CompilerParams(vmem_limit_bytes=24 * 1024 * 1024),
    )


def per_device(
    queries,
    new_kv,
    long_cache,
    short_cache,
    lengths,
    residual,
    out_weight,
    final_gain,
    head_weight,
    targets,
):
    row_count, heads = queries.shape[1], queries.shape[2]
    block_len, short_len = long_cache.shape[2], short_cache.shape[2]
    width, vocab = residual.shape[2], head_weight.shape[1]
    ctx_size, tp_size = lax.axis_size("ctx"), lax.axis_size("tp")
    chips = ctx_size // 2
    rows = 2 * row_count
    share = vocab // ctx_size
    padded = -(-(share + 1) // 128) * 128
    pairs = row_count * heads
    packed = HEAD_DIM // 2 + 8
    cores = [(i, i ^ 1) for i in range(ctx_size)]
    same_core = [list(range(which, ctx_size, 2)) for which in range(2)]

    flat_queries = queries.reshape(2, pairs, HEAD_DIM)
    long_rows = long_cache.reshape(2, row_count, block_len, HEAD_DIM)
    short_rows = short_cache.reshape(2, row_count, short_len, HEAD_DIM)
    fresh = new_kv.reshape(2, 2, row_count, HEAD_DIM)

    chunks = 4
    state = call(
        functools.partial(long_kernel, chunks),
        [((packed, 128), F32)],
        [SMEM, VMEM, ANY],
        "long_attention",
        [
            pltpu.VMEM(long_rows.shape, BF16),
            pltpu.VMEM((pairs, HEAD_DIM), F32),
            pltpu.VMEM((pairs, HEAD_DIM), F32),
            pltpu.SemaphoreType.DMA((2 * chunks,)),
        ],
        moved=2 * 1024 * 1024,
    )(lengths, flat_queries, long_rows)
    other = lax.ppermute(state, "ctx", cores)
    aux = call(
        short_kernel, [((3, pairs, HEAD_DIM), F32)], [VMEM] * 3, "short_attention", moved=1024 * 1024
    )(flat_queries, short_rows, fresh)
    spread = call(pair_kernel, [((chips, packed, 128), F32)], [VMEM] * 2, "merge_cores")(
        state, other
    )
    states = lax.all_to_all(spread, "ctx", 0, 0, tiled=True, axis_index_groups=same_core)
    spread = call(project_kernel, [((tp_size, rows, width), F32)], [VMEM] * 3, "project")(
        states, aux, out_weight
    )
    parts = lax.all_to_all(spread, "tp", 0, 0, tiled=True)

    weight_rows = head_weight.T
    reach = -(-sems_rows(share) // 128) * 128
    scratch = [pltpu.VMEM((chips, reach, width), BF16), pltpu.SemaphoreType.DMA((chips,))]
    theirs, scaled, squares = call(
        functools.partial(other_kernel, share),
        [((chips, rows, padded), F32), ((rows, width), BF16), ((rows, 128), F32)],
        [VMEM, VMEM, VMEM, ANY],
        "head_other",
        scratch,
        moved=4 * 1024 * 1024,
    )(parts, residual.reshape(rows, width), final_gain.reshape(1, width), weight_rows)
    arrived = lax.ppermute(theirs, "ctx", cores)
    mine = call(
        functools.partial(same_kernel, share),
        [((chips, rows, padded), F32)],
        [VMEM, VMEM, ANY],
        "head_same",
        scratch,
        moved=4 * 1024 * 1024,
    )(scaled, squares, weight_rows)
    blocks = call(add_kernel, [((chips, rows, padded), F32)], [VMEM] * 2, "add_cores")(
        mine, arrived
    )
    parts = lax.all_to_all(blocks, "ctx", 0, 0, tiled=True, axis_index_groups=same_core)

    devices = ctx_size * tp_size
    logits, spread = call(
        functools.partial(stats_kernel, share, vocab),
        [((rows, padded), F32), ((devices, 128), F32)],
        [SMEM, VMEM],
        "vocab_stats",
    )(targets, parts)
    everyone = lax.all_to_all(
        spread.reshape(devices, 1, 128), ("ctx", "tp"), 0, 0, tiled=True
    ).reshape(devices, 128)
    scores, chosen = call(
        functools.partial(scores_kernel, share),
        [((row_count, share), F32), ((1, row_count), F32)],
        [VMEM, VMEM],
        "scores",
    )(everyone, logits)
    return (scores, chosen.reshape(row_count))


def solution(mesh):
    placed = (
        P(None, None, "tp", None),
        P(None, None, None, "tp", None),
        P(None, None, "ctx", "tp", None),
        P(None, None, None, "tp", None),
        P(),
        P(None, None, "ctx"),
        P("tp", "ctx"),
        P("ctx"),
        P("ctx", "tp"),
        P(),
    )
    return jax.shard_map(
        per_device,
        mesh=mesh,
        in_specs=placed,
        out_specs=(P(None, ("tp", "ctx")), P()),
        check_vma=False,
    )
```

time: 565 us -> 100 us (0.18)
  blocking collectives: 474 us -> 49.3 us
  waiting for transfers between devices: 43.9 us -> 7.07 us
  Pallas kernels: 0 us -> 18.8 us
  between operations: 14.8 us -> 0.72 us
  matrix products: 13.2 us -> 0 us
  starting transfers between devices: 0.04 us -> 12 us
  other arithmetic: 11.4 us -> 0 us
  local copies, waits for them, and re-layouts: 0.87 us -> 11.4 us
    psum x3 -> x0, blocking collectives: 222 us -> none  [the longest x1 122 us: per_device(): lax.psum((totals * factor, output * factor[..., None]), 'ctx')]
    all_gather x3 -> x0, blocking collectives: 187 us -> none  [combined_all(): everything = jax.tree.map(lambda part: lax.all_gather(part, axis), value)]
    pmax x1 -> x0, blocking collectives: 65.3 us -> none  [per_device(): peak_all = lax.pmax(peak_local, 'ctx')]
    all_to_all x0 -> x3, blocking collectives: none -> 49.3 us  [the longest x1 20.2 us: per_device(): lax.all_to_all(spread.reshape(devices, 1, 128), ('ctx', 'tp'), 0, 0, tile...]
    unnamed x2 -> x0, waiting for transfers between devices: 43.9 us -> none
    pallas_call x0 -> x9, Pallas kernels: none -> 18.8 us  [the longest x1 5.4 us: per_device(): call(functools.partial(other_kernel, share), [((chips, rows, padded), F32...]
    dot_general x8 -> x0, matrix products: 13.2 us -> none  [the longest x1 6.64 us: per_device(): jnp.dot(scaled, head_weight, preferred_element_type=jnp.float32)]
    unnamed x13 -> x24, local copies, waits for them, and re-layouts: 0.62 us -> 11.4 us
  transfers between devices with their start and end apart: 1 -> 3, of which waited for: 1 -> 2; matrix products, arithmetic and copies ran while one was open for 0% -> 0% of each run, Pallas kernels for 0% -> 7%
where the time goes in v2:
time: 100 us; the launch traced here: 99.4 us
  blocking collectives  49.3 us (49%)
  Pallas kernels  18.8 us (19%)
  starting transfers between devices  12 us (12%)
  local copies, waits for them, and re-layouts  11.4 us (11%)
  waiting for transfers between devices  7.07 us (7%)
    all_to_all x1, blocking collectives, per_device(): lax.all_to_all(spread.reshape(devices, 1, 128), ('ctx', 'tp'), 0, 0, tile...  20.2 us
    all_to_all x1, blocking collectives, per_device(): parts = lax.all_to_all(spread, 'tp', 0, 0, tiled=True)  16 us
    all_to_all x1, blocking collectives, per_device(): lax.all_to_all(blocks, 'ctx', 0, 0, tiled=True, axis_index_groups=same_core)  13.1 us
    unnamed x24, local copies, waits for them, and re-layouts  11.4 us
    all_to_all x1, waiting for transfers between devices, per_device(): lax.all_to_all(spread, 'ctx', 0, 0, tiled=True, axis_index_groups=same_core)  6.2 us
    pallas_call x1, Pallas kernels, per_device(): call(functools.partial(other_kernel, share), [((chips, rows, padded), F32...  5.4 us
    pallas_call x1, Pallas kernels, per_device(): call(functools.partial(same_kernel, share), [((chips, rows, padded), F32)...  5.31 us
    all_to_all x1, starting transfers between devices, per_device(): lax.all_to_all(spread, 'ctx', 0, 0, tiled=True, axis_index_groups=same_core)  5.02 us
  transfers between devices with their start and end apart: 3, of which 2 were waited for; matrix products, arithmetic and copies ran while one was open for 0% of the time, Pallas kernels for 7%

profile of v2, /device:TPU:1, one launch (start us, length us, event | category | flops | bytes accessed | tf_op | source)
XLA Modules:
  0.0 99.4 jit_solution(7212441445067916748)
XLA Ops:
  0.6 0.0 copy-start.2
  0.6 1.6 %copy-done.2 = bf16[2,8,512,1,128]{4,2,3,1,0:T(8,128)(2,1)S(1)} copy-done((bf16[2,8,512,1,128]{4,2,3,1,0:T(8,128)(2,1)S(1)}, bf16[2,8,512,1,128]{4,2,3,1,0:T(8,128)(2,1)}, u32[]{:S(2)}) %copy-start.2) | copy-done | bytes 2097176
  2.2 0.8 copy-done.5
  3.0 0.7 copy-done.10
  3.6 3.0 %long_attention.1.one = f32[72,128]{1,0:T(8,128)S(1)} custom-call(s32[8]{0:T(128)S(1)} %copy-done.10, bf16[2,64,128]{2,1,0:T(8,128)(2,1)S(1)} %bitcast.17, bf16[2,8,512,128]{3,2,1,0:T(8,128)(2,1)S(1)} %bitcast.14), custom_call_target="tpu_custom_call" | custom-call | bytes 2097152 | tf_op jit(solution)/shard_map/long_attention/pallas_call | solution.py:318
  6.6 3.3 %collective-permute-start = (f32[72,128]{1,0:T(8,128)S(1)}, f32[72,128]{1,0:T(8,128)S(1)}, u32[]{:S(2)}, u32[]{:S(2)}) collective-permute-start(f32[72,128]{1,0:T(8,128)S(1)} %long_attention.1.one), channel_id=1, source_target_pairs={{0,8},{8,0},{16,24},{24,16},{32,40},{40,32},{48,56},{56,48},{64,72... | collective-permute-start | bytes 110600 | tf_op jit(solution)/shard_map/ppermute | solution.py:331
  9.9 0.9 collective-permute-done.two
  10.8 0.9 merge_cores.1
  11.7 5.0 %all-to-all-start = ((f32[16,72,128]{2,1,0:T(8,128)}), f32[16,72,128]{2,1,0:T(8,128)S(1)}, u32[]{:S(2)}, u32[]{:S(2)}) async-start(f32[16,72,128]{2,1,0:T(8,128)} %merge_cores.1), calls=%async_computation | async-start | bytes 1179648 | tf_op jit(solution)/shard_map/all_to_all | solution.py:338
  16.7 0.0 copy-start.3
  16.7 1.2 %copy-done.3 = bf16[2,8,256,1,128]{4,2,3,1,0:T(8,128)(2,1)S(1)} copy-done((bf16[2,8,256,1,128]{4,2,3,1,0:T(8,128)(2,1)S(1)}, bf16[2,8,256,1,128]{4,2,3,1,0:T(8,128)(2,1)}, u32[]{:S(2)}) %copy-start.3) | copy-done | bytes 1048600
  17.9 0.8 copy-done.6
  18.7 0.7 copy-done.7
  19.4 2.0 %short_attention.1.aux = f32[3,64,128]{2,1,0:T(8,128)S(1)} custom-call(bf16[2,64,128]{2,1,0:T(8,128)(2,1)S(1)} %bitcast.18, bf16[2,8,256,128]{3,2,1,0:T(8,128)(2,1)S(1)} %bitcast.15, bf16[2,2,8,128]{3,2,1,0:T(8,128)(2,1)S(1)} %bitcast.20), custom_call_target="tpu_custom_call" | custom-call | bytes 1048576 | tf_op jit(solution)/shard_map/short_attention/pallas_call | solution.py:332
  21.4 6.2 %all-to-all-done.states = f32[16,72,128]{2,1,0:T(8,128)S(1)} async-done(((f32[16,72,128]{2,1,0:T(8,128)}), f32[16,72,128]{2,1,0:T(8,128)S(1)}, u32[]{:S(2)}, u32[]{:S(2)}) %all-to-all-start) | async-done | bytes 589856 | tf_op jit(solution)/shard_map/all_to_all | solution.py:338
  27.6 1.0 %copy-done.4 = bf16[1024,256]{1,0:T(8,128)(2,1)S(1)} copy-done((bf16[1024,256]{1,0:T(8,128)(2,1)S(1)}, bf16[1024,256]{1,0:T(8,128)(2,1)}, u32[]{:S(2)}) %copy-start.4) | copy-done | bytes 524312
  28.6 0.5 project.1
  29.1 16.0 %all_to_all.20.parts = f32[8,16,256]{2,1,0:T(8,128)S(1)} all-to-all(f32[8,16,256]{2,1,0:T(8,128)S(1)} %project.1), channel_id=1, replica_groups=mesh['ctx'=32,'tp'=8] {'tp'}, dimensions={0} | all-to-all | bytes 262144 | tf_op jit(solution)/shard_map/all_to_all | solution.py:342
  45.2 3.3 %copy-done = bf16[256,16032]{0,1:T(8,128)(2,1)S(1)} copy-done((bf16[256,16032]{0,1:T(8,128)(2,1)S(1)}, bf16[256,16032]{0,1:T(8,128)(2,1)}, u32[]{:S(2)}) %copy-start) | copy-done | bytes 8208408
  48.5 0.7 copy-done.8
  49.2 0.7 copy-done.9
  49.9 5.4 %head_other.1 = (f32[16,16,512]{2,1,0:T(8,128)S(1)}, bf16[16,256]{1,0:T(8,128)(2,1)S(1)}, f32[16,128]{1,0:T(8,128)S(1)}) custom-call(f32[8,16,256]{2,1,0:T(8,128)S(1)} %all_to_all.20.parts, bf16[16,256]{1,0:T(8,128)(2,1)S(1)} %bitcast.21, f32[1,256]{1,0:T(1,128)S(1)} %bitcast.22, bf16[16032,256]{1,0:T(8,128)(2,1)S(1)} %bitcast.12), custom_call_target="tpu_custom_call" | custom-call | bytes 4194304 | tf_op jit(solution)/shard_map/head_other/pallas_call | solution.py:347
  55.3 3.7 %collective-permute-start.1 = (f32[16,16,512]{2,1,0:T(8,128)S(1)}, f32[16,16,512]{2,1,0:T(8,128)S(1)}, u32[]{:S(2)}, u32[]{:S(2)}) collective-permute-start(f32[16,16,512]{2,1,0:T(8,128)S(1)} %get-tuple-element.11), channel_id=1, source_target_pairs={{0,8},{8,0},{16,24},{24,16},{32,40},{40,32},{48,56},{56,48},{64,72... | collective-permute-start | bytes 1572872 | tf_op jit(solution)/shard_map/ppermute | solution.py:355
  59.0 0.0 copy-done.1
  59.0 5.3 %head_same.1.one = f32[16,16,512]{2,1,0:T(8,128)S(1)} custom-call(bf16[16,256]{1,0:T(8,128)(2,1)S(1)} %get-tuple-element.9.scaled, f32[16,128]{1,0:T(8,128)S(1)} %get-tuple-element.10.squares, bf16[16032,256]{1,0:T(8,128)(2,1)S(1)} %bitcast.13), custom_call_target="tpu_custom_call" | custom-call | bytes 4194304 | tf_op jit(solution)/shard_map/head_same/pallas_call | solution.py:356
  64.3 0.0 collective-permute-done.1.two
  64.3 0.1 add_cores.1
  64.4 13.1 %all_to_all.21.parts = f32[16,16,512]{2,1,0:T(8,128)S(1)} all-to-all(f32[16,16,512]{2,1,0:T(8,128)S(1)} %add_cores.1), channel_id=1, replica_groups={{0,16,32,48,64,80,96,112,128,144,160,176,192,208,224,240},{8,24,40,56,7..., dimensions={0} | all-to-all | bytes 1048576 | tf_op jit(solution)/shard_map/all_to_all | solution.py:367
  77.5 0.0 copy-done.11
  77.5 0.8 vocab_stats.1
  78.3 20.2 %all_to_all.22 = f32[256,1,128]{2,1,0:T(1,128)S(1)} all-to-all(f32[256,1,128]{2,1,0:T(1,128)S(1)} %bitcast.19), channel_id=1, replica_groups=mesh['ctx'=32,'tp'=8] {'ctx','tp'}, dimensions={0} | all-to-all | bytes 262144 | tf_op jit(solution)/shard_map/all_to_all | solution.py:376
  98.5 0.9 scores.1
  (10 shorter events, 0.0 us)
Async XLA Ops:
  0.6 1.6 %copy-start.2 = (bf16[2,8,512,1,128]{4,2,3,1,0:T(8,128)(2,1)S(1)}, bf16[2,8,512,1,128]{4,2,3,1,0:T(8,128)(2,1)}, u32[]{:S(2)}) copy-start(bf16[2,8,512,1,128]{4,2,3,1,0:T(8,128)(2,1)} %param.12) | copy-start | bytes 6291460
  2.2 0.8 copy-start.5
  3.0 0.7 copy-start.10
  6.6 4.2 %collective-permute-start = (f32[72,128]{1,0:T(8,128)S(1)}, f32[72,128]{1,0:T(8,128)S(1)}, u32[]{:S(2)}, u32[]{:S(2)}) collective-permute-start(f32[72,128]{1,0:T(8,128)S(1)} %long_attention.1.one), channel_id=1, source_target_pairs={{0,8},{8,0},{16,24},{24,16},{32,40},{40,32},{48,56},{56,48},{64,72... | collective-permute-start | bytes 110600 | tf_op jit(solution)/shard_map/ppermute | solution.py:331
  11.7 15.9 %all-to-all-start = ((f32[16,72,128]{2,1,0:T(8,128)}), f32[16,72,128]{2,1,0:T(8,128)S(1)}, u32[]{:S(2)}, u32[]{:S(2)}) async-start(f32[16,72,128]{2,1,0:T(8,128)} %merge_cores.1), calls=%async_computation | async-start | bytes 1179648 | tf_op jit(solution)/shard_map/all_to_all | solution.py:338
  16.7 1.2 %copy-start.3 = (bf16[2,8,256,1,128]{4,2,3,1,0:T(8,128)(2,1)S(1)}, bf16[2,8,256,1,128]{4,2,3,1,0:T(8,128)(2,1)}, u32[]{:S(2)}) copy-start(bf16[2,8,256,1,128]{4,2,3,1,0:T(8,128)(2,1)} %param.13) | copy-start | bytes 3145732
  17.9 0.8 copy-start.6
  18.7 0.7 copy-start.7
  27.6 1.0 %copy-start.4 = (bf16[1024,256]{1,0:T(8,128)(2,1)S(1)}, bf16[1024,256]{1,0:T(8,128)(2,1)}, u32[]{:S(2)}) copy-start(bf16[1024,256]{1,0:T(8,128)(2,1)} %weight.1) | copy-start | bytes 1572868
  45.2 3.3 %copy-start = (bf16[256,16032]{0,1:T(8,128)(2,1)S(1)}, bf16[256,16032]{0,1:T(8,128)(2,1)}, u32[]{:S(2)}) copy-start(bf16[256,16032]{0,1:T(8,128)(2,1)} %param.18) | copy-start | bytes 24625156
  48.5 0.7 copy-start.8
  49.2 0.7 copy-start.9
  49.9 9.1 %copy-start.1 = (bf16[256,16032]{0,1:T(8,128)(2,1)S(1)}, bf16[256,16032]{0,1:T(8,128)(2,1)}, u32[]{:S(2)}) copy-start(bf16[256,16032]{0,1:T(8,128)(2,1)} %param.18) | copy-start | bytes 24625156
  49.9 27.6 %copy-start.11 = (s32[8]{0:T(128)S(1)}, s32[8]{0:T(128)}, u32[]{:S(2)}) copy-start(s32[8]{0:T(128)} %targets.1) | copy-start | bytes 100
  55.3 9.0 %collective-permute-start.1 = (f32[16,16,512]{2,1,0:T(8,128)S(1)}, f32[16,16,512]{2,1,0:T(8,128)S(1)}, u32[]{:S(2)}, u32[]{:S(2)}) collective-permute-start(f32[16,16,512]{2,1,0:T(8,128)S(1)} %get-tuple-element.11), channel_id=1, source_target_pairs={{0,8},{8,0},{16,24},{24,16},{32,40},{40,32},{48,56},{56,48},{64,72... | collective-permute-start | bytes 1572872 | tf_op jit(solution)/shard_map/ppermute | solution.py:355

commit v3 on v2

--- a/solution.py
+++ b/solution.py
@@ -19,7 +19,6 @@
 F32 = jnp.float32
 BF16 = jnp.bfloat16
 VMEM = pl.BlockSpec(memory_space=pltpu.VMEM)
-SMEM = pl.BlockSpec(memory_space=pltpu.SMEM)
 ANY = pl.BlockSpec(memory_space=pl.ANY)
 
 
@@ -31,9 +30,17 @@
     return lax.broadcasted_iota(jnp.int32, shape, axis)
 
 
-def long_kernel(chunks, lengths, queries, cache, state, held, wide, stat, sems):
+def long_kernel(
+    chunks, lengths_far, queries_far, cache, state, held, queries, lengths, wide, stat, sems
+):
     rows, block_len = cache.shape[1], cache.shape[2]
     per = rows // chunks
+    small = [
+        pltpu.make_async_copy(lengths_far, lengths, sems.at[2 * chunks]),
+        pltpu.make_async_copy(queries_far.at[0], queries, sems.at[2 * chunks + 1]),
+    ]
+    for copy in small:
+        copy.start()
     copies = [
         pltpu.make_async_copy(
             cache.at[part, pl.ds(c * per, per)],
@@ -46,7 +53,9 @@
     for copy in copies:
         copy.start()
     start = lax.axis_index("ctx") * block_len
-    query = queries[0].astype(F32)
+    for copy in small:
+        copy.wait()
+    query = queries[...].astype(F32)
     heads = query.shape[0] // rows
     position = start + iota((heads, block_len), 1)
     lane = iota((heads, HEAD_DIM), 1)
@@ -75,7 +84,60 @@
     state[half : half + 8, :] = jnp.concatenate([turned, turned], axis=1)
 
 
-def short_kernel(queries, cache, fresh, aux):
+def short_kernel(
+    share,
+    queries_far,
+    cache_far,
+    fresh_far,
+    out_far,
+    head_far,
+    residual_far,
+    gain_far,
+    targets_far,
+    aux,
+    out_near,
+    head_near,
+    residual,
+    gain,
+    wanted,
+    queries,
+    cache,
+    fresh,
+    targets,
+    sems,
+    head_sems,
+):
+    moves = (
+        (queries_far, queries),
+        (cache_far.at[0], cache.at[0]),
+        (fresh_far, fresh),
+        (cache_far.at[1], cache.at[1]),
+        (targets_far, targets),
+        (out_far, out_near),
+        (residual_far, residual),
+        (gain_far, gain),
+    )
+    copies = [pltpu.make_async_copy(*move, sems.at[n]) for n, move in enumerate(moves)]
+    for copy in copies:
+        copy.start()
+    fetched = fetched_rows(share)
+    blocks = [
+        pltpu.make_async_copy(
+            head_far.at[pl.ds(min(j * share // 16 * 16, head_far.shape[0] - fetched), fetched)],
+            head_near.at[j, pl.ds(0, fetched)],
+            head_sems.at[j],
+        )
+        for j in range(head_near.shape[0])
+    ]
+    for copy in blocks:
+        copy.start()
+    for copy in copies:
+        copy.wait()
+    row = iota(wanted.shape, 0)
+    aim = jnp.zeros(wanted.shape, jnp.int32)
+    for b in range(targets.shape[0]):
+        aim = jnp.where(lax.rem(row, targets.shape[0]) == b, targets[b], aim)
+    wanted[...] = aim
     rows = cache.shape[1]
     query = [queries[0].astype(F32), queries[1].astype(F32)]
     heads = query[0].shape[0] // rows
@@ -100,6 +162,8 @@
         aux[0, where, :] = mixed / (total * older + newer)
         aux[1, where, :] = jnp.broadcast_to(own[0], (heads, HEAD_DIM))
         aux[2, where, :] = jnp.broadcast_to(value[0][b : b + 1], (heads, HEAD_DIM))
+    for copy in blocks:
+        copy.wait()
 
 
 def merge_states(parts):
@@ -153,59 +217,36 @@
         spread[k] = projected
 
 
-def head_blocks(other, share, scaled, squares, weight, blocks, held, sems):
-    count, vocab = blocks.shape[0], weight.shape[0]
-    padded, reach = blocks.shape[2], held.shape[1]
-    fetched = sems_rows(share)
+def fetched_rows(share):
+    return -(-(share + 15) // 16) * 16
+
+
+def head_blocks(other, share, vocab, left, fill, weight, blocks):
+    padded, reach = blocks.shape[2], weight.shape[1]
     core = lax.rem(lax.axis_index("ctx"), 2)
     which = 1 - core if other else core
-
-    def place(k):
-        offset = (2 * k + which) * share
-        base = jnp.minimum(offset // 16 * 16, vocab - fetched)
-        return pl.multiple_of(base, 16), offset - base
-
-    def copy(k):
-        return pltpu.make_async_copy(
-            weight.at[pl.ds(place(k)[0], fetched)], held.at[k, pl.ds(0, fetched)], sems.at[k]
-        )
-
-    for k in range(count):
-        copy(k).start()
     lane = iota((blocks.shape[1], padded), 1)
-    left, fill = scaled(), squares()
-
-    def block(k, carry):
-        copy(k).wait()
-        product = dot_rows(left, held[k])
-        moved = pltpu.roll(product, lax.rem(reach - place(k)[1], reach), 1)[:, :padded]
+    for k in range(blocks.shape[0]):
+        j = 2 * k + which
+        offset = j * share
+        ahead = offset - jnp.minimum(offset // 16 * 16, vocab - fetched_rows(share))
+        product = dot_rows(left, weight[j])
+        moved = pltpu.roll(product, lax.rem(reach - ahead, reach), 1)[:, :padded]
         blocks[k] = jnp.where(lane < share, moved, fill)
-        return carry
-
-    lax.fori_loop(0, count, block, 0, unroll=True)
-
-
-def sems_rows(share):
-    return -(-(share + 15) // 16) * 16
-
-
-def other_kernel(share, parts, residual, gain, weight, blocks, scaled, squares, held, sems):
-    def first():
-        projected = sum(parts[k] for k in range(parts.shape[0]))
-        stream = residual[...].astype(F32) + projected
-        squares[...] = jnp.broadcast_to(
-            jnp.sum(stream * stream, axis=1, keepdims=True), squares.shape
-        )
-        scaled[...] = (stream * gain[...]).astype(BF16)
-        return scaled[...]
-
-    head_blocks(True, share, first, lambda: squares[:, 0:1], weight, blocks, held, sems)
-
-
-def same_kernel(share, scaled, squares, weight, blocks, held, sems):
-    head_blocks(
-        False, share, lambda: scaled[...], lambda: squares[:, 0:1], weight, blocks, held, sems
-    )
+
+
+def other_kernel(share, vocab, parts, residual, gain, weight, blocks, scaled, squares):
+    projected = sum(parts[k] for k in range(parts.shape[0]))
+    stream = residual[...].astype(F32) + projected
+    fill = jnp.sum(stream * stream, axis=1, keepdims=True)
+    squares[...] = jnp.broadcast_to(fill, squares.shape)
+    left = (stream * gain[...]).astype(BF16)
+    scaled[...] = left
+    head_blocks(True, share, vocab, left, fill, weight, blocks)
+
+
+def same_kernel(share, vocab, scaled, squares, weight, blocks):
+    head_blocks(False, share, vocab, scaled[...], squares[:, 0:1], weight, blocks)
 
 
 def add_kernel(one, two, out):
@@ -217,7 +258,7 @@
     return jnp.sum(jnp.where(iota(shape, 0) == iota(shape, 1), values, 0.0), axis=1, keepdims=True)
 
 
-def stats_kernel(share, vocab, targets, parts, logits, spread):
+def stats_kernel(share, vocab, wanted, parts, logits, spread):
     rows, padded = logits.shape
     summed = sum(parts[k] for k in range(parts.shape[0]))
     inverse = lax.rsqrt(summed[:, share : share + 1] * (1.0 / D) + NORM_EPS)
@@ -227,12 +268,8 @@
     logits[...] = local
     peak = jnp.max(jnp.where(valid, local, -jnp.inf), axis=1, keepdims=True)
     total = jnp.sum(jnp.where(valid, jnp.exp(local - peak), 0.0), axis=1, keepdims=True)
-    row = iota((rows, 1), 0)
-    wanted = jnp.zeros((rows, 1), jnp.int32)
-    for b in range(rows // 2):
-        wanted = jnp.where(lax.rem(row, rows // 2) == b, targets[b], wanted)
     start = lax.axis_index("tp") * vocab + lax.axis_index("ctx") * share
-    hit = jnp.logical_and(valid, lane + start == wanted)
+    hit = jnp.logical_and(valid, lane + start == wanted[:, 0:1])
     picks = jnp.sum(jnp.where(hit, local, 0.0), axis=1, keepdims=True)
     place = iota((rows, 128), 1)
     mixed = jnp.where(place < rows, peak, jnp.where(place < 2 * rows, total, picks))
@@ -269,10 +306,10 @@
     scores[...] = result[:, :share]
 
 
-def call(kernel, out, in_specs, name, scratch=(), flops=0, moved=0):
-    outs = [jax.ShapeDtypeStruct(shape, kind) for shape, kind in out]
+def call(kernel, out, in_specs, name, scratch=(), flops=0, moved=0, near=pltpu.VMEM):
+    outs = [near(shape, kind) for shape, kind in out]
     specs = [VMEM] * len(outs)
-    return pl.pallas_call(
+    run = pl.pallas_call(
         kernel,
         out_shape=outs if len(outs) > 1 else outs[0],
         in_specs=in_specs,
@@ -280,8 +317,18 @@
         scratch_shapes=list(scratch),
         name=name,
         cost_estimate=pl.CostEstimate(flops=flops, bytes_accessed=moved, transcendentals=0),
-        compiler_params=pltpu.CompilerParams(vmem_limit_bytes=24 * 1024 * 1024),
-    )
+        compiler_params=pltpu.CompilerParams(vmem_limit_bytes=16 * 1024 * 1024),
+    )
+
+    def pinned(*operands):
+        return run(
+            *(
+                pltpu.with_memory_space_constraint(operand, pltpu.HBM) if spec is ANY else operand
+                for operand, spec in zip(operands, in_specs)
+            )
+        )
+
+    return pinned
 
 
 def per_device(
@@ -318,49 +365,76 @@
     state = call(
         functools.partial(long_kernel, chunks),
         [((packed, 128), F32)],
-        [SMEM, VMEM, ANY],
+        [ANY, ANY, ANY],
         "long_attention",
         [
             pltpu.VMEM(long_rows.shape, BF16),
+            pltpu.VMEM((pairs, HEAD_DIM), BF16),
+            pltpu.SMEM((row_count,), jnp.int32),
             pltpu.VMEM((pairs, HEAD_DIM), F32),
             pltpu.VMEM((pairs, HEAD_DIM), F32),
-            pltpu.SemaphoreType.DMA((2 * chunks,)),
+            pltpu.SemaphoreType.DMA((2 * chunks + 2,)),
         ],
         moved=2 * 1024 * 1024,
     )(lengths, flat_queries, long_rows)
     other = lax.ppermute(state, "ctx", cores)
-    aux = call(
-        short_kernel, [((3, pairs, HEAD_DIM), F32)], [VMEM] * 3, "short_attention", moved=1024 * 1024
-    )(flat_queries, short_rows, fresh)
     spread = call(pair_kernel, [((chips, packed, 128), F32)], [VMEM] * 2, "merge_cores")(
         state, other
     )
+    spread, fresh = lax.optimization_barrier((spread, fresh))
     states = lax.all_to_all(spread, "ctx", 0, 0, tiled=True, axis_index_groups=same_core)
+    reach = -(-fetched_rows(share) // 128) * 128
+    aux, out_near, head_near, residual_near, gain_near, wanted = call(
+        functools.partial(short_kernel, share),
+        [
+            ((3, pairs, HEAD_DIM), F32),
+            (out_weight.shape, BF16),
+            ((ctx_size, reach, width), BF16),
+            ((rows, width), BF16),
+            ((1, width), F32),
+            ((rows, 128), jnp.int32),
+        ],
+        [ANY] * 8,
+        "short_attention",
+        [
+            pltpu.VMEM(flat_queries.shape, BF16),
+            pltpu.VMEM(short_rows.shape, BF16),
+            pltpu.VMEM(fresh.shape, BF16),
+            pltpu.SMEM((row_count,), jnp.int32),
+            pltpu.SemaphoreType.DMA((8,)),
+            pltpu.SemaphoreType.DMA((ctx_size,)),
+        ],
+        moved=10 * 1024 * 1024,
+    )(
+        flat_queries,
+        short_rows,
+        fresh,
+        out_weight,
+        head_weight.T,
+        residual.reshape(rows, width),
+        final_gain.reshape(1, width),
+        targets,
+    )
     spread = call(project_kernel, [((tp_size, rows, width), F32)], [VMEM] * 3, "project")(
-        states, aux, out_weight
+        states, aux, out_near
     )
     parts = lax.all_to_all(spread, "tp", 0, 0, tiled=True)
 
-    weight_rows = head_weight.T
-    reach = -(-sems_rows(share) // 128) * 128
-    scratch = [pltpu.VMEM((chips, reach, width), BF16), pltpu.SemaphoreType.DMA((chips,))]
     theirs, scaled, squares = call(
-        functools.partial(other_kernel, share),
+        functools.partial(other_kernel, share, vocab),
         [((chips, rows, padded), F32), ((rows, width), BF16), ((rows, 128), F32)],
-        [VMEM, VMEM, VMEM, ANY],
+        [VMEM] * 4,
         "head_other",
-        scratch,
         moved=4 * 1024 * 1024,
-    )(parts, residual.reshape(rows, width), final_gain.reshape(1, width), weight_rows)
+    )(parts, residual_near, gain_near, head_near)
     arrived = lax.ppermute(theirs, "ctx", cores)
     mine = call(
-        functools.partial(same_kernel, share),
+        functools.partial(same_kernel, share, vocab),
         [((chips, rows, padded), F32)],
-        [VMEM, VMEM, ANY],
+        [VMEM] * 3,
         "head_same",
-        scratch,
         moved=4 * 1024 * 1024,
-    )(scaled, squares, weight_rows)
+    )(scaled, squares, head_near)
     blocks = call(add_kernel, [((chips, rows, padded), F32)], [VMEM] * 2, "add_cores")(
         mine, arrived
     )
@@ -370,9 +444,9 @@
     logits, spread = call(
         functools.partial(stats_kernel, share, vocab),
         [((rows, padded), F32), ((devices, 128), F32)],
-        [SMEM, VMEM],
+        [VMEM, VMEM],
         "vocab_stats",
-    )(targets, parts)
+    )(wanted, parts)
     everyone = lax.all_to_all(
         spread.reshape(devices, 1, 128), ("ctx", "tp"), 0, 0, tiled=True
     ).reshape(devices, 128)
@@ -381,6 +455,7 @@
         [((row_count, share), F32), ((1, row_count), F32)],
         [VMEM, VMEM],
         "scores",
+        near=jax.ShapeDtypeStruct,
     )(everyone, logits)
     return (scores, chosen.reshape(row_count))
 

time: 100 us -> 88.4 us (0.88)
  waiting for transfers between devices: 7.07 us -> 1.67 us
  Pallas kernels: 18.8 us -> 15.1 us
  local copies, waits for them, and re-layouts: 11.4 us -> 7.95 us
  blocking collectives: 49.3 us -> 50.6 us
    all_to_all x1, waiting for transfers between devices: 6.2 us -> 0.8 us  [per_device(): lax.all_to_all(spread, 'ctx', 0, 0, tiled=True, axis_index_groups=same_core)]
    pallas_call x9, Pallas kernels: 18.8 us -> 15.1 us  [pinned(): run(*(pltpu.with_memory_space_constraint(operand, pltpu.HBM) if spec is A...]
    unnamed x24 -> x4, local copies, waits for them, and re-layouts: 11.4 us -> 7.95 us
    all_to_all x1, blocking collectives: 13.1 us -> 14.7 us  [per_device(): lax.all_to_all(blocks, 'ctx', 0, 0, tiled=True, axis_index_groups=same_core)]
  transfers between devices with their start and end apart: 3 -> 3, of which waited for: 2 -> 2; matrix products, arithmetic and copies ran while one was open for 0% -> 0% of each run, Pallas kernels for 7% -> 9%
where the time goes in v3:
time: 88.4 us; the launch traced here: 88.1 us
  blocking collectives  50.6 us (57%)
  Pallas kernels  15.1 us (17%)
  starting transfers between devices  12 us (14%)
  local copies, waits for them, and re-layouts  7.95 us (9%)
  waiting for transfers between devices  1.67 us (2%)
    all_to_all x1, blocking collectives, per_device(): lax.all_to_all(spread.reshape(devices, 1, 128), ('ctx', 'tp'), 0, 0, tile...  20 us
    all_to_all x1, blocking collectives, per_device(): parts = lax.all_to_all(spread, 'tp', 0, 0, tiled=True)  16 us
    pallas_call x9, Pallas kernels, pinned(): run(*(pltpu.with_memory_space_constraint(operand, pltpu.HBM) if spec is A...  15.1 us
    all_to_all x1, blocking collectives, per_device(): lax.all_to_all(blocks, 'ctx', 0, 0, tiled=True, axis_index_groups=same_core)  14.7 us
    unnamed x4, local copies, waits for them, and re-layouts  7.95 us
    all_to_all x1, starting transfers between devices, per_device(): lax.all_to_all(spread, 'ctx', 0, 0, tiled=True, axis_index_groups=same_core)  5.02 us
    ppermute x1, starting transfers between devices, per_device(): arrived = lax.ppermute(theirs, 'ctx', cores)  3.69 us
    ppermute x1, starting transfers between devices, per_device(): other = lax.ppermute(state, 'ctx', cores)  3.33 us
  transfers between devices with their start and end apart: 3, of which 2 were waited for; matrix products, arithmetic and copies ran while one was open for 0% of the time, Pallas kernels for 9%

profile of v3, /device:TPU:1, one launch (start us, length us, event | category | flops | bytes accessed | tf_op | source)
XLA Modules:
  0.0 88.1 jit_solution(9169036554222193213)
XLA Ops:
  0.6 3.2 %long_attention.1.one = f32[72,128]{1,0:T(8,128)S(1)} custom-call(s32[8]{0:T(128)} %lengths_far.1, bf16[2,64,128]{2,1,0:T(8,128)(2,1)} %bitcast.17, bf16[2,8,512,128]{3,2,1,0:T(8,128)(2,1)} %bitcast.15), custom_call_target="tpu_custom_call" | custom-call | bytes 2097152 | tf_op jit(solution)/shard_map/long_attention/pallas_call | solution.py:324
  3.9 3.3 %collective-permute-start = (f32[72,128]{1,0:T(8,128)S(1)}, f32[72,128]{1,0:T(8,128)S(1)}, u32[]{:S(2)}, u32[]{:S(2)}) collective-permute-start(f32[72,128]{1,0:T(8,128)S(1)} %long_attention.1.one), channel_id=1, source_target_pairs={{0,8},{8,0},{16,24},{24,16},{32,40},{40,32},{48,56},{56,48},{64,72... | collective-permute-start | bytes 110600 | tf_op jit(solution)/shard_map/ppermute | solution.py:380
  7.2 0.9 collective-permute-done.two
  8.1 0.9 %merge_cores.1 = f32[16,72,128]{2,1,0:T(8,128)} custom-call(f32[72,128]{1,0:T(8,128)S(1)} %long_attention.1.one, f32[72,128]{1,0:T(8,128)S(1)} %collective-permute-done.two), custom_call_target="tpu_custom_call" | custom-call | tf_op jit(solution)/shard_map/merge_cores/pallas_call | solution.py:324
  9.0 5.0 %all-to-all-start = ((f32[16,72,128]{2,1,0:T(8,128)}), f32[16,72,128]{2,1,0:T(8,128)S(1)}, u32[]{:S(2)}, u32[]{:S(2)}) async-start(f32[16,72,128]{2,1,0:T(8,128)} %merge_cores.1), calls=%async_computation | async-start | bytes 1179648 | tf_op jit(solution)/shard_map/all_to_all | solution.py:385
  14.0 6.1 %short_attention.1 = (f32[3,64,128]{2,1,0:T(8,128)S(1)}, bf16[1024,256]{1,0:T(8,128)(2,1)S(1)}, bf16[32,640,256]{2,1,0:T(8,128)(2,1)S(1)}, bf16[16,256]{1,0:T(8,...) custom-call(bf16[2,64,128]{2,1,0:T(8,128)(2,1)} %bitcast.18, bf16[2,8,256,128]{3,2,1,0:T(8,128)(2,1)} %bitcast.16, ...), custom_call_target="tpu_custom_call" | custom-call | bytes 10485760 | tf_op jit(solution)/shard_map/short_attention/pallas_call | solution.py:324
  20.1 0.0 copy-start
  20.1 4.0 %copy-done = bf16[32,640,256]{2,1,0:T(8,128)(2,1)} copy-done((bf16[32,640,256]{2,1,0:T(8,128)(2,1)}, bf16[32,640,256]{2,1,0:T(8,128)(2,1)S(1)}, u32[]{:S(2)}) %copy-start) | copy-done | bytes 10485784
  24.1 0.8 all-to-all-done.states
  24.9 0.5 project.1
  25.4 16.0 %all_to_all.20.parts = f32[8,16,256]{2,1,0:T(8,128)S(1)} all-to-all(f32[8,16,256]{2,1,0:T(8,128)S(1)} %project.1), channel_id=1, replica_groups=mesh['ctx'=32,'tp'=8] {'tp'}, dimensions={0} | all-to-all | bytes 262144 | tf_op jit(solution)/shard_map/all_to_all | solution.py:421
  41.4 0.0 copy-start.1
  41.4 4.0 %copy-done.1 = bf16[32,640,256]{2,1,0:T(8,128)(2,1)S(1)} copy-done((bf16[32,640,256]{2,1,0:T(8,128)(2,1)S(1)}, bf16[32,640,256]{2,1,0:T(8,128)(2,1)}, u32[]{:S(2)}) %copy-start.1) | copy-done | bytes 10485784
  45.4 1.6 %head_other.1 = (f32[16,16,512]{2,1,0:T(8,128)S(1)}, bf16[16,256]{1,0:T(8,128)(2,1)S(1)}, f32[16,128]{1,0:T(8,128)S(1)}) custom-call(f32[8,16,256]{2,1,0:T(8,128)S(1)} %all_to_all.20.parts, bf16[16,256]{1,0:T(8,128)(2,1)S(1)} %get-tuple-element.22.residual, f32[1,256]{1,0:T(1,128)S(1)} %get-tuple-element.23.gain, bf16[32,640,256]{2,1,0:T(8,128)(2,1)S(1)} %copy-done.1), custom_call_target="tpu_custom_call" | custom-call | bytes 4194304 | tf_op jit(solution)/shard_map/head_other/pallas_call | solution.py:324
  46.9 3.7 %collective-permute-start.1 = (f32[16,16,512]{2,1,0:T(8,128)S(1)}, f32[16,16,512]{2,1,0:T(8,128)S(1)}, u32[]{:S(2)}, u32[]{:S(2)}) collective-permute-start(f32[16,16,512]{2,1,0:T(8,128)S(1)} %get-tuple-element.27), channel_id=1, source_target_pairs={{0,8},{8,0},{16,24},{24,16},{32,40},{40,32},{48,56},{56,48},{64,72... | collective-permute-start | bytes 1572872 | tf_op jit(solution)/shard_map/ppermute | solution.py:430
  50.6 1.5 %head_same.1.one = f32[16,16,512]{2,1,0:T(8,128)S(1)} custom-call(bf16[16,256]{1,0:T(8,128)(2,1)S(1)} %get-tuple-element.25.scaled, f32[16,128]{1,0:T(8,128)S(1)} %get-tuple-element.26.squares, bf16[32,640,256]{2,1,0:T(8,128)(2,1)S(1)} %copy-done.1), custom_call_target="tpu_custom_call" | custom-call | bytes 4194304 | tf_op jit(solution)/shard_map/head_same/pallas_call | solution.py:324
  52.2 0.0 collective-permute-done.1.two
  52.2 0.1 add_cores.1
  52.3 14.7 %all_to_all.21.parts = f32[16,16,512]{2,1,0:T(8,128)S(1)} all-to-all(f32[16,16,512]{2,1,0:T(8,128)S(1)} %add_cores.1), channel_id=1, replica_groups={{0,16,32,48,64,80,96,112,128,144,160,176,192,208,224,240},{8,24,40,56,7..., dimensions={0} | all-to-all | bytes 1048576 | tf_op jit(solution)/shard_map/all_to_all | solution.py:441
  66.9 0.3 vocab_stats.1
  67.2 20.0 %all_to_all.22 = f32[256,1,128]{2,1,0:T(1,128)S(1)} all-to-all(f32[256,1,128]{2,1,0:T(1,128)S(1)} %bitcast.13), channel_id=1, replica_groups=mesh['ctx'=32,'tp'=8] {'ctx','tp'}, dimensions={0} | all-to-all | bytes 262144 | tf_op jit(solution)/shard_map/all_to_all | solution.py:450
  87.2 0.9 %scores.1 = (f32[8,501]{1,0:T(8,128)}, f32[1,8]{1,0:T(1,128)}) custom-call(f32[256,128]{1,0:T(8,128)S(1)} %bitcast.12, f32[16,512]{1,0:T(8,128)S(1)} %get-tuple-element.29.logits), custom_call_target="tpu_custom_call" | custom-call | tf_op jit(solution)/shard_map/scores/pallas_call | solution.py:324
Async XLA Ops:
  3.9 4.2 %collective-permute-start = (f32[72,128]{1,0:T(8,128)S(1)}, f32[72,128]{1,0:T(8,128)S(1)}, u32[]{:S(2)}, u32[]{:S(2)}) collective-permute-start(f32[72,128]{1,0:T(8,128)S(1)} %long_attention.1.one), channel_id=1, source_target_pairs={{0,8},{8,0},{16,24},{24,16},{32,40},{40,32},{48,56},{56,48},{64,72... | collective-permute-start | bytes 110600 | tf_op jit(solution)/shard_map/ppermute | solution.py:380
  9.0 15.9 %all-to-all-start = ((f32[16,72,128]{2,1,0:T(8,128)}), f32[16,72,128]{2,1,0:T(8,128)S(1)}, u32[]{:S(2)}, u32[]{:S(2)}) async-start(f32[16,72,128]{2,1,0:T(8,128)} %merge_cores.1), calls=%async_computation | async-start | bytes 1179648 | tf_op jit(solution)/shard_map/all_to_all | solution.py:385
  20.1 4.0 %copy-start = (bf16[32,640,256]{2,1,0:T(8,128)(2,1)}, bf16[32,640,256]{2,1,0:T(8,128)(2,1)S(1)}, u32[]{:S(2)}) copy-start(bf16[32,640,256]{2,1,0:T(8,128)(2,1)S(1)} %get-tuple-element.24.weight) | copy-start | bytes 31457284
  41.4 4.0 %copy-start.1 = (bf16[32,640,256]{2,1,0:T(8,128)(2,1)S(1)}, bf16[32,640,256]{2,1,0:T(8,128)(2,1)}, u32[]{:S(2)}) copy-start(bf16[32,640,256]{2,1,0:T(8,128)(2,1)} %copy-done) | copy-start | bytes 31457284
  46.9 5.2 %collective-permute-start.1 = (f32[16,16,512]{2,1,0:T(8,128)S(1)}, f32[16,16,512]{2,1,0:T(8,128)S(1)}, u32[]{:S(2)}, u32[]{:S(2)}) collective-permute-start(f32[16,16,512]{2,1,0:T(8,128)S(1)} %get-tuple-element.27), channel_id=1, source_target_pairs={{0,8},{8,0},{16,24},{24,16},{32,40},{40,32},{48,56},{56,48},{64,72... | collective-permute-start | bytes 1572872 | tf_op jit(solution)/shard_map/ppermute | solution.py:430

commit v4 on v3

--- a/solution.py
+++ b/solution.py
@@ -85,18 +85,15 @@
 
 
 def short_kernel(
-    share,
     queries_far,
     cache_far,
     fresh_far,
     out_far,
-    head_far,
     residual_far,
     gain_far,
     targets_far,
     aux,
     out_near,
-    head_near,
     residual,
     gain,
     wanted,
@@ -105,7 +102,6 @@
     fresh,
     targets,
     sems,
-    head_sems,
 ):
     moves = (
         (queries_far, queries),
@@ -119,17 +115,6 @@
     )
     copies = [pltpu.make_async_copy(*move, sems.at[n]) for n, move in enumerate(moves)]
     for copy in copies:
-        copy.start()
-    fetched = fetched_rows(share)
-    blocks = [
-        pltpu.make_async_copy(
-            head_far.at[pl.ds(min(j * share // 16 * 16, head_far.shape[0] - fetched), fetched)],
-            head_near.at[j, pl.ds(0, fetched)],
-            head_sems.at[j],
-        )
-        for j in range(head_near.shape[0])
-    ]
-    for copy in blocks:
         copy.start()
     for copy in copies:
         copy.wait()
@@ -162,8 +147,6 @@
         aux[0, where, :] = mixed / (total * older + newer)
         aux[1, where, :] = jnp.broadcast_to(own[0], (heads, HEAD_DIM))
         aux[2, where, :] = jnp.broadcast_to(value[0][b : b + 1], (heads, HEAD_DIM))
-    for copy in blocks:
-        copy.wait()
 
 
 def merge_states(parts):
@@ -221,32 +204,56 @@
     return -(-(share + 15) // 16) * 16
 
 
-def head_blocks(other, share, vocab, left, fill, weight, blocks):
+def block_start(j, share, vocab):
+    return jnp.minimum(j * share // 16 * 16, vocab - fetched_rows(share))
+
+
+def head_block(k, which, share, vocab, left, fill, weight, blocks):
     padded, reach = blocks.shape[2], weight.shape[1]
+    j = 2 * k + which
+    ahead = j * share - block_start(j, share, vocab)
+    product = dot_rows(left, weight[k])
+    moved = pltpu.roll(product, lax.rem(reach - ahead, reach), 1)[:, :padded]
+    lane = iota(moved.shape, 1)
+    blocks[k] = jnp.where(lane < share, moved, fill)
+
+
+def other_kernel(
+    share, group, parts, residual, gain, weight, blocks, scaled, squares, kept, held, sems
+):
+    vocab, count = weight.shape[0], blocks.shape[0]
+    fetched = fetched_rows(share)
     core = lax.rem(lax.axis_index("ctx"), 2)
-    which = 1 - core if other else core
-    lane = iota((blocks.shape[1], padded), 1)
-    for k in range(blocks.shape[0]):
-        j = 2 * k + which
-        offset = j * share
-        ahead = offset - jnp.minimum(offset // 16 * 16, vocab - fetched_rows(share))
-        product = dot_rows(left, weight[j])
-        moved = pltpu.roll(product, lax.rem(reach - ahead, reach), 1)[:, :padded]
-        blocks[k] = jnp.where(lane < share, moved, fill)
-
-
-def other_kernel(share, vocab, parts, residual, gain, weight, blocks, scaled, squares):
+
+    def copy(k, which, place, sem):
+        base = pl.multiple_of(block_start(2 * k + which, share, vocab), 16)
+        return pltpu.make_async_copy(
+            weight.at[pl.ds(base, fetched)], place.at[k, pl.ds(0, fetched)], sem
+        )
+
+    first = [copy(k, 1 - core, held, sems.at[k]) for k in range(count)]
+    second = [copy(k, core, kept, sems.at[count + k]) for k in range(count)]
+    for one in first + second:
+        one.start()
     projected = sum(parts[k] for k in range(parts.shape[0]))
     stream = residual[...].astype(F32) + projected
     fill = jnp.sum(stream * stream, axis=1, keepdims=True)
     squares[...] = jnp.broadcast_to(fill, squares.shape)
     left = (stream * gain[...]).astype(BF16)
     scaled[...] = left
-    head_blocks(True, share, vocab, left, fill, weight, blocks)
+    for start in range(0, count, group):
+        for one in first[start : start + group]:
+            one.wait()
+        for k in range(start, start + group):
+            head_block(k, 1 - core, share, vocab, left, fill, held, blocks)
+    for one in second:
+        one.wait()
 
 
 def same_kernel(share, vocab, scaled, squares, weight, blocks):
-    head_blocks(False, share, vocab, scaled[...], squares[:, 0:1], weight, blocks)
+    core = lax.rem(lax.axis_index("ctx"), 2)
+    for k in range(blocks.shape[0]):
+        head_block(k, core, share, vocab, scaled[...], squares[:, 0:1], weight, blocks)
 
 
 def add_kernel(one, two, out):
@@ -383,18 +390,16 @@
     )
     spread, fresh = lax.optimization_barrier((spread, fresh))
     states = lax.all_to_all(spread, "ctx", 0, 0, tiled=True, axis_index_groups=same_core)
-    reach = -(-fetched_rows(share) // 128) * 128
-    aux, out_near, head_near, residual_near, gain_near, wanted = call(
-        functools.partial(short_kernel, share),
+    aux, out_near, residual_near, gain_near, wanted = call(
+        short_kernel,
         [
             ((3, pairs, HEAD_DIM), F32),
             (out_weight.shape, BF16),
-            ((ctx_size, reach, width), BF16),
             ((rows, width), BF16),
             ((1, width), F32),
             ((rows, 128), jnp.int32),
         ],
-        [ANY] * 8,
+        [ANY] * 7,
         "short_attention",
         [
             pltpu.VMEM(flat_queries.shape, BF16),
@@ -402,15 +407,13 @@
             pltpu.VMEM(fresh.shape, BF16),
             pltpu.SMEM((row_count,), jnp.int32),
             pltpu.SemaphoreType.DMA((8,)),
-            pltpu.SemaphoreType.DMA((ctx_size,)),
-        ],
-        moved=10 * 1024 * 1024,
+        ],
+        moved=2 * 1024 * 1024,
     )(
         flat_queries,
         short_rows,
         fresh,
         out_weight,
-        head_weight.T,
         residual.reshape(rows, width),
         final_gain.reshape(1, width),
         targets,
@@ -420,13 +423,23 @@
     )
     parts = lax.all_to_all(spread, "tp", 0, 0, tiled=True)
 
-    theirs, scaled, squares = call(
-        functools.partial(other_kernel, share, vocab),
-        [((chips, rows, padded), F32), ((rows, width), BF16), ((rows, 128), F32)],
-        [VMEM] * 4,
+    reach = -(-fetched_rows(share) // 128) * 128
+    theirs, scaled, squares, head_near = call(
+        functools.partial(other_kernel, share, chips // 4),
+        [
+            ((chips, rows, padded), F32),
+            ((rows, width), BF16),
+            ((rows, 128), F32),
+            ((chips, reach, width), BF16),
+        ],
+        [VMEM, VMEM, VMEM, ANY],
         "head_other",
-        moved=4 * 1024 * 1024,
-    )(parts, residual_near, gain_near, head_near)
+        [
+            pltpu.VMEM((chips, reach, width), BF16),
+            pltpu.SemaphoreType.DMA((2 * chips,)),
+        ],
+        moved=8 * 1024 * 1024,
+    )(parts, residual_near, gain_near, head_weight.T)
     arrived = lax.ppermute(theirs, "ctx", cores)
     mine = call(
         functools.partial(same_kernel, share, vocab),

time: 88.4 us -> 85.3 us (0.965)
  local copies, waits for them, and re-layouts: 7.95 us -> 0 us
  waiting for transfers between devices: 1.67 us -> 8.27 us
  blocking collectives: 50.6 us -> 49.3 us
    unnamed x4 -> x0, local copies, waits for them, and re-layouts: 7.95 us -> none
    all_to_all x1, waiting for transfers between devices: 0.8 us -> 7.4 us  [per_device(): lax.all_to_all(spread, 'ctx', 0, 0, tiled=True, axis_index_groups=same_core)]
    all_to_all x1, blocking collectives: 14.7 us -> 13.3 us  [per_device(): lax.all_to_all(blocks, 'ctx', 0, 0, tiled=True, axis_index_groups=same_core)]
  transfers between devices with their start and end apart: 3 -> 3, of which waited for: 2 -> 2; matrix products, arithmetic and copies ran while one was open for 0% -> 0% of each run, Pallas kernels for 9% -> 6%
where the time goes in v4:
time: 85.3 us; the launch traced here: 84.9 us
  blocking collectives  49.3 us (58%)
  Pallas kernels  14.6 us (17%)
  starting transfers between devices  12 us (14%)
  waiting for transfers between devices  8.27 us (10%)
    all_to_all x1, blocking collectives, per_device(): lax.all_to_all(spread.reshape(devices, 1, 128), ('ctx', 'tp'), 0, 0, tile...  20 us
    all_to_all x1, blocking collectives, per_device(): parts = lax.all_to_all(spread, 'tp', 0, 0, tiled=True)  16 us
    pallas_call x9, Pallas kernels, pinned(): run(*(pltpu.with_memory_space_constraint(operand, pltpu.HBM) if spec is A...  14.6 us
    all_to_all x1, blocking collectives, per_device(): lax.all_to_all(blocks, 'ctx', 0, 0, tiled=True, axis_index_groups=same_core)  13.3 us
    all_to_all x1, waiting for transfers between devices, per_device(): lax.all_to_all(spread, 'ctx', 0, 0, tiled=True, axis_index_groups=same_core)  7.4 us
    all_to_all x1, starting transfers between devices, per_device(): lax.all_to_all(spread, 'ctx', 0, 0, tiled=True, axis_index_groups=same_core)  5.02 us
    ppermute x1, starting transfers between devices, per_device(): arrived = lax.ppermute(theirs, 'ctx', cores)  3.69 us
    ppermute x1, starting transfers between devices, per_device(): other = lax.ppermute(state, 'ctx', cores)  3.33 us
  transfers between devices with their start and end apart: 3, of which 2 were waited for; matrix products, arithmetic and copies ran while one was open for 0% of the time, Pallas kernels for 6%

profile of v4, /device:TPU:1, one launch (start us, length us, event | category | flops | bytes accessed | tf_op | source)
XLA Modules:
  0.0 84.9 jit_solution(17660723340463836290)
XLA Ops:
  0.6 3.2 %long_attention.1.one = f32[72,128]{1,0:T(8,128)S(1)} custom-call(s32[8]{0:T(128)} %lengths_far.1, bf16[2,64,128]{2,1,0:T(8,128)(2,1)} %bitcast.17, bf16[2,8,512,128]{3,2,1,0:T(8,128)(2,1)} %bitcast.15), custom_call_target="tpu_custom_call" | custom-call | bytes 2097152 | tf_op jit(solution)/shard_map/long_attention/pallas_call | solution.py:331
  3.9 3.3 %collective-permute-start = (f32[72,128]{1,0:T(8,128)S(1)}, f32[72,128]{1,0:T(8,128)S(1)}, u32[]{:S(2)}, u32[]{:S(2)}) collective-permute-start(f32[72,128]{1,0:T(8,128)S(1)} %long_attention.1.one), channel_id=1, source_target_pairs={{0,8},{8,0},{16,24},{24,16},{32,40},{40,32},{48,56},{56,48},{64,72... | collective-permute-start | bytes 110600 | tf_op jit(solution)/shard_map/ppermute | solution.py:387
  7.2 0.9 %collective-permute-done.two = f32[72,128]{1,0:T(8,128)S(1)} collective-permute-done((f32[72,128]{1,0:T(8,128)S(1)}, f32[72,128]{1,0:T(8,128)S(1)}, u32[]{:S(2)}, u32[]{:S(2)}) %collective-permute-start) | collective-permute-done | bytes 36896 | tf_op jit(solution)/shard_map/ppermute | solution.py:387
  8.1 0.9 %merge_cores.1 = f32[16,72,128]{2,1,0:T(8,128)} custom-call(f32[72,128]{1,0:T(8,128)S(1)} %long_attention.1.one, f32[72,128]{1,0:T(8,128)S(1)} %collective-permute-done.two), custom_call_target="tpu_custom_call" | custom-call | tf_op jit(solution)/shard_map/merge_cores/pallas_call | solution.py:331
  8.9 5.0 %all-to-all-start = ((f32[16,72,128]{2,1,0:T(8,128)}), f32[16,72,128]{2,1,0:T(8,128)S(1)}, u32[]{:S(2)}, u32[]{:S(2)}) async-start(f32[16,72,128]{2,1,0:T(8,128)} %merge_cores.1), calls=%async_computation | async-start | bytes 1179648 | tf_op jit(solution)/shard_map/all_to_all | solution.py:392
  14.0 3.5 %short_attention.1 = (f32[3,64,128]{2,1,0:T(8,128)S(1)}, bf16[1024,256]{1,0:T(8,128)(2,1)S(1)}, bf16[16,256]{1,0:T(8,128)(2,1)S(1)}, f32[1,256]{1,0:T(1,128)S(1)}, s32[16,128]{1,0:T(8,128)S(1)}) custom-call(bf16[2,64,128]{2,1,0:T(8,128)(2,1)} %bitcast.18, bf16[2,8,256,128]{3,2,1,0:T(8,128)(2,1)} %bitcast.16, bf16[2,2,8,128]{3,2,1,0:T(8,128)(2,1)} %bitcast.19, ...), custom_call_target="tpu_custom_call" | custom-call | bytes 2097152 | tf_op jit(solution)/shard_map/short_attention/pallas_call | solution.py:331
  17.4 7.4 %all-to-all-done.states = f32[16,72,128]{2,1,0:T(8,128)S(1)} async-done(((f32[16,72,128]{2,1,0:T(8,128)}), f32[16,72,128]{2,1,0:T(8,128)S(1)}, u32[]{:S(2)}, u32[]{:S(2)}) %all-to-all-start) | async-done | bytes 589856 | tf_op jit(solution)/shard_map/all_to_all | solution.py:392
  24.8 0.5 project.1
  25.4 16.0 %all_to_all.20.parts = f32[8,16,256]{2,1,0:T(8,128)S(1)} all-to-all(f32[8,16,256]{2,1,0:T(8,128)S(1)} %project.1), channel_id=1, replica_groups=mesh['ctx'=32,'tp'=8] {'tp'}, dimensions={0} | all-to-all | bytes 262144 | tf_op jit(solution)/shard_map/all_to_all | solution.py:424
  41.4 3.8 %head_other.1 = (f32[16,16,512]{2,1,0:T(8,128)S(1)}, bf16[16,256]{1,0:T(8,128)(2,1)S(1)}, f32[16,128]{1,0:T(8,128)S(1)}, bf16[16,640,256]{2,1,0:T(8,128)(2,1)S(1)}) custom-call(f32[8,16,256]{2,1,0:T(8,128)S(1)} %all_to_all.20.parts, bf16[16,256]{1,0:T(8,128)(2,1)S(1)} %get-tuple-element.22.residual, f32[1,256]{1,0:T(1,128)S(1)} %get-tuple-element.23.gain, ...), custom_call_target="tpu_custom_call" | custom-call | bytes 8388608 | tf_op jit(solution)/shard_map/head_other/pallas_call | solution.py:331
  45.1 3.7 %collective-permute-start.1 = (f32[16,16,512]{2,1,0:T(8,128)S(1)}, f32[16,16,512]{2,1,0:T(8,128)S(1)}, u32[]{:S(2)}, u32[]{:S(2)}) collective-permute-start(f32[16,16,512]{2,1,0:T(8,128)S(1)} %get-tuple-element.27), channel_id=1, source_target_pairs={{0,8},{8,0},{16,24},{24,16},{32,40},{40,32},{48,56},{56,48},{64,72... | collective-permute-start | bytes 1572872 | tf_op jit(solution)/shard_map/ppermute | solution.py:443
  48.8 1.6 %head_same.1.one = f32[16,16,512]{2,1,0:T(8,128)S(1)} custom-call(bf16[16,256]{1,0:T(8,128)(2,1)S(1)} %get-tuple-element.24.scaled, f32[16,128]{1,0:T(8,128)S(1)} %get-tuple-element.25.squares, bf16[16,640,256]{2,1,0:T(8,128)(2,1)S(1)} %get-tuple-element.26.weight), custom_call_target="tpu_custom_call" | custom-call | bytes 4194304 | tf_op jit(solution)/shard_map/head_same/pallas_call | solution.py:331
  50.4 0.0 collective-permute-done.1.two
  50.4 0.1 add_cores.1
  50.5 13.3 %all_to_all.21.parts = f32[16,16,512]{2,1,0:T(8,128)S(1)} all-to-all(f32[16,16,512]{2,1,0:T(8,128)S(1)} %add_cores.1), channel_id=1, replica_groups={{0,16,32,48,64,80,96,112,128,144,160,176,192,208,224,240},{8,24,40,56,7..., dimensions={0} | all-to-all | bytes 1048576 | tf_op jit(solution)/shard_map/all_to_all | solution.py:454
  63.8 0.3 vocab_stats.1
  64.1 20.0 %all_to_all.22 = f32[256,1,128]{2,1,0:T(1,128)S(1)} all-to-all(f32[256,1,128]{2,1,0:T(1,128)S(1)} %bitcast.13), channel_id=1, replica_groups=mesh['ctx'=32,'tp'=8] {'ctx','tp'}, dimensions={0} | all-to-all | bytes 262144 | tf_op jit(solution)/shard_map/all_to_all | solution.py:463
  84.0 0.9 %scores.1 = (f32[8,501]{1,0:T(8,128)}, f32[1,8]{1,0:T(1,128)}) custom-call(f32[256,128]{1,0:T(8,128)S(1)} %bitcast.12, f32[16,512]{1,0:T(8,128)S(1)} %get-tuple-element.29.logits), custom_call_target="tpu_custom_call" | custom-call | tf_op jit(solution)/shard_map/scores/pallas_call | solution.py:331
Async XLA Ops:
  3.9 4.2 %collective-permute-start = (f32[72,128]{1,0:T(8,128)S(1)}, f32[72,128]{1,0:T(8,128)S(1)}, u32[]{:S(2)}, u32[]{:S(2)}) collective-permute-start(f32[72,128]{1,0:T(8,128)S(1)} %long_attention.1.one), channel_id=1, source_target_pairs={{0,8},{8,0},{16,24},{24,16},{32,40},{40,32},{48,56},{56,48},{64,72... | collective-permute-start | bytes 110600 | tf_op jit(solution)/shard_map/ppermute | solution.py:387
  8.9 15.9 %all-to-all-start = ((f32[16,72,128]{2,1,0:T(8,128)}), f32[16,72,128]{2,1,0:T(8,128)S(1)}, u32[]{:S(2)}, u32[]{:S(2)}) async-start(f32[16,72,128]{2,1,0:T(8,128)} %merge_cores.1), calls=%async_computation | async-start | bytes 1179648 | tf_op jit(solution)/shard_map/all_to_all | solution.py:392
  45.1 5.3 %collective-permute-start.1 = (f32[16,16,512]{2,1,0:T(8,128)S(1)}, f32[16,16,512]{2,1,0:T(8,128)S(1)}, u32[]{:S(2)}, u32[]{:S(2)}) collective-permute-start(f32[16,16,512]{2,1,0:T(8,128)S(1)} %get-tuple-element.27), channel_id=1, source_target_pairs={{0,8},{8,0},{16,24},{24,16},{32,40},{40,32},{48,56},{56,48},{64,72... | collective-permute-start | bytes 1572872 | tf_op jit(solution)/shard_map/ppermute | solution.py:443

commit v5 on v2

v5 whole, which is shorter than its diff:
```python
import functools

import jax
import jax.numpy as jnp
from jax import lax
from jax.experimental import pallas as pl
from jax.experimental.pallas import tpu as pltpu
from jax.sharding import PartitionSpec as P

D = 8192
HEAD_DIM = 128
SCORE_SCALE = HEAD_DIM ** (-0.5)

NEG_FILL = -1e30
NORM_EPS = 1e-05
CONTRAST_WEIGHT = 0.5
LOG_FLOOR = -2.302585092994046

F32 = jnp.float32
BF16 = jnp.bfloat16
VMEM = pl.BlockSpec(memory_space=pltpu.VMEM)
ANY = pl.BlockSpec(memory_space=pl.ANY)


def dot_rows(left, right):
    return lax.dot_general(left, right, (((1,), (1,)), ((), ())), preferred_element_type=F32)


def iota(shape, axis):
    return lax.broadcasted_iota(jnp.int32, shape, axis)


def finish(copies):
    @pl.when(lax.axis_index("ctx") >= 0)
    def _():
        for copy in copies:
            copy.wait()


def attention_kernel(
    pieces,
    lengths_far,
    queries_far,
    long_far,
    short_far,
    fresh_far,
    targets_far,
    residual_far,
    gain_far,
    out_far,
    head_far,
    state,
    aux,
    wanted,
    residual,
    gain,
    out_near,
    head_near,
    lengths,
    targets,
    queries,
    fresh,
    long_near,
    short_near,
    wide,
    stat,
    sems,
):
    step = head_far.shape[0] // pieces // 16 * 16
    cuts = [step * n for n in range(pieces)] + [head_far.shape[0]]
    moves = [
        (lengths_far, lengths),
        (queries_far, queries),
        (long_far.at[0], long_near.at[0]),
        (fresh_far, fresh),
        (short_far.at[0], short_near.at[0]),
        (long_far.at[1], long_near.at[1]),
        (short_far.at[1], short_near.at[1]),
        (targets_far, targets),
        (residual_far, residual),
        (gain_far, gain),
        (out_far, out_near),
    ] + [
        (head_far.at[pl.ds(low, high - low)], head_near.at[pl.ds(low, high - low)])
        for low, high in zip(cuts, cuts[1:])
    ]
    copies = [pltpu.make_async_copy(*move, sems.at[n]) for n, move in enumerate(moves)]
    for copy in copies:
        copy.start()
    rows, block_len = long_far.shape[1], long_far.shape[2]
    finish(copies[:5])
    query = [queries[0].astype(F32), queries[1].astype(F32)]
    heads = query[0].shape[0] // rows
    key = [fresh[0, 0].astype(F32), fresh[1, 0].astype(F32)]
    value = [fresh[0, 1].astype(F32), fresh[1, 1].astype(F32)]
    position = lax.axis_index("ctx") * block_len + iota((heads, block_len), 1)
    lane = iota((heads, HEAD_DIM), 1)
    kept, kept_short = [], []
    for b in range(rows):
        part = [q[b * heads : (b + 1) * heads] for q in query]
        mask = position < lengths[b]
        scores = dot_rows(part[0].astype(BF16), long_near[0, b]) * SCORE_SCALE
        scores = jnp.where(mask, scores, NEG_FILL)
        top = jnp.max(scores, axis=1, keepdims=True)
        weights = jnp.where(mask, jnp.exp(scores - top), 0.0)
        total = jnp.sum(weights, axis=1, keepdims=True)
        stat[pl.ds(b, heads, stride=rows), :] = jnp.where(lane == 0, top, total)
        kept.append(weights.astype(BF16))
        own = [
            jnp.sum(part[n] * key[n][b : b + 1], axis=1, keepdims=True) * SCORE_SCALE
            for n in range(2)
        ]
        scores = dot_rows(part[1].astype(BF16), short_near[0, b]) * SCORE_SCALE
        top = jnp.max(scores, axis=1, keepdims=True)
        weights = jnp.exp(scores - top)
        final = jnp.maximum(top, own[1])
        older = jnp.exp(top - final)
        newer = jnp.exp(own[1] - final)
        scale = 1.0 / (jnp.sum(weights, axis=1, keepdims=True) * older + newer)
        kept_short.append((weights.astype(BF16), older * scale, newer * scale))
        where = pl.ds(b, heads, stride=rows)
        aux[1, where, :] = jnp.broadcast_to(own[0], (heads, HEAD_DIM))
        aux[2, where, :] = jnp.broadcast_to(value[0][b : b + 1], (heads, HEAD_DIM))
    finish(copies[5:8])
    for b in range(rows):
        where = pl.ds(b, heads, stride=rows)
        wide[where, :] = jnp.dot(kept[b], long_near[1, b], preferred_element_type=F32)
        weights, older, newer = kept_short[b]
        output = jnp.dot(weights, short_near[1, b], preferred_element_type=F32)
        aux[0, where, :] = output * older + newer * value[1][b : b + 1]
    half = HEAD_DIM // 2
    turned = wide[...].T
    state[0:half, :] = jnp.concatenate([turned[:half], turned[half:]], axis=1)
    turned = stat[...].T[:8]
    state[half : half + 8, :] = jnp.concatenate([turned, turned], axis=1)
    row = iota(wanted.shape, 0)
    aim = jnp.zeros(wanted.shape, jnp.int32)
    for b in range(rows):
        aim = jnp.where(lax.rem(row, rows) == b, targets[b], aim)
    wanted[...] = aim
    finish(copies[8:])


def merge_states(parts):
    half = HEAD_DIM // 2
    tops = [part[half : half + 1, :] for part in parts]
    peak = functools.reduce(jnp.maximum, tops)
    factors = [jnp.exp(top - peak) for top in tops]
    total = sum(part[half + 1 : half + 2, :] * f for part, f in zip(parts, factors))
    values = sum(part[0:half, :] * f for part, f in zip(parts, factors))
    return values, peak, total


def packed_stats(peak, total):
    return jnp.where(iota((8, HEAD_DIM), 0) == 0, peak, total)


def pair_kernel(one, two, spread):
    half = HEAD_DIM // 2
    values, peak, total = merge_states([one, two])
    stats = packed_stats(peak, total)
    for k in range(spread.shape[0]):
        spread[k, 0:half, :] = values
        spread[k, half : half + 8, :] = stats


def project_kernel(states, aux, weight, spread):
    half = HEAD_DIM // 2
    values, peak, total = merge_states([states.at[k] for k in range(states.shape[0])])
    blank = jnp.zeros((half - 8, HEAD_DIM), F32)
    turned = jnp.concatenate([values, packed_stats(peak, total), blank], axis=0).T
    left, right = turned[:half], turned[half:]
    lane = iota((half, HEAD_DIM), 1)
    output = jnp.where(lane < half, left, pltpu.roll(right, half, 1))
    peak, total = left[:, half : half + 1], left[:, half + 1 : half + 2]
    own = aux[1][:, 0:1]
    final = jnp.maximum(peak, own)
    older = jnp.exp(peak - final)
    newer = jnp.exp(own - final)
    attended = [(output * older + newer * aux[2]) / (total * older + newer), aux[0]]
    rows = 8
    heads = half // rows
    rows_wide = jnp.concatenate(
        [
            jnp.concatenate([part[h * rows : (h + 1) * rows] for part in attended], axis=0)
            for h in range(heads)
        ],
        axis=1,
    )
    projected = jnp.dot(rows_wide.astype(BF16), weight[...], preferred_element_type=F32)
    for k in range(spread.shape[0]):
        spread[k] = projected


def head_blocks(other, share, left, fill, weight, blocks):
    vocab, padded = weight.shape[0], blocks.shape[2]
    reach = -(-(share + 15) // 128) * 128
    core = lax.rem(lax.axis_index("ctx"), 2)
    which = 1 - core if other else core
    lane = iota((blocks.shape[1], padded), 1)
    for k in range(blocks.shape[0]):
        offset = (2 * k + which) * share
        base = pl.multiple_of(jnp.minimum(offset // 16 * 16, vocab - reach), 16)
        product = dot_rows(left, weight[pl.ds(base, reach), :])
        moved = pltpu.roll(product, lax.rem(reach - (offset - base), reach), 1)[:, :padded]
        blocks[k] = jnp.where(lane < share, moved, fill)


def other_kernel(share, parts, residual, gain, weight, blocks, scaled, squares):
    projected = sum(parts[k] for k in range(parts.shape[0]))
    stream = residual[...].astype(F32) + projected
    fill = jnp.sum(stream * stream, axis=1, keepdims=True)
    squares[...] = jnp.broadcast_to(fill, squares.shape)
    left = (stream * gain[...]).astype(BF16)
    scaled[...] = left
    head_blocks(True, share, left, fill, weight, blocks)


def same_kernel(share, scaled, squares, weight, blocks):
    head_blocks(False, share, scaled[...], squares[:, 0:1], weight, blocks)


def add_kernel(one, two, out):
    out[...] = one[...] + two[...]


def column_of(values, rows):
    shape = (rows, values.shape[1])
    return jnp.sum(jnp.where(iota(shape, 0) == iota(shape, 1), values, 0.0), axis=1, keepdims=True)


def stats_kernel(share, vocab, wanted, parts, logits, spread):
    rows, padded = logits.shape
    summed = sum(parts[k] for k in range(parts.shape[0]))
    inverse = lax.rsqrt(summed[:, share : share + 1] * (1.0 / D) + NORM_EPS)
    lane = iota((rows, padded), 1)
    valid = lane < share
    local = summed * inverse
    logits[...] = local
    peak = jnp.max(jnp.where(valid, local, -jnp.inf), axis=1, keepdims=True)
    total = jnp.sum(jnp.where(valid, jnp.exp(local - peak), 0.0), axis=1, keepdims=True)
    start = lax.axis_index("tp") * vocab + lax.axis_index("ctx") * share
    hit = jnp.logical_and(valid, lane + start == wanted[:, 0:1])
    picks = jnp.sum(jnp.where(hit, local, 0.0), axis=1, keepdims=True)
    place = iota((rows, 128), 1)
    mixed = jnp.where(place < rows, peak, jnp.where(place < 2 * rows, total, picks))
    keep = jnp.logical_and(lax.rem(place, rows) == iota((rows, 128), 0), place < 3 * rows)
    line = jnp.sum(jnp.where(keep, mixed, 0.0), axis=0, keepdims=True)
    spread[...] = jnp.broadcast_to(line, spread.shape)


def scores_kernel(share, everyone, logits, scores, chosen):
    rows = logits.shape[0]
    half = rows // 2
    data = everyone[...]
    peak = jnp.max(data, axis=0, keepdims=True)
    scale = jnp.exp(data - peak)
    lane = iota(peak.shape, 1)
    total = jnp.sum(pltpu.roll(scale, rows, 1) * data, axis=0, keepdims=True)
    total = jnp.where(lane < rows, pltpu.roll(total, 128 - rows, 1), 1.0)
    picks = pltpu.roll(jnp.sum(data, axis=0, keepdims=True), 128 - 2 * rows, 1)
    lse = peak + jnp.log(total)
    picked = picks - lse
    line = (
        (1.0 + CONTRAST_WEIGHT) * picked
        - CONTRAST_WEIGHT * pltpu.roll(picked, 128 - half, 1)
        + jnp.minimum(0.0, picks - peak - LOG_FLOOR)
    )
    chosen[...] = line[:, :half]
    logp = logits[...] - column_of(lse, rows)
    top = column_of(peak, rows)
    result = (
        (1.0 + CONTRAST_WEIGHT) * logp[:half]
        - CONTRAST_WEIGHT * logp[half:]
        + jnp.minimum(0.0, logits[:half] - top[:half] - LOG_FLOOR)
    )
    scores[...] = result[:, :share]


def call(kernel, out, in_specs, name, scratch=(), flops=0, moved=0, near=pltpu.VMEM):
    outs = [near(shape, kind) for shape, kind in out]
    specs = [VMEM] * len(outs)
    run = pl.pallas_call(
        kernel,
        out_shape=outs if len(outs) > 1 else outs[0],
        in_specs=in_specs,
        out_specs=specs if len(outs) > 1 else specs[0],
        scratch_shapes=list(scratch),
        name=name,
        cost_estimate=pl.CostEstimate(flops=flops, bytes_accessed=moved, transcendentals=0),
        compiler_params=pltpu.CompilerParams(vmem_limit_bytes=16 * 1024 * 1024),
    )

    def pinned(*operands):
        return run(
            *(
                pltpu.with_memory_space_constraint(operand, pltpu.HBM) if spec is ANY else operand
                for operand, spec in zip(operands, in_specs)
            )
        )

    return pinned


def per_device(
    queries,
    new_kv,
    long_cache,
    short_cache,
    lengths,
    residual,
    out_weight,
    final_gain,
    head_weight,
    targets,
):
    row_count, heads = queries.shape[1], queries.shape[2]
    block_len, short_len = long_cache.shape[2], short_cache.shape[2]
    width, vocab = residual.shape[2], head_weight.shape[1]
    ctx_size, tp_size = lax.axis_size("ctx"), lax.axis_size("tp")
    chips = ctx_size // 2
    rows = 2 * row_count
    share = vocab // ctx_size
    padded = -(-(share + 1) // 128) * 128
    pairs = row_count * heads
    packed = HEAD_DIM // 2 + 8
    cores = [(i, i ^ 1) for i in range(ctx_size)]
    same_core = [list(range(which, ctx_size, 2)) for which in range(2)]

    flat_queries = queries.reshape(2, pairs, HEAD_DIM)
    long_rows = long_cache.reshape(2, row_count, block_len, HEAD_DIM)
    short_rows = short_cache.reshape(2, row_count, short_len, HEAD_DIM)
    fresh = new_kv.reshape(2, 2, row_count, HEAD_DIM)

    weight_rows = head_weight.T
    pieces = 4
    state, aux, wanted, residual_near, gain_near, out_near, head_near = call(
        functools.partial(attention_kernel, pieces),
        [
            ((packed, 128), F32),
            ((3, pairs, HEAD_DIM), F32),
            ((rows, 128), jnp.int32),
            ((rows, width), BF16),
            ((1, width), F32),
            (out_weight.shape, BF16),
            (weight_rows.shape, BF16),
        ],
        [ANY] * 10,
        "attention",
        [
            pltpu.SMEM((row_count,), jnp.int32),
            pltpu.SMEM((row_count,), jnp.int32),
            pltpu.VMEM(flat_queries.shape, BF16),
            pltpu.VMEM(fresh.shape, BF16),
            pltpu.VMEM(long_rows.shape, BF16),
            pltpu.VMEM(short_rows.shape, BF16),
            pltpu.VMEM((pairs, HEAD_DIM), F32),
            pltpu.VMEM((pairs, HEAD_DIM), F32),
            pltpu.SemaphoreType.DMA((11 + pieces,)),
        ],
        moved=12 * 1024 * 1024,
    )(
        lengths,
        flat_queries,
        long_rows,
        short_rows,
        fresh,
        targets,
        residual.reshape(rows, width),
        final_gain.reshape(1, width),
        out_weight,
        weight_rows,
    )
    other = lax.ppermute(state, "ctx", cores)
    spread = call(pair_kernel, [((chips, packed, 128), F32)], [VMEM] * 2, "merge_cores")(
        state, other
    )
    states = lax.all_to_all(spread, "ctx", 0, 0, tiled=True, axis_index_groups=same_core)
    spread = call(project_kernel, [((tp_size, rows, width), F32)], [VMEM] * 3, "project")(
        states, aux, out_near
    )
    parts = lax.all_to_all(spread, "tp", 0, 0, tiled=True)

    theirs, scaled, squares = call(
        functools.partial(other_kernel, share),
        [((chips, rows, padded), F32), ((rows, width), BF16), ((rows, 128), F32)],
        [VMEM] * 4,
        "head_other",
        moved=4 * 1024 * 1024,
    )(parts, residual_near, gain_near, head_near)
    arrived = lax.ppermute(theirs, "ctx", cores)
    mine = call(
        functools.partial(same_kernel, share),
        [((chips, rows, padded), F32)],
        [VMEM] * 3,
        "head_same",
        moved=4 * 1024 * 1024,
    )(scaled, squares, head_near)
    blocks = call(add_kernel, [((chips, rows, padded), F32)], [VMEM] * 2, "add_cores")(
        mine, arrived
    )
    parts = lax.all_to_all(blocks, "ctx", 0, 0, tiled=True, axis_index_groups=same_core)

    devices = ctx_size * tp_size
    logits, spread = call(
        functools.partial(stats_kernel, share, vocab),
        [((rows, padded), F32), ((devices, 128), F32)],
        [VMEM, VMEM],
        "vocab_stats",
    )(wanted, parts)
    everyone = lax.all_to_all(
        spread.reshape(devices, 1, 128), ("ctx", "tp"), 0, 0, tiled=True
    ).reshape(devices, 128)
    scores, chosen = call(
        functools.partial(scores_kernel, share),
        [((row_count, share), F32), ((1, row_count), F32)],
        [VMEM, VMEM],
        "scores",
        near=jax.ShapeDtypeStruct,
    )(everyone, logits)
    return (scores, chosen.reshape(row_count))


def solution(mesh):
    placed = (
        P(None, None, "tp", None),
        P(None, None, None, "tp", None),
        P(None, None, "ctx", "tp", None),
        P(None, None, None, "tp", None),
        P(),
        P(None, None, "ctx"),
        P("tp", "ctx"),
        P("ctx"),
        P("ctx", "tp"),
        P(),
    )
    return jax.shard_map(
        per_device,
        mesh=mesh,
        in_specs=placed,
        out_specs=(P(None, ("tp", "ctx")), P()),
        check_vma=False,
    )
```

time: 100 us -> 83.4 us (0.83)
  blocking collectives: 49.3 us -> 65.6 us
  local copies, waits for them, and re-layouts: 11.4 us -> 0 us
  Pallas kernels: 18.8 us -> 9.59 us
  waiting for transfers between devices: 7.07 us -> 0.87 us
  starting transfers between devices: 12 us -> 6.43 us
    all_to_all x0 -> x1, blocking collectives: none -> 16.3 us  [per_device(): lax.all_to_all(spread, 'ctx', 0, 0, tiled=True, axis_index_groups=same_core)]
    unnamed x24 -> x0, local copies, waits for them, and re-layouts: 11.4 us -> none
    pallas_call x9 -> x8, Pallas kernels: 18.8 us -> 9.59 us  [pinned(): run(*(pltpu.with_memory_space_constraint(operand, pltpu.HBM) if spec is A...]
    all_to_all x1 -> x0, waiting for transfers between devices: 6.2 us -> none  [per_device(): lax.all_to_all(spread, 'ctx', 0, 0, tiled=True, axis_index_groups=same_core)]
    all_to_all x1 -> x0, starting transfers between devices: 5.02 us -> none  [per_device(): lax.all_to_all(spread, 'ctx', 0, 0, tiled=True, axis_index_groups=same_core)]
  transfers between devices with their start and end apart: 3 -> 2, of which waited for: 2 -> 1; matrix products, arithmetic and copies ran while one was open for 0% -> 0% of each run, Pallas kernels for 7% -> 2%
where the time goes in v5:
time: 83.4 us; the launch traced here: 83.2 us
  blocking collectives  65.6 us (79%)
  Pallas kernels  9.59 us (11%)
  starting transfers between devices  6.43 us (8%)
  waiting for transfers between devices  0.87 us (1%)
    all_to_all x1, blocking collectives, per_device(): lax.all_to_all(spread.reshape(devices, 1, 128), ('ctx', 'tp'), 0, 0, tile...  20 us
    all_to_all x1, blocking collectives, per_device(): lax.all_to_all(spread, 'ctx', 0, 0, tiled=True, axis_index_groups=same_core)  16.3 us
    all_to_all x1, blocking collectives, per_device(): parts = lax.all_to_all(spread, 'tp', 0, 0, tiled=True)  16 us
    all_to_all x1, blocking collectives, per_device(): lax.all_to_all(blocks, 'ctx', 0, 0, tiled=True, axis_index_groups=same_core)  13.3 us
    pallas_call x8, Pallas kernels, pinned(): run(*(pltpu.with_memory_space_constraint(operand, pltpu.HBM) if spec is A...  9.59 us
    ppermute x1, starting transfers between devices, per_device(): other = lax.ppermute(state, 'ctx', cores)  3.33 us
    ppermute x1, starting transfers between devices, per_device(): arrived = lax.ppermute(theirs, 'ctx', cores)  3.1 us
  transfers between devices with their start and end apart: 2, of which 1 were waited for; matrix products, arithmetic and copies ran while one was open for 0% of the time, Pallas kernels for 2%

profile of v5, /device:TPU:1, one launch (start us, length us, event | category | flops | bytes accessed | tf_op | source)
XLA Modules:
  0.0 83.2 jit_solution(2279305829362738822)
XLA Ops:
  0.6 4.7 %attention.1 = (f32[72,128]{1,0:T(8,128)S(1)}, f32[3,64,128]{2,1,0:T(8,128)S(1)}, s32[16,128]{1,0:T(8,128)S(1)}, bf16[16,256]{1,0:T(8,128)(2,1)S(1)}, f32[1,256]...) custom-call(s32[8]{0:T(128)} %lengths_far.1, bf16[2,64,128]{2,1,0:T(8,128)(2,1)} %bitcast.17, ...), custom_call_target="tpu_custom_call" | custom-call | bytes 12582912 | tf_op jit(solution)/shard_map/attention/pallas_call | solution.py:295
  5.3 3.3 %collective-permute-start = (f32[72,128]{1,0:T(8,128)S(1)}, f32[72,128]{1,0:T(8,128)S(1)}, u32[]{:S(2)}, u32[]{:S(2)}) collective-permute-start(f32[72,128]{1,0:T(8,128)S(1)} %get-tuple-element.17.one), channel_id=1, source_target_pairs={{0,8},{8,0},{16,24},{24,16},{32,40},{40,32},{48,56},{56,48},{64,72... | collective-permute-start | bytes 110600 | tf_op jit(solution)/shard_map/ppermute | solution.py:374
  8.6 0.9 %collective-permute-done.two = f32[72,128]{1,0:T(8,128)S(1)} collective-permute-done((f32[72,128]{1,0:T(8,128)S(1)}, f32[72,128]{1,0:T(8,128)S(1)}, u32[]{:S(2)}, u32[]{:S(2)}) %collective-permute-start) | collective-permute-done | bytes 36896 | tf_op jit(solution)/shard_map/ppermute | solution.py:374
  9.6 16.3 %all_to_all.20.states = f32[16,72,128]{2,1,0:T(8,128)S(1)} all-to-all(f32[16,72,128]{2,1,0:T(8,128)S(1)} %merge_cores.1), channel_id=1, replica_groups={{0,16,32,48,64,80,96,112,128,144,160,176,192,208,224,240},{8,24,40,56,7..., dimensions={0} | all-to-all | bytes 1179648 | tf_op jit(solution)/shard_map/all_to_all | solution.py:378
  25.9 0.5 project.1
  26.4 16.0 %all_to_all.21.parts = f32[8,16,256]{2,1,0:T(8,128)S(1)} all-to-all(f32[8,16,256]{2,1,0:T(8,128)S(1)} %project.1), channel_id=1, replica_groups=mesh['ctx'=32,'tp'=8] {'tp'}, dimensions={0} | all-to-all | bytes 262144 | tf_op jit(solution)/shard_map/all_to_all | solution.py:382
  42.4 1.6 %head_other.1 = (f32[16,16,512]{2,1,0:T(8,128)S(1)}, bf16[16,256]{1,0:T(8,128)(2,1)S(1)}, f32[16,128]{1,0:T(8,128)S(1)}) custom-call(f32[8,16,256]{2,1,0:T(8,128)S(1)} %all_to_all.21.parts, bf16[16,256]{1,0:T(8,128)(2,1)S(1)} %get-tuple-element.20.residual, f32[1,256]{1,0:T(1,128)S(1)} %get-tuple-element.21.gain, bf16[16032,256]{1,0:T(8,128)(2,1)S(1)} %get-tuple-element.22.weight), custom_call_target="tpu_custom_call" | custom-call | bytes 4194304 | tf_op jit(solution)/shard_map/head_other/pallas_call | solution.py:295
  44.0 3.1 %collective-permute-start.1 = (f32[16,16,512]{2,1,0:T(8,128)S(1)}, f32[16,16,512]{2,1,0:T(8,128)S(1)}, u32[]{:S(2)}, u32[]{:S(2)}) collective-permute-start(f32[16,16,512]{2,1,0:T(8,128)S(1)} %get-tuple-element.25), channel_id=1, source_target_pairs={{0,8},{8,0},{16,24},{24,16},{32,40},{40,32},{48,56},{56,48},{64,72... | collective-permute-start | bytes 1572872 | tf_op jit(solution)/shard_map/ppermute | solution.py:391
  47.1 1.6 %head_same.1.one = f32[16,16,512]{2,1,0:T(8,128)S(1)} custom-call(bf16[16,256]{1,0:T(8,128)(2,1)S(1)} %get-tuple-element.23.scaled, f32[16,128]{1,0:T(8,128)S(1)} %get-tuple-element.24.squares, bf16[16032,256]{1,0:T(8,128)(2,1)S(1)} %get-tuple-element.22.weight), custom_call_target="tpu_custom_call" | custom-call | bytes 4194304 | tf_op jit(solution)/shard_map/head_same/pallas_call | solution.py:295
  48.7 0.0 collective-permute-done.1.two
  48.7 0.1 add_cores.1
  48.7 13.3 %all_to_all.22.parts = f32[16,16,512]{2,1,0:T(8,128)S(1)} all-to-all(f32[16,16,512]{2,1,0:T(8,128)S(1)} %add_cores.1), channel_id=1, replica_groups={{0,16,32,48,64,80,96,112,128,144,160,176,192,208,224,240},{8,24,40,56,7..., dimensions={0} | all-to-all | bytes 1048576 | tf_op jit(solution)/shard_map/all_to_all | solution.py:402
  62.0 0.3 vocab_stats.1
  62.3 20.0 %all_to_all.23 = f32[256,1,128]{2,1,0:T(1,128)S(1)} all-to-all(f32[256,1,128]{2,1,0:T(1,128)S(1)} %bitcast.13), channel_id=1, replica_groups=mesh['ctx'=32,'tp'=8] {'ctx','tp'}, dimensions={0} | all-to-all | bytes 262144 | tf_op jit(solution)/shard_map/all_to_all | solution.py:411
  82.3 0.9 %scores.1 = (f32[8,501]{1,0:T(8,128)}, f32[1,8]{1,0:T(1,128)}) custom-call(f32[256,128]{1,0:T(8,128)S(1)} %bitcast.12, f32[16,512]{1,0:T(8,128)S(1)} %get-tuple-element.27.logits), custom_call_target="tpu_custom_call" | custom-call | tf_op jit(solution)/shard_map/scores/pallas_call | solution.py:295
  (1 shorter events, 0.0 us)
Async XLA Ops:
  5.3 4.2 %collective-permute-start = (f32[72,128]{1,0:T(8,128)S(1)}, f32[72,128]{1,0:T(8,128)S(1)}, u32[]{:S(2)}, u32[]{:S(2)}) collective-permute-start(f32[72,128]{1,0:T(8,128)S(1)} %get-tuple-element.17.one), channel_id=1, source_target_pairs={{0,8},{8,0},{16,24},{24,16},{32,40},{40,32},{48,56},{56,48},{64,72... | collective-permute-start | bytes 110600 | tf_op jit(solution)/shard_map/ppermute | solution.py:374
  44.0 4.7 %collective-permute-start.1 = (f32[16,16,512]{2,1,0:T(8,128)S(1)}, f32[16,16,512]{2,1,0:T(8,128)S(1)}, u32[]{:S(2)}, u32[]{:S(2)}) collective-permute-start(f32[16,16,512]{2,1,0:T(8,128)S(1)} %get-tuple-element.25), channel_id=1, source_target_pairs={{0,8},{8,0},{16,24},{24,16},{32,40},{40,32},{48,56},{56,48},{64,72... | collective-permute-start | bytes 1572872 | tf_op jit(solution)/shard_map/ppermute | solution.py:391

commit v6 on v5

--- a/solution.py
+++ b/solution.py
@@ -17,6 +17,7 @@
 LOG_FLOOR = -2.302585092994046
 
 F32 = jnp.float32
+BESIDE = 30 * 10**9
 BF16 = jnp.bfloat16
 VMEM = pl.BlockSpec(memory_space=pltpu.VMEM)
 ANY = pl.BlockSpec(memory_space=pl.ANY)
@@ -38,7 +39,6 @@
 
 
 def attention_kernel(
-    pieces,
     lengths_far,
     queries_far,
     long_far,
@@ -47,15 +47,11 @@
     targets_far,
     residual_far,
     gain_far,
-    out_far,
-    head_far,
     state,
     aux,
     wanted,
     residual,
     gain,
-    out_near,
-    head_near,
     lengths,
     targets,
     queries,
@@ -66,8 +62,6 @@
     stat,
     sems,
 ):
-    step = head_far.shape[0] // pieces // 16 * 16
-    cuts = [step * n for n in range(pieces)] + [head_far.shape[0]]
     moves = [
         (lengths_far, lengths),
         (queries_far, queries),
@@ -79,10 +73,6 @@
         (targets_far, targets),
         (residual_far, residual),
         (gain_far, gain),
-        (out_far, out_near),
-    ] + [
-        (head_far.at[pl.ds(low, high - low)], head_near.at[pl.ds(low, high - low)])
-        for low, high in zip(cuts, cuts[1:])
     ]
     copies = [pltpu.make_async_copy(*move, sems.at[n]) for n, move in enumerate(moves)]
     for copy in copies:
@@ -333,19 +323,16 @@
     fresh = new_kv.reshape(2, 2, row_count, HEAD_DIM)
 
     weight_rows = head_weight.T
-    pieces = 4
-    state, aux, wanted, residual_near, gain_near, out_near, head_near = call(
-        functools.partial(attention_kernel, pieces),
+    state, aux, wanted, residual_near, gain_near = call(
+        attention_kernel,
         [
             ((packed, 128), F32),
             ((3, pairs, HEAD_DIM), F32),
             ((rows, 128), jnp.int32),
             ((rows, width), BF16),
             ((1, width), F32),
-            (out_weight.shape, BF16),
-            (weight_rows.shape, BF16),
         ],
-        [ANY] * 10,
+        [ANY] * 8,
         "attention",
         [
             pltpu.SMEM((row_count,), jnp.int32),
@@ -356,9 +343,9 @@
             pltpu.VMEM(short_rows.shape, BF16),
             pltpu.VMEM((pairs, HEAD_DIM), F32),
             pltpu.VMEM((pairs, HEAD_DIM), F32),
-            pltpu.SemaphoreType.DMA((11 + pieces,)),
+            pltpu.SemaphoreType.DMA((10,)),
         ],
-        moved=12 * 1024 * 1024,
+        moved=3 * 1024 * 1024,
     )(
         lengths,
         flat_queries,
@@ -368,16 +355,14 @@
         targets,
         residual.reshape(rows, width),
         final_gain.reshape(1, width),
-        out_weight,
-        weight_rows,
     )
     other = lax.ppermute(state, "ctx", cores)
-    spread = call(pair_kernel, [((chips, packed, 128), F32)], [VMEM] * 2, "merge_cores")(
+    spread = call(pair_kernel, [((chips, packed, 128), F32)], [VMEM] * 2, "merge_cores", flops=BESIDE)(
         state, other
     )
     states = lax.all_to_all(spread, "ctx", 0, 0, tiled=True, axis_index_groups=same_core)
-    spread = call(project_kernel, [((tp_size, rows, width), F32)], [VMEM] * 3, "project")(
-        states, aux, out_near
+    spread = call(project_kernel, [((tp_size, rows, width), F32)], [VMEM] * 3, "project", flops=BESIDE)(
+        states, aux, out_weight
     )
     parts = lax.all_to_all(spread, "tp", 0, 0, tiled=True)
 
@@ -387,7 +372,7 @@
         [VMEM] * 4,
         "head_other",
         moved=4 * 1024 * 1024,
-    )(parts, residual_near, gain_near, head_near)
+    )(parts, residual_near, gain_near, weight_rows)
     arrived = lax.ppermute(theirs, "ctx", cores)
     mine = call(
         functools.partial(same_kernel, share),
@@ -395,7 +380,7 @@
         [VMEM] * 3,
         "head_same",
         moved=4 * 1024 * 1024,
-    )(scaled, squares, head_near)
+    )(scaled, squares, weight_rows)
     blocks = call(add_kernel, [((chips, rows, padded), F32)], [VMEM] * 2, "add_cores")(
         mine, arrived
     )

time: 83.4 us -> 81.7 us (0.980)
  Pallas kernels: 9.59 us -> 7.62 us
    pallas_call x8, Pallas kernels: 9.59 us -> 7.62 us  [pinned(): run(*(pltpu.with_memory_space_constraint(operand, pltpu.HBM) if spec is A...]
where the time goes in v6:
time: 81.7 us; the launch traced here: 81.5 us
  blocking collectives  65.9 us (81%)
  Pallas kernels  7.62 us (9%)
  starting transfers between devices  6.43 us (8%)
  waiting for transfers between devices  0.87 us (1%)
    all_to_all x1, blocking collectives, per_device(): lax.all_to_all(spread.reshape(devices, 1, 128), ('ctx', 'tp'), 0, 0, tile...  20 us
    all_to_all x1, blocking collectives, per_device(): lax.all_to_all(spread, 'ctx', 0, 0, tiled=True, axis_index_groups=same_core)  16.6 us
    all_to_all x1, blocking collectives, per_device(): parts = lax.all_to_all(spread, 'tp', 0, 0, tiled=True)  16 us
    all_to_all x1, blocking collectives, per_device(): lax.all_to_all(blocks, 'ctx', 0, 0, tiled=True, axis_index_groups=same_core)  13.3 us
    pallas_call x8, Pallas kernels, pinned(): run(*(pltpu.with_memory_space_constraint(operand, pltpu.HBM) if spec is A...  7.62 us
    ppermute x1, starting transfers between devices, per_device(): other = lax.ppermute(state, 'ctx', cores)  3.33 us
    ppermute x1, starting transfers between devices, per_device(): arrived = lax.ppermute(theirs, 'ctx', cores)  3.1 us
  transfers between devices with their start and end apart: 2, of which 1 were waited for; matrix products, arithmetic and copies ran while one was open for 0% of the time, Pallas kernels for 2%

profile of v6, /device:TPU:1, one launch (start us, length us, event | category | flops | bytes accessed | tf_op | source)
XLA Modules:
  0.0 81.5 jit_solution(2937762333525113522)
XLA Ops:
  0.6 2.7 %attention.1 = (f32[72,128]{1,0:T(8,128)S(1)}, f32[3,64,128]{2,1,0:T(8,128)S(1)}, s32[16,128]{1,0:T(8,128)S(1)}, bf16[16,256]{1,0:T(8,128)(2,1)S(1)}, f32[1,256]{1,0:T(1,128)S(1)}) custom-call(s32[8]{0:T(128)} %lengths_far.1, bf16[2,64,128]{2,1,0:T(8,128)(2,1)} %bitcast.20, bf16[2,8,512,128]{3,2,1,0:T(8,128)(2,1)} %bitcast.18, ...), custom_call_target="tpu_custom_call" | custom-call | bytes 3145728 | tf_op jit(solution)/shard_map/attention/pallas_call | solution.py:285
  3.3 0.0 copy-start
  3.3 3.3 %collective-permute-start = (f32[72,128]{1,0:T(8,128)S(1)}, f32[72,128]{1,0:T(8,128)S(1)}, u32[]{:S(2)}, u32[]{:S(2)}) collective-permute-start(f32[72,128]{1,0:T(8,128)S(1)} %get-tuple-element.15.one), channel_id=1, source_target_pairs={{0,8},{8,0},{16,24},{24,16},{32,40},{40,32},{48,56},{56,48},{64,72... | collective-permute-start | bytes 110600 | tf_op jit(solution)/shard_map/ppermute | solution.py:359
  6.7 0.9 %collective-permute-done.two = f32[72,128]{1,0:T(8,128)S(1)} collective-permute-done((f32[72,128]{1,0:T(8,128)S(1)}, f32[72,128]{1,0:T(8,128)S(1)}, u32[]{:S(2)}, u32[]{:S(2)}) %collective-permute-start) | collective-permute-done | bytes 36896 | tf_op jit(solution)/shard_map/ppermute | solution.py:359
  7.5 0.0 slice-start
  7.6 0.0 slice-start.1
  7.6 16.6 %all_to_all.20.states = f32[16,72,128]{2,1,0:T(8,128)S(1)} all-to-all(f32[16,72,128]{2,1,0:T(8,128)S(1)} %merge_cores.1), channel_id=1, replica_groups={{0,16,32,48,64,80,96,112,128,144,160,176,192,208,224,240},{8,24,40,56,7..., dimensions={0} | all-to-all | bytes 1179648 | tf_op jit(solution)/shard_map/all_to_all | solution.py:363
  24.2 0.0 copy-done
  24.2 0.5 project.1
  24.7 16.0 %all_to_all.21.parts = f32[8,16,256]{2,1,0:T(8,128)S(1)} all-to-all(f32[8,16,256]{2,1,0:T(8,128)S(1)} %project.1), channel_id=1, replica_groups=mesh['ctx'=32,'tp'=8] {'tp'}, dimensions={0} | all-to-all | bytes 262144 | tf_op jit(solution)/shard_map/all_to_all | solution.py:367
  40.7 0.0 slice-done
  40.7 0.0 slice-done.1
  40.7 1.6 %head_other.1 = (f32[16,16,512]{2,1,0:T(8,128)S(1)}, bf16[16,256]{1,0:T(8,128)(2,1)S(1)}, f32[16,128]{1,0:T(8,128)S(1)}) custom-call(f32[8,16,256]{2,1,0:T(8,128)S(1)} %all_to_all.21.parts, bf16[16,256]{1,0:T(8,128)(2,1)S(1)} %get-tuple-element.17.residual, f32[1,256]{1,0:T(1,128)S(1)} %get-tuple-element.18.gain, bf16[16032,256]{1,0:T(8,128)(2,1)S(1)} %bitcast.14), custom_call_target="tpu_custom_call" | custom-call | bytes 4194304 | tf_op jit(solution)/shard_map/head_other/pallas_call | solution.py:285
  42.3 3.1 %collective-permute-start.1 = (f32[16,16,512]{2,1,0:T(8,128)S(1)}, f32[16,16,512]{2,1,0:T(8,128)S(1)}, u32[]{:S(2)}, u32[]{:S(2)}) collective-permute-start(f32[16,16,512]{2,1,0:T(8,128)S(1)} %get-tuple-element.21), channel_id=1, source_target_pairs={{0,8},{8,0},{16,24},{24,16},{32,40},{40,32},{48,56},{56,48},{64,72... | collective-permute-start | bytes 1572872 | tf_op jit(solution)/shard_map/ppermute | solution.py:376
  45.4 1.6 %head_same.1.one = f32[16,16,512]{2,1,0:T(8,128)S(1)} custom-call(bf16[16,256]{1,0:T(8,128)(2,1)S(1)} %get-tuple-element.19.scaled, f32[16,128]{1,0:T(8,128)S(1)} %get-tuple-element.20.squares, bf16[16032,256]{1,0:T(8,128)(2,1)S(1)} %bitcast.15), custom_call_target="tpu_custom_call" | custom-call | bytes 4194304 | tf_op jit(solution)/shard_map/head_same/pallas_call | solution.py:285
  47.0 0.0 collective-permute-done.1.two
  47.0 0.1 add_cores.1
  47.0 13.3 %all_to_all.22.parts = f32[16,16,512]{2,1,0:T(8,128)S(1)} all-to-all(f32[16,16,512]{2,1,0:T(8,128)S(1)} %add_cores.1), channel_id=1, replica_groups={{0,16,32,48,64,80,96,112,128,144,160,176,192,208,224,240},{8,24,40,56,7..., dimensions={0} | all-to-all | bytes 1048576 | tf_op jit(solution)/shard_map/all_to_all | solution.py:387
  60.4 0.3 vocab_stats.1
  60.6 20.0 %all_to_all.23 = f32[256,1,128]{2,1,0:T(1,128)S(1)} all-to-all(f32[256,1,128]{2,1,0:T(1,128)S(1)} %bitcast.17), channel_id=1, replica_groups=mesh['ctx'=32,'tp'=8] {'ctx','tp'}, dimensions={0} | all-to-all | bytes 262144 | tf_op jit(solution)/shard_map/all_to_all | solution.py:396
  80.6 0.9 %scores.1 = (f32[8,501]{1,0:T(8,128)}, f32[1,8]{1,0:T(1,128)}) custom-call(f32[256,128]{1,0:T(8,128)S(1)} %bitcast.16, f32[16,512]{1,0:T(8,128)S(1)} %get-tuple-element.23.logits), custom_call_target="tpu_custom_call" | custom-call | tf_op jit(solution)/shard_map/scores/pallas_call | solution.py:285
  (2 shorter events, 0.0 us)
Async XLA Ops:
  3.3 20.9 %copy-start = (bf16[1024,256]{1,0:T(8,128)(2,1)S(1)}, bf16[1024,256]{1,0:T(8,128)(2,1)}, u32[]{:S(2)}) copy-start(bf16[1024,256]{1,0:T(8,128)(2,1)} %weight.1) | copy-start | bytes 1572868
  3.3 4.2 %collective-permute-start = (f32[72,128]{1,0:T(8,128)S(1)}, f32[72,128]{1,0:T(8,128)S(1)}, u32[]{:S(2)}, u32[]{:S(2)}) collective-permute-start(f32[72,128]{1,0:T(8,128)S(1)} %get-tuple-element.15.one), channel_id=1, source_target_pairs={{0,8},{8,0},{16,24},{24,16},{32,40},{40,32},{48,56},{56,48},{64,72... | collective-permute-start | bytes 110600 | tf_op jit(solution)/shard_map/ppermute | solution.py:359
  7.5 33.2 %slice-start = ((s8[8208384]{0:T(1024)(128)(4,1)}), s8[4194304]{0:T(1024)(128)(4,1)S(1)}, s32[]{:S(2)}) async-start(s8[8208384]{0:T(1024)(128)(4,1)} %bitcast.12), calls=%async_computation.4 | async-start | bytes 8388608
  7.6 33.1 %slice-start.1 = ((s8[8208384]{0:T(1024)(128)(4,1)}), s8[4014080]{0:T(1024)(128)(4,1)S(1)}, s32[]{:S(2)}) async-start(s8[8208384]{0:T(1024)(128)(4,1)} %bitcast.12), calls=%async_computation.5 | async-start | bytes 8028160
  42.3 4.7 %collective-permute-start.1 = (f32[16,16,512]{2,1,0:T(8,128)S(1)}, f32[16,16,512]{2,1,0:T(8,128)S(1)}, u32[]{:S(2)}, u32[]{:S(2)}) collective-permute-start(f32[16,16,512]{2,1,0:T(8,128)S(1)} %get-tuple-element.21), channel_id=1, source_target_pairs={{0,8},{8,0},{16,24},{24,16},{32,40},{40,32},{48,56},{56,48},{64,72... | collective-permute-start | bytes 1572872 | tf_op jit(solution)/shard_map/ppermute | solution.py:376

commit v7 on v6

--- a/solution.py
+++ b/solution.py
@@ -145,18 +145,16 @@
     return jnp.where(iota((8, HEAD_DIM), 0) == 0, peak, total)
 
 
-def pair_kernel(one, two, spread):
+def join_kernel(*refs):
     half = HEAD_DIM // 2
-    values, peak, total = merge_states([one, two])
-    stats = packed_stats(peak, total)
-    for k in range(spread.shape[0]):
-        spread[k, 0:half, :] = values
-        spread[k, half : half + 8, :] = stats
-
-
-def project_kernel(states, aux, weight, spread):
+    values, peak, total = merge_states(refs[:-1])
+    refs[-1][0:half, :] = values
+    refs[-1][half : half + 8, :] = packed_stats(peak, total)
+
+
+def project_kernel(s0, s1, s2, s3, aux, weight, spread):
     half = HEAD_DIM // 2
-    values, peak, total = merge_states([states.at[k] for k in range(states.shape[0])])
+    values, peak, total = merge_states([s0, s1, s2, s3])
     blank = jnp.zeros((half - 8, HEAD_DIM), F32)
     turned = jnp.concatenate([values, packed_stats(peak, total), blank], axis=0).T
     left, right = turned[:half], turned[half:]
@@ -236,6 +234,16 @@
     mixed = jnp.where(place < rows, peak, jnp.where(place < 2 * rows, total, picks))
     keep = jnp.logical_and(lax.rem(place, rows) == iota((rows, 128), 0), place < 3 * rows)
     line = jnp.sum(jnp.where(keep, mixed, 0.0), axis=0, keepdims=True)
+    spread[...] = jnp.broadcast_to(line, spread.shape)
+
+
+def join_stats(rows, one, two, spread):
+    a, b = one[0:1, :], two[0:1, :]
+    peak = jnp.maximum(a, b)
+    fa, fb = jnp.exp(a - peak), jnp.exp(b - peak)
+    total = a * pltpu.roll(fa, rows, 1) + b * pltpu.roll(fb, rows, 1)
+    lane = iota(peak.shape, 1)
+    line = jnp.where(lane < rows, peak, jnp.where(lane < 2 * rows, total, a + b))
     spread[...] = jnp.broadcast_to(line, spread.shape)
 
 
@@ -357,13 +365,20 @@
         final_gain.reshape(1, width),
     )
     other = lax.ppermute(state, "ctx", cores)
-    spread = call(pair_kernel, [((chips, packed, 128), F32)], [VMEM] * 2, "merge_cores", flops=BESIDE)(
+    def ring(value, masks):
+        return [
+            lax.ppermute(value, "ctx", [(i, i ^ m) for i in range(ctx_size)]) for m in masks
+        ]
+
+    state = call(join_kernel, [((packed, 128), F32)], [VMEM] * 2, "merge_cores", flops=BESIDE)(
         state, other
     )
-    states = lax.all_to_all(spread, "ctx", 0, 0, tiled=True, axis_index_groups=same_core)
-    spread = call(project_kernel, [((tp_size, rows, width), F32)], [VMEM] * 3, "project", flops=BESIDE)(
-        states, aux, out_weight
-    )
+    state = call(join_kernel, [((packed, 128), F32)], [VMEM] * 4, "merge_y", flops=BESIDE)(
+        state, *ring(state, (2, 6, 4))
+    )
+    spread = call(
+        project_kernel, [((tp_size, rows, width), F32)], [VMEM] * 6, "project", flops=BESIDE
+    )(state, *ring(state, (8, 24, 16)), aux, out_weight)
     parts = lax.all_to_all(spread, "tp", 0, 0, tiled=True)
 
     theirs, scaled, squares = call(
@@ -386,15 +401,23 @@
     )
     parts = lax.all_to_all(blocks, "ctx", 0, 0, tiled=True, axis_index_groups=same_core)
 
-    devices = ctx_size * tp_size
-    logits, spread = call(
+    devices = chips * tp_size
+    logits, line = call(
         functools.partial(stats_kernel, share, vocab),
-        [((rows, padded), F32), ((devices, 128), F32)],
+        [((rows, padded), F32), ((8, 128), F32)],
         [VMEM, VMEM],
         "vocab_stats",
     )(wanted, parts)
+    arrived = lax.ppermute(line, "ctx", cores)
+    spread = call(
+        functools.partial(join_stats, rows), [((devices, 128), F32)], [VMEM] * 2, "join_stats"
+    )(line, arrived)
+    groups = [
+        [c * tp_size + t for c in range(which, ctx_size, 2) for t in range(tp_size)]
+        for which in range(2)
+    ]
     everyone = lax.all_to_all(
-        spread.reshape(devices, 1, 128), ("ctx", "tp"), 0, 0, tiled=True
+        spread.reshape(devices, 1, 128), ("ctx", "tp"), 0, 0, tiled=True, axis_index_groups=groups
     ).reshape(devices, 128)
     scores, chosen = call(
         functools.partial(scores_kernel, share),

time: 81.7 us -> 79.4 us (0.972)
  blocking collectives: 65.9 us -> 45.3 us
  starting transfers between devices: 6.43 us -> 17.5 us
  waiting for transfers between devices: 0.87 us -> 8.09 us
    all_to_all x1 -> x0, blocking collectives: 16.6 us -> none  [per_device(): lax.all_to_all(spread, 'ctx', 0, 0, tiled=True, axis_index_groups=same_core)]
    ppermute x0 -> x7, starting transfers between devices: none -> 9.13 us  [the longest x6 7.08 us: ring(): lax.ppermute(value, 'ctx', [(i, i ^ m) for i in range(ctx_size)])]
    ppermute x0 -> x7, waiting for transfers between devices: none -> 7.23 us  [the longest x6 6.4 us: ring(): lax.ppermute(value, 'ctx', [(i, i ^ m) for i in range(ctx_size)])]
    all_to_all x1, blocking collectives: 20 us -> 16.1 us  [per_device(): lax.all_to_all(spread.reshape(devices, 1, 128), ('ctx', 'tp'), 0, 0, tile...]
    ppermute x1, starting transfers between devices: 3.1 us -> 5.08 us  [per_device(): arrived = lax.ppermute(theirs, 'ctx', cores)]
    pallas_call x8 -> x10, Pallas kernels: 7.62 us -> 7.62 us  [pinned(): run(*(pltpu.with_memory_space_constraint(operand, pltpu.HBM) if spec is A...]
  transfers between devices with their start and end apart: 2 -> 9, of which waited for: 1 -> 6; matrix products, arithmetic and copies ran while one was open for 0% -> 0% of each run, Pallas kernels for 2% -> 2%
where the time goes in v7:
time: 79.4 us; the launch traced here: 79.2 us
  blocking collectives  45.3 us (57%)
  starting transfers between devices  17.5 us (22%)
  waiting for transfers between devices  8.09 us (10%)
  Pallas kernels  7.62 us (10%)
    all_to_all x1, blocking collectives, per_device(): lax.all_to_all(spread.reshape(devices, 1, 128), ('ctx', 'tp'), 0, 0, tile...  16.1 us
    all_to_all x1, blocking collectives, per_device(): parts = lax.all_to_all(spread, 'tp', 0, 0, tiled=True)  16 us
    all_to_all x1, blocking collectives, per_device(): lax.all_to_all(blocks, 'ctx', 0, 0, tiled=True, axis_index_groups=same_core)  13.1 us
    pallas_call x10, Pallas kernels, pinned(): run(*(pltpu.with_memory_space_constraint(operand, pltpu.HBM) if spec is A...  7.62 us
    ppermute x6, starting transfers between devices, ring(): lax.ppermute(value, 'ctx', [(i, i ^ m) for i in range(ctx_size)])  7.08 us
    ppermute x6, waiting for transfers between devices, ring(): lax.ppermute(value, 'ctx', [(i, i ^ m) for i in range(ctx_size)])  6.4 us
    ppermute x1, starting transfers between devices, per_device(): arrived = lax.ppermute(theirs, 'ctx', cores)  5.08 us
    ppermute x1, starting transfers between devices, per_device(): other = lax.ppermute(state, 'ctx', cores)  3.33 us
  transfers between devices with their start and end apart: 9, of which 6 were waited for; matrix products, arithmetic and copies ran while one was open for 0% of the time, Pallas kernels for 2%

profile of v7, /device:TPU:1, one launch (start us, length us, event | category | flops | bytes accessed | tf_op | source)
XLA Modules:
  0.0 79.2 jit_solution(4787821169721219081)
XLA Ops:
  0.6 2.7 %attention.1 = (f32[72,128]{1,0:T(8,128)S(1)}, f32[3,64,128]{2,1,0:T(8,128)S(1)}, s32[16,128]{1,0:T(8,128)S(1)}, bf16[16,256]{1,0:T(8,128)(2,1)S(1)}, f32[1,256]{1,0:T(1,128)S(1)}) custom-call(s32[8]{0:T(128)} %lengths_far.1, bf16[2,64,128]{2,1,0:T(8,128)(2,1)} %bitcast.20, bf16[2,8,512,128]{3,2,1,0:T(8,128)(2,1)} %bitcast.18, ...), custom_call_target="tpu_custom_call" | custom-call | bytes 3145728 | tf_op jit(solution)/shard_map/attention/pallas_call | solution.py:293
  3.3 3.3 %collective-permute-start = (f32[72,128]{1,0:T(8,128)S(1)}, f32[72,128]{1,0:T(8,128)S(1)}, u32[]{:S(2)}, u32[]{:S(2)}) collective-permute-start(f32[72,128]{1,0:T(8,128)S(1)} %get-tuple-element.15.refs_0_), channel_id=1, source_target_pairs={{0,8},{8,0},{16,24},{24,16},{32,40},{40,32},{48,56},{56,48},{64,72... | collective-permute-start | bytes 110600 | tf_op jit(solution)/shard_map/ppermute | solution.py:367
  6.7 0.9 %collective-permute-done.refs_1_ = f32[72,128]{1,0:T(8,128)S(1)} collective-permute-done((f32[72,128]{1,0:T(8,128)S(1)}, f32[72,128]{1,0:T(8,128)S(1)}, u32[]{:S(2)}, u32[]{:S(2)}) %collective-permute-start) | collective-permute-done | bytes 36896 | tf_op jit(solution)/shard_map/ppermute | solution.py:367
  7.5 0.0 copy-start
  7.6 0.1 collective-permute-start.1
  7.7 1.4 %collective-permute-start.2 = (f32[72,128]{1,0:T(8,128)S(1)}, f32[72,128]{1,0:T(8,128)S(1)}, u32[]{:S(2)}, u32[]{:S(2)}) collective-permute-start(f32[72,128]{1,0:T(8,128)S(1)} %merge_cores.1.refs_0_), channel_id=1, source_target_pairs={{0,48},{8,56},{16,32},{24,40},{32,16},{40,24},{48,0},{56,8},{64,11... | collective-permute-start | bytes 110600 | tf_op jit(solution)/shard_map/ppermute | solution.py:370
  9.1 1.8 %collective-permute-start.3 = (f32[72,128]{1,0:T(8,128)S(1)}, f32[72,128]{1,0:T(8,128)S(1)}, u32[]{:S(2)}, u32[]{:S(2)}) collective-permute-start(f32[72,128]{1,0:T(8,128)S(1)} %merge_cores.1.refs_0_), channel_id=1, source_target_pairs={{0,32},{8,40},{16,48},{24,56},{32,0},{40,8},{48,16},{56,24},{64,96... | collective-permute-start | bytes 110600 | tf_op jit(solution)/shard_map/ppermute | solution.py:370
  10.9 0.0 collective-permute-done.1.refs_1_
  10.9 0.9 %collective-permute-done.2.refs_2_ = f32[72,128]{1,0:T(8,128)S(1)} collective-permute-done((f32[72,128]{1,0:T(8,128)S(1)}, f32[72,128]{1,0:T(8,128)S(1)}, u32[]{:S(2)}, u32[]{:S(2)}) %collective-permute-start.2) | collective-permute-done | bytes 36896 | tf_op jit(solution)/shard_map/ppermute | solution.py:370
  11.8 1.7 %collective-permute-done.3.refs_3_ = f32[72,128]{1,0:T(8,128)S(1)} collective-permute-done((f32[72,128]{1,0:T(8,128)S(1)}, f32[72,128]{1,0:T(8,128)S(1)}, u32[]{:S(2)}, u32[]{:S(2)}) %collective-permute-start.3) | collective-permute-done | bytes 36896 | tf_op jit(solution)/shard_map/ppermute | solution.py:370
  13.5 1.3 %collective-permute-start.4 = (f32[72,128]{1,0:T(8,128)S(1)}, f32[72,128]{1,0:T(8,128)S(1)}, u32[]{:S(2)}, u32[]{:S(2)}) collective-permute-start(f32[72,128]{1,0:T(8,128)S(1)} %merge_y.1.s0), channel_id=1, source_target_pairs={{0,64},{8,72},{16,80},{24,88},{32,96},{40,104},{48,112},{56,120},{... | collective-permute-start | bytes 110600 | tf_op jit(solution)/shard_map/ppermute | solution.py:370
  14.8 1.8 %collective-permute-start.5 = (f32[72,128]{1,0:T(8,128)S(1)}, f32[72,128]{1,0:T(8,128)S(1)}, u32[]{:S(2)}, u32[]{:S(2)}) collective-permute-start(f32[72,128]{1,0:T(8,128)S(1)} %merge_y.1.s0), channel_id=1, source_target_pairs={{0,192},{8,200},{16,208},{24,216},{32,224},{40,232},{48,240},{56,2... | collective-permute-start | bytes 110600 | tf_op jit(solution)/shard_map/ppermute | solution.py:370
  16.6 0.6 collective-permute-start.6
  17.2 0.0 collective-permute-done.4.s1
  17.2 1.6 %collective-permute-done.5.s2 = f32[72,128]{1,0:T(8,128)S(1)} collective-permute-done((f32[72,128]{1,0:T(8,128)S(1)}, f32[72,128]{1,0:T(8,128)S(1)}, u32[]{:S(2)}, u32[]{:S(2)}) %collective-permute-start.5) | collective-permute-done | bytes 36896 | tf_op jit(solution)/shard_map/ppermute | solution.py:370
  18.8 2.3 %collective-permute-done.6.s3 = f32[72,128]{1,0:T(8,128)S(1)} collective-permute-done((f32[72,128]{1,0:T(8,128)S(1)}, f32[72,128]{1,0:T(8,128)S(1)}, u32[]{:S(2)}, u32[]{:S(2)}) %collective-permute-start.6) | collective-permute-done | bytes 36896 | tf_op jit(solution)/shard_map/ppermute | solution.py:370
  21.1 0.0 copy-done
  21.1 0.5 project.1
  21.6 16.0 %all_to_all.15.parts = f32[8,16,256]{2,1,0:T(8,128)S(1)} all-to-all(f32[8,16,256]{2,1,0:T(8,128)S(1)} %project.1), channel_id=1, replica_groups=mesh['ctx'=32,'tp'=8] {'tp'}, dimensions={0} | all-to-all | bytes 262144 | tf_op jit(solution)/shard_map/all_to_all | solution.py:382
  37.6 0.0 slice-done
  37.6 1.6 %head_other.1 = (f32[16,16,512]{2,1,0:T(8,128)S(1)}, bf16[16,256]{1,0:T(8,128)(2,1)S(1)}, f32[16,128]{1,0:T(8,128)S(1)}) custom-call(f32[8,16,256]{2,1,0:T(8,128)S(1)} %all_to_all.15.parts, bf16[16,256]{1,0:T(8,128)(2,1)S(1)} %get-tuple-element.17.residual, f32[1,256]{1,0:T(1,128)S(1)} %get-tuple-element.18.gain, bf16[16032,256]{1,0:T(8,128)(2,1)S(1)} %bitcast.14), custom_call_target="tpu_custom_call" | custom-call | bytes 4194304 | tf_op jit(solution)/shard_map/head_other/pallas_call | solution.py:293
  39.2 5.1 %collective-permute-start.7 = (f32[16,16,512]{2,1,0:T(8,128)S(1)}, f32[16,16,512]{2,1,0:T(8,128)S(1)}, u32[]{:S(2)}, u32[]{:S(2)}) collective-permute-start(f32[16,16,512]{2,1,0:T(8,128)S(1)} %get-tuple-element.21), channel_id=1, source_target_pairs={{0,8},{8,0},{16,24},{24,16},{32,40},{40,32},{48,56},{56,48},{64,72... | collective-permute-start | bytes 1572872 | tf_op jit(solution)/shard_map/ppermute | solution.py:391
  44.3 1.6 %head_same.1.one = f32[16,16,512]{2,1,0:T(8,128)S(1)} custom-call(bf16[16,256]{1,0:T(8,128)(2,1)S(1)} %get-tuple-element.19.scaled, f32[16,128]{1,0:T(8,128)S(1)} %get-tuple-element.20.squares, bf16[16032,256]{1,0:T(8,128)(2,1)S(1)} %bitcast.15), custom_call_target="tpu_custom_call" | custom-call | bytes 4194304 | tf_op jit(solution)/shard_map/head_same/pallas_call | solution.py:293
  45.9 0.0 collective-permute-done.7.two
  45.9 0.1 add_cores.1
  45.9 13.1 %all_to_all.16.parts = f32[16,16,512]{2,1,0:T(8,128)S(1)} all-to-all(f32[16,16,512]{2,1,0:T(8,128)S(1)} %add_cores.1), channel_id=1, replica_groups={{0,16,32,48,64,80,96,112,128,144,160,176,192,208,224,240},{8,24,40,56,7..., dimensions={0} | all-to-all | bytes 1048576 | tf_op jit(solution)/shard_map/all_to_all | solution.py:402
  59.0 0.3 vocab_stats.1
  59.3 2.0 %collective-permute-start.8 = (f32[8,128]{1,0:T(8,128)S(1)}, f32[8,128]{1,0:T(8,128)S(1)}, u32[]{:S(2)}, u32[]{:S(2)}) collective-permute-start(f32[8,128]{1,0:T(8,128)S(1)} %get-tuple-element.22.one), channel_id=1, source_target_pairs={{0,8},{8,0},{16,24},{24,16},{32,40},{40,32},{48,56},{56,48},{64,72... | collective-permute-start | bytes 12296 | tf_op jit(solution)/shard_map/ppermute | solution.py:411
  61.3 0.8 %collective-permute-done.8.two = f32[8,128]{1,0:T(8,128)S(1)} collective-permute-done((f32[8,128]{1,0:T(8,128)S(1)}, f32[8,128]{1,0:T(8,128)S(1)}, u32[]{:S(2)}, u32[]{:S(2)}) %collective-permute-start.8) | collective-permute-done | bytes 4128 | tf_op jit(solution)/shard_map/ppermute | solution.py:411
  62.2 0.1 join_stats.1
  62.2 16.1 %all_to_all.17 = f32[128,1,128]{2,1,0:T(1,128)S(1)} all-to-all(f32[128,1,128]{2,1,0:T(1,128)S(1)} %bitcast.17), channel_id=1, replica_groups={{0,1,2,3,4,5,6,7,16,17,18,19,20,21,22,23,32,33,34,35,36,37,38,39,48,49,..., dimensions={0} | all-to-all | bytes 131072 | tf_op jit(solution)/shard_map/all_to_all | solution.py:419
  78.4 0.9 %scores.1 = (f32[8,501]{1,0:T(8,128)}, f32[1,8]{1,0:T(1,128)}) custom-call(f32[128,128]{1,0:T(8,128)S(1)} %bitcast.16, f32[16,512]{1,0:T(8,128)S(1)} %get-tuple-element.23.logits), custom_call_target="tpu_custom_call" | custom-call | tf_op jit(solution)/shard_map/scores/pallas_call | solution.py:293
  (6 shorter events, 0.0 us)
Async XLA Ops:
  3.3 4.2 %collective-permute-start = (f32[72,128]{1,0:T(8,128)S(1)}, f32[72,128]{1,0:T(8,128)S(1)}, u32[]{:S(2)}, u32[]{:S(2)}) collective-permute-start(f32[72,128]{1,0:T(8,128)S(1)} %get-tuple-element.15.refs_0_), channel_id=1, source_target_pairs={{0,8},{8,0},{16,24},{24,16},{32,40},{40,32},{48,56},{56,48},{64,72... | collective-permute-start | bytes 110600 | tf_op jit(solution)/shard_map/ppermute | solution.py:367
  7.5 13.5 %copy-start = (bf16[1024,256]{1,0:T(8,128)(2,1)S(1)}, bf16[1024,256]{1,0:T(8,128)(2,1)}, u32[]{:S(2)}) copy-start(bf16[1024,256]{1,0:T(8,128)(2,1)} %weight.1) | copy-start | bytes 1572868
  7.6 3.3 %collective-permute-start.1 = (f32[72,128]{1,0:T(8,128)S(1)}, f32[72,128]{1,0:T(8,128)S(1)}, u32[]{:S(2)}, u32[]{:S(2)}) collective-permute-start(f32[72,128]{1,0:T(8,128)S(1)} %merge_cores.1.refs_0_), channel_id=1, source_target_pairs={{0,16},{8,24},{16,0},{24,8},{32,48},{40,56},{48,32},{56,40},{64,80... | collective-permute-start | bytes 110600 | tf_op jit(solution)/shard_map/ppermute | solution.py:370
  7.7 4.1 %collective-permute-start.2 = (f32[72,128]{1,0:T(8,128)S(1)}, f32[72,128]{1,0:T(8,128)S(1)}, u32[]{:S(2)}, u32[]{:S(2)}) collective-permute-start(f32[72,128]{1,0:T(8,128)S(1)} %merge_cores.1.refs_0_), channel_id=1, source_target_pairs={{0,48},{8,56},{16,32},{24,40},{32,16},{40,24},{48,0},{56,8},{64,11... | collective-permute-start | bytes 110600 | tf_op jit(solution)/shard_map/ppermute | solution.py:370
  9.1 4.3 %collective-permute-start.3 = (f32[72,128]{1,0:T(8,128)S(1)}, f32[72,128]{1,0:T(8,128)S(1)}, u32[]{:S(2)}, u32[]{:S(2)}) collective-permute-start(f32[72,128]{1,0:T(8,128)S(1)} %merge_cores.1.refs_0_), channel_id=1, source_target_pairs={{0,32},{8,40},{16,48},{24,56},{32,0},{40,8},{48,16},{56,24},{64,96... | collective-permute-start | bytes 110600 | tf_op jit(solution)/shard_map/ppermute | solution.py:370
  13.4 24.2 %slice-start = ((s8[8208384]{0:T(1024)(128)(4,1)}), s8[4194304]{0:T(1024)(128)(4,1)S(1)}, s32[]{:S(2)}) async-start(s8[8208384]{0:T(1024)(128)(4,1)} %bitcast.12), calls=%async_computation.3 | async-start | bytes 8388608
  13.5 3.8 %collective-permute-start.4 = (f32[72,128]{1,0:T(8,128)S(1)}, f32[72,128]{1,0:T(8,128)S(1)}, u32[]{:S(2)}, u32[]{:S(2)}) collective-permute-start(f32[72,128]{1,0:T(8,128)S(1)} %merge_y.1.s0), channel_id=1, source_target_pairs={{0,64},{8,72},{16,80},{24,88},{32,96},{40,104},{48,112},{56,120},{... | collective-permute-start | bytes 110600 | tf_op jit(solution)/shard_map/ppermute | solution.py:370
  14.8 4.0 %collective-permute-start.5 = (f32[72,128]{1,0:T(8,128)S(1)}, f32[72,128]{1,0:T(8,128)S(1)}, u32[]{:S(2)}, u32[]{:S(2)}) collective-permute-start(f32[72,128]{1,0:T(8,128)S(1)} %merge_y.1.s0), channel_id=1, source_target_pairs={{0,192},{8,200},{16,208},{24,216},{32,224},{40,232},{48,240},{56,2... | collective-permute-start | bytes 110600 | tf_op jit(solution)/shard_map/ppermute | solution.py:370
  16.6 4.5 %collective-permute-start.6 = (f32[72,128]{1,0:T(8,128)S(1)}, f32[72,128]{1,0:T(8,128)S(1)}, u32[]{:S(2)}, u32[]{:S(2)}) collective-permute-start(f32[72,128]{1,0:T(8,128)S(1)} %merge_y.1.s0), channel_id=1, source_target_pairs={{0,128},{8,136},{16,144},{24,152},{32,160},{40,168},{48,176},{56,1... | collective-permute-start | bytes 110600 | tf_op jit(solution)/shard_map/ppermute | solution.py:370
  21.1 16.5 %slice-start.1 = ((s8[8208384]{0:T(1024)(128)(4,1)}), s8[4014080]{0:T(1024)(128)(4,1)S(1)}, s32[]{:S(2)}) async-start(s8[8208384]{0:T(1024)(128)(4,1)} %bitcast.12), calls=%async_computation.4 | async-start | bytes 8028160
  39.2 6.6 %collective-permute-start.7 = (f32[16,16,512]{2,1,0:T(8,128)S(1)}, f32[16,16,512]{2,1,0:T(8,128)S(1)}, u32[]{:S(2)}, u32[]{:S(2)}) collective-permute-start(f32[16,16,512]{2,1,0:T(8,128)S(1)} %get-tuple-element.21), channel_id=1, source_target_pairs={{0,8},{8,0},{16,24},{24,16},{32,40},{40,32},{48,56},{56,48},{64,72... | collective-permute-start | bytes 1572872 | tf_op jit(solution)/shard_map/ppermute | solution.py:391
  59.3 2.9 %collective-permute-start.8 = (f32[8,128]{1,0:T(8,128)S(1)}, f32[8,128]{1,0:T(8,128)S(1)}, u32[]{:S(2)}, u32[]{:S(2)}) collective-permute-start(f32[8,128]{1,0:T(8,128)S(1)} %get-tuple-element.22.one), channel_id=1, source_target_pairs={{0,8},{8,0},{16,24},{24,16},{32,40},{40,32},{48,56},{56,48},{64,72... | collective-permute-start | bytes 12296 | tf_op jit(solution)/shard_map/ppermute | solution.py:411

commit v8 on v7

--- a/solution.py
+++ b/solution.py
@@ -38,97 +38,112 @@
             copy.wait()
 
 
-def attention_kernel(
-    lengths_far,
-    queries_far,
-    long_far,
-    short_far,
-    fresh_far,
-    targets_far,
-    residual_far,
-    gain_far,
-    state,
-    aux,
-    wanted,
-    residual,
-    gain,
-    lengths,
-    targets,
-    queries,
-    fresh,
-    long_near,
-    short_near,
-    wide,
-    stat,
-    sems,
-):
-    moves = [
-        (lengths_far, lengths),
-        (queries_far, queries),
-        (long_far.at[0], long_near.at[0]),
-        (fresh_far, fresh),
-        (short_far.at[0], short_near.at[0]),
-        (long_far.at[1], long_near.at[1]),
-        (short_far.at[1], short_near.at[1]),
-        (targets_far, targets),
-        (residual_far, residual),
-        (gain_far, gain),
-    ]
+def begin(moves, sems):
     copies = [pltpu.make_async_copy(*move, sems.at[n]) for n, move in enumerate(moves)]
     for copy in copies:
         copy.start()
-    rows, block_len = long_far.shape[1], long_far.shape[2]
-    finish(copies[:5])
-    query = [queries[0].astype(F32), queries[1].astype(F32)]
-    heads = query[0].shape[0] // rows
-    key = [fresh[0, 0].astype(F32), fresh[1, 0].astype(F32)]
-    value = [fresh[0, 1].astype(F32), fresh[1, 1].astype(F32)]
+    return copies
+
+
+def long_kernel(
+    lengths_far, queries_far, cache_far, state, lengths, queries, cache, wide, stat, sems
+):
+    copies = begin(
+        [
+            (lengths_far, lengths),
+            (queries_far.at[0], queries),
+            (cache_far.at[0], cache.at[0]),
+            (cache_far.at[1], cache.at[1]),
+        ],
+        sems,
+    )
+    rows, block_len = cache.shape[1], cache.shape[2]
+    finish(copies[:3])
+    query = queries[...].astype(F32)
+    heads = query.shape[0] // rows
     position = lax.axis_index("ctx") * block_len + iota((heads, block_len), 1)
     lane = iota((heads, HEAD_DIM), 1)
-    kept, kept_short = [], []
+    kept = []
     for b in range(rows):
-        part = [q[b * heads : (b + 1) * heads] for q in query]
         mask = position < lengths[b]
-        scores = dot_rows(part[0].astype(BF16), long_near[0, b]) * SCORE_SCALE
-        scores = jnp.where(mask, scores, NEG_FILL)
+        scores = dot_rows(query[b * heads : (b + 1) * heads].astype(BF16), cache[0, b])
+        scores = jnp.where(mask, scores * SCORE_SCALE, NEG_FILL)
         top = jnp.max(scores, axis=1, keepdims=True)
         weights = jnp.where(mask, jnp.exp(scores - top), 0.0)
         total = jnp.sum(weights, axis=1, keepdims=True)
         stat[pl.ds(b, heads, stride=rows), :] = jnp.where(lane == 0, top, total)
         kept.append(weights.astype(BF16))
-        own = [
-            jnp.sum(part[n] * key[n][b : b + 1], axis=1, keepdims=True) * SCORE_SCALE
-            for n in range(2)
-        ]
-        scores = dot_rows(part[1].astype(BF16), short_near[0, b]) * SCORE_SCALE
-        top = jnp.max(scores, axis=1, keepdims=True)
-        weights = jnp.exp(scores - top)
-        final = jnp.maximum(top, own[1])
-        older = jnp.exp(top - final)
-        newer = jnp.exp(own[1] - final)
-        scale = 1.0 / (jnp.sum(weights, axis=1, keepdims=True) * older + newer)
-        kept_short.append((weights.astype(BF16), older * scale, newer * scale))
-        where = pl.ds(b, heads, stride=rows)
-        aux[1, where, :] = jnp.broadcast_to(own[0], (heads, HEAD_DIM))
-        aux[2, where, :] = jnp.broadcast_to(value[0][b : b + 1], (heads, HEAD_DIM))
-    finish(copies[5:8])
+    finish(copies[3:])
     for b in range(rows):
-        where = pl.ds(b, heads, stride=rows)
-        wide[where, :] = jnp.dot(kept[b], long_near[1, b], preferred_element_type=F32)
-        weights, older, newer = kept_short[b]
-        output = jnp.dot(weights, short_near[1, b], preferred_element_type=F32)
-        aux[0, where, :] = output * older + newer * value[1][b : b + 1]
+        wide[pl.ds(b, heads, stride=rows), :] = jnp.dot(
+            kept[b], cache[1, b], preferred_element_type=F32
+        )
     half = HEAD_DIM // 2
     turned = wide[...].T
     state[0:half, :] = jnp.concatenate([turned[:half], turned[half:]], axis=1)
     turned = stat[...].T[:8]
     state[half : half + 8, :] = jnp.concatenate([turned, turned], axis=1)
+
+
+def short_kernel(
+    queries_far,
+    cache_far,
+    fresh_far,
+    targets_far,
+    residual_far,
+    gain_far,
+    aux,
+    wanted,
+    residual,
+    gain,
+    targets,
+    queries,
+    fresh,
+    cache,
+    sems,
+):
+    copies = begin(
+        [
+            (queries_far, queries),
+            (fresh_far, fresh),
+            (cache_far.at[0], cache.at[0]),
+            (cache_far.at[1], cache.at[1]),
+            (targets_far, targets),
+            (residual_far, residual),
+            (gain_far, gain),
+        ],
+        sems,
+    )
+    finish(copies)
+    rows = cache.shape[1]
+    query = [queries[0].astype(F32), queries[1].astype(F32)]
+    heads = query[0].shape[0] // rows
+    key = [fresh[0, 0].astype(F32), fresh[1, 0].astype(F32)]
+    value = [fresh[0, 1].astype(F32), fresh[1, 1].astype(F32)]
+    for b in range(rows):
+        part = [q[b * heads : (b + 1) * heads] for q in query]
+        own = [
+            jnp.sum(part[n] * key[n][b : b + 1], axis=1, keepdims=True) * SCORE_SCALE
+            for n in range(2)
+        ]
+        scores = dot_rows(part[1].astype(BF16), cache[0, b]) * SCORE_SCALE
+        top = jnp.max(scores, axis=1, keepdims=True)
+        weights = jnp.exp(scores - top)
+        total = jnp.sum(weights, axis=1, keepdims=True)
+        output = jnp.dot(weights.astype(BF16), cache[1, b], preferred_element_type=F32)
+        final = jnp.maximum(top, own[1])
+        older = jnp.exp(top - final)
+        newer = jnp.exp(own[1] - final)
+        mixed = output * older + newer * value[1][b : b + 1]
+        where = pl.ds(b, heads, stride=rows)
+        aux[0, where, :] = mixed / (total * older + newer)
+        aux[1, where, :] = jnp.broadcast_to(own[0], (heads, HEAD_DIM))
+        aux[2, where, :] = jnp.broadcast_to(value[0][b : b + 1], (heads, HEAD_DIM))
     row = iota(wanted.shape, 0)
     aim = jnp.zeros(wanted.shape, jnp.int32)
     for b in range(rows):
         aim = jnp.where(lax.rem(row, rows) == b, targets[b], aim)
     wanted[...] = aim
-    finish(copies[8:])
 
 
 def merge_states(parts):
@@ -182,14 +197,23 @@
 
 def head_blocks(other, share, left, fill, weight, blocks):
     vocab, padded = weight.shape[0], blocks.shape[2]
-    reach = -(-(share + 15) // 128) * 128
+    fetched = -(-(share + 15) // 16) * 16
+    reach = -(-fetched // 128) * 128
+    blank = jnp.zeros((blocks.shape[1], reach - fetched), F32)
     core = lax.rem(lax.axis_index("ctx"), 2)
     which = 1 - core if other else core
     lane = iota((blocks.shape[1], padded), 1)
     for k in range(blocks.shape[0]):
         offset = (2 * k + which) * share
-        base = pl.multiple_of(jnp.minimum(offset // 16 * 16, vocab - reach), 16)
-        product = dot_rows(left, weight[pl.ds(base, reach), :])
+        base = pl.multiple_of(jnp.minimum(offset // 16 * 16, vocab - fetched), 16)
+        product = jnp.concatenate(
+            [
+                dot_rows(left, weight[pl.ds(base, padded), :]),
+                dot_rows(left, weight[pl.ds(base + padded, fetched - padded), :]),
+                blank,
+            ],
+            axis=1,
+        )
         moved = pltpu.roll(product, lax.rem(reach - (offset - base), reach), 1)[:, :padded]
         blocks[k] = jnp.where(lane < share, moved, fill)
 
@@ -331,54 +355,65 @@
     fresh = new_kv.reshape(2, 2, row_count, HEAD_DIM)
 
     weight_rows = head_weight.T
-    state, aux, wanted, residual_near, gain_near = call(
-        attention_kernel,
-        [
-            ((packed, 128), F32),
+    state = call(
+        long_kernel,
+        [((packed, 128), F32)],
+        [ANY] * 3,
+        "long_attention",
+        [
+            pltpu.SMEM((row_count,), jnp.int32),
+            pltpu.VMEM((pairs, HEAD_DIM), BF16),
+            pltpu.VMEM(long_rows.shape, BF16),
+            pltpu.VMEM((pairs, HEAD_DIM), F32),
+            pltpu.VMEM((pairs, HEAD_DIM), F32),
+            pltpu.SemaphoreType.DMA((4,)),
+        ],
+        moved=2 * 1024 * 1024,
+    )(lengths, flat_queries, long_rows)
+    other = lax.ppermute(state, "ctx", cores)
+    def ring(value, masks):
+        return [
+            lax.ppermute(value, "ctx", [(i, i ^ m) for i in range(ctx_size)]) for m in masks
+        ]
+
+    state = call(join_kernel, [((packed, 128), F32)], [VMEM] * 2, "merge_cores", flops=BESIDE)(
+        state, other
+    )
+    near_y = ring(state, (2, 6, 4))
+    state = call(join_kernel, [((packed, 128), F32)], [VMEM] * 4, "merge_y", flops=BESIDE)(
+        state, *near_y
+    )
+    state, fresh = lax.optimization_barrier((state, fresh))
+    near_x = ring(state, (8, 24, 16))
+    aux, wanted, residual_near, gain_near = call(
+        short_kernel,
+        [
             ((3, pairs, HEAD_DIM), F32),
             ((rows, 128), jnp.int32),
             ((rows, width), BF16),
             ((1, width), F32),
         ],
-        [ANY] * 8,
-        "attention",
-        [
-            pltpu.SMEM((row_count,), jnp.int32),
+        [ANY] * 6,
+        "short_attention",
+        [
             pltpu.SMEM((row_count,), jnp.int32),
             pltpu.VMEM(flat_queries.shape, BF16),
             pltpu.VMEM(fresh.shape, BF16),
-            pltpu.VMEM(long_rows.shape, BF16),
             pltpu.VMEM(short_rows.shape, BF16),
-            pltpu.VMEM((pairs, HEAD_DIM), F32),
-            pltpu.VMEM((pairs, HEAD_DIM), F32),
-            pltpu.SemaphoreType.DMA((10,)),
-        ],
-        moved=3 * 1024 * 1024,
+            pltpu.SemaphoreType.DMA((7,)),
+        ],
+        moved=1024 * 1024,
     )(
-        lengths,
         flat_queries,
-        long_rows,
         short_rows,
         fresh,
         targets,
         residual.reshape(rows, width),
         final_gain.reshape(1, width),
     )
-    other = lax.ppermute(state, "ctx", cores)
-    def ring(value, masks):
-        return [
-            lax.ppermute(value, "ctx", [(i, i ^ m) for i in range(ctx_size)]) for m in masks
-        ]
-
-    state = call(join_kernel, [((packed, 128), F32)], [VMEM] * 2, "merge_cores", flops=BESIDE)(
-        state, other
-    )
-    state = call(join_kernel, [((packed, 128), F32)], [VMEM] * 4, "merge_y", flops=BESIDE)(
-        state, *ring(state, (2, 6, 4))
-    )
     spread = call(
         project_kernel, [((tp_size, rows, width), F32)], [VMEM] * 6, "project", flops=BESIDE
-    )(state, *ring(state, (8, 24, 16)), aux, out_weight)
+    )(state, *near_x, aux, out_weight)
     parts = lax.all_to_all(spread, "tp", 0, 0, tiled=True)
 
     theirs, scaled, squares = call(

time: 79.4 us -> 79 us (level)
  waiting for transfers between devices: 8.09 us -> 4.83 us
  Pallas kernels: 7.62 us -> 10.2 us
    ppermute x6, waiting for transfers between devices: 6.4 us -> 2.93 us  [ring(): lax.ppermute(value, 'ctx', [(i, i ^ m) for i in range(ctx_size)])]
    pallas_call x10 -> x11, Pallas kernels: 7.62 us -> 10.2 us  [pinned(): run(*(pltpu.with_memory_space_constraint(operand, pltpu.HBM) if spec is A...]
  transfers between devices with their start and end apart: 9 -> 9, of which waited for: 6 -> 6; matrix products, arithmetic and copies ran while one was open for 0% -> 0% of each run, Pallas kernels for 2% -> 6%
where the time goes in v8:
time: 79 us; the launch traced here: 78.7 us
  blocking collectives  45.3 us (57%)
  starting transfers between devices  17.7 us (22%)
  Pallas kernels  10.2 us (13%)
  waiting for transfers between devices  4.83 us (6%)
    all_to_all x1, blocking collectives, per_device(): lax.all_to_all(spread.reshape(devices, 1, 128), ('ctx', 'tp'), 0, 0, tile...  16.1 us
    all_to_all x1, blocking collectives, per_device(): parts = lax.all_to_all(spread, 'tp', 0, 0, tiled=True)  15.9 us
    all_to_all x1, blocking collectives, per_device(): lax.all_to_all(blocks, 'ctx', 0, 0, tiled=True, axis_index_groups=same_core)  13.3 us
    pallas_call x11, Pallas kernels, pinned(): run(*(pltpu.with_memory_space_constraint(operand, pltpu.HBM) if spec is A...  10.2 us
    ppermute x6, starting transfers between devices, ring(): lax.ppermute(value, 'ctx', [(i, i ^ m) for i in range(ctx_size)])  7.08 us
    ppermute x1, starting transfers between devices, per_device(): arrived = lax.ppermute(theirs, 'ctx', cores)  5.08 us
    ppermute x1, starting transfers between devices, per_device(): other = lax.ppermute(state, 'ctx', cores)  3.33 us
    ppermute x6, waiting for transfers between devices, ring(): lax.ppermute(value, 'ctx', [(i, i ^ m) for i in range(ctx_size)])  2.93 us
  transfers between devices with their start and end apart: 9, of which 6 were waited for; matrix products, arithmetic and copies ran while one was open for 0% of the time, Pallas kernels for 6%

profile of v8, /device:TPU:1, one launch (start us, length us, event | category | flops | bytes accessed | tf_op | source)
XLA Modules:
  0.0 78.7 jit_solution(9719072943335998191)
XLA Ops:
  0.6 2.3 %long_attention.1.refs_0_ = f32[72,128]{1,0:T(8,128)S(1)} custom-call(s32[8]{0:T(128)} %lengths_far.1, bf16[2,64,128]{2,1,0:T(8,128)(2,1)} %bitcast.20, bf16[2,8,512,128]{3,2,1,0:T(8,128)(2,1)} %bitcast.18), custom_call_target="tpu_custom_call" | custom-call | bytes 2097152 | tf_op jit(solution)/shard_map/long_attention/pallas_call | solution.py:317
  2.9 3.3 %collective-permute-start = (f32[72,128]{1,0:T(8,128)S(1)}, f32[72,128]{1,0:T(8,128)S(1)}, u32[]{:S(2)}, u32[]{:S(2)}) collective-permute-start(f32[72,128]{1,0:T(8,128)S(1)} %long_attention.1.refs_0_), channel_id=1, source_target_pairs={{0,8},{8,0},{16,24},{24,16},{32,40},{40,32},{48,56},{56,48},{64,72... | collective-permute-start | bytes 110600 | tf_op jit(solution)/shard_map/ppermute | solution.py:373
  6.2 0.9 %collective-permute-done.refs_1_ = f32[72,128]{1,0:T(8,128)S(1)} collective-permute-done((f32[72,128]{1,0:T(8,128)S(1)}, f32[72,128]{1,0:T(8,128)S(1)}, u32[]{:S(2)}, u32[]{:S(2)}) %collective-permute-start) | collective-permute-done | bytes 36896 | tf_op jit(solution)/shard_map/ppermute | solution.py:373
  7.1 0.0 copy-start
  7.1 0.1 collective-permute-start.1
  7.2 1.4 %collective-permute-start.2 = (f32[72,128]{1,0:T(8,128)S(1)}, f32[72,128]{1,0:T(8,128)S(1)}, u32[]{:S(2)}, u32[]{:S(2)}) collective-permute-start(f32[72,128]{1,0:T(8,128)S(1)} %merge_cores.1.refs_0_), channel_id=1, source_target_pairs={{0,48},{8,56},{16,32},{24,40},{32,16},{40,24},{48,0},{56,8},{64,11... | collective-permute-start | bytes 110600 | tf_op jit(solution)/shard_map/ppermute | solution.py:376
  8.7 1.8 %collective-permute-start.3 = (f32[72,128]{1,0:T(8,128)S(1)}, f32[72,128]{1,0:T(8,128)S(1)}, u32[]{:S(2)}, u32[]{:S(2)}) collective-permute-start(f32[72,128]{1,0:T(8,128)S(1)} %merge_cores.1.refs_0_), channel_id=1, source_target_pairs={{0,32},{8,40},{16,48},{24,56},{32,0},{40,8},{48,16},{56,24},{64,96... | collective-permute-start | bytes 110600 | tf_op jit(solution)/shard_map/ppermute | solution.py:376
  10.5 0.0 collective-permute-done.1.refs_1_
  10.5 0.9 %collective-permute-done.2.refs_2_ = f32[72,128]{1,0:T(8,128)S(1)} collective-permute-done((f32[72,128]{1,0:T(8,128)S(1)}, f32[72,128]{1,0:T(8,128)S(1)}, u32[]{:S(2)}, u32[]{:S(2)}) %collective-permute-start.2) | collective-permute-done | bytes 36896 | tf_op jit(solution)/shard_map/ppermute | solution.py:376
  11.3 1.7 %collective-permute-done.3.refs_3_ = f32[72,128]{1,0:T(8,128)S(1)} collective-permute-done((f32[72,128]{1,0:T(8,128)S(1)}, f32[72,128]{1,0:T(8,128)S(1)}, u32[]{:S(2)}, u32[]{:S(2)}) %collective-permute-start.3) | collective-permute-done | bytes 36896 | tf_op jit(solution)/shard_map/ppermute | solution.py:376
  13.0 1.3 %collective-permute-start.4 = (f32[72,128]{1,0:T(8,128)S(1)}, f32[72,128]{1,0:T(8,128)S(1)}, u32[]{:S(2)}, u32[]{:S(2)}) collective-permute-start(f32[72,128]{1,0:T(8,128)S(1)} %merge_y.1.s0), channel_id=1, source_target_pairs={{0,64},{8,72},{16,80},{24,88},{32,96},{40,104},{48,112},{56,120},{... | collective-permute-start | bytes 110600 | tf_op jit(solution)/shard_map/ppermute | solution.py:376
  14.3 1.8 %collective-permute-start.5 = (f32[72,128]{1,0:T(8,128)S(1)}, f32[72,128]{1,0:T(8,128)S(1)}, u32[]{:S(2)}, u32[]{:S(2)}) collective-permute-start(f32[72,128]{1,0:T(8,128)S(1)} %merge_y.1.s0), channel_id=1, source_target_pairs={{0,192},{8,200},{16,208},{24,216},{32,224},{40,232},{48,240},{56,2... | collective-permute-start | bytes 110600 | tf_op jit(solution)/shard_map/ppermute | solution.py:376
  16.1 0.6 collective-permute-start.6
  16.8 3.4 %short_attention.1 = (f32[3,64,128]{2,1,0:T(8,128)S(1)}, s32[16,128]{1,0:T(8,128)S(1)}, bf16[16,256]{1,0:T(8,128)(2,1)S(1)}, f32[1,256]{1,0:T(1,128)S(1)}) custom-call(bf16[2,64,128]{2,1,0:T(8,128)(2,1)} %bitcast.21, bf16[2,8,256,128]{3,2,1,0:T(8,128)(2,1)} %bitcast.19, bf16[2,2,8,128]{3,2,1,0:T(8,128)(2,1)} %bitcast.22, s32[8]{0:T(128)} %targets_far.1, ...), custom_call_target="tpu_custom_call" | custom-call | bytes 1048576 | tf_op jit(solution)/shard_map/short_attention/pallas_call | solution.py:317
  20.2 0.0 collective-permute-done.4.s1
  20.2 0.0 collective-permute-done.5.s2
  20.3 0.4 collective-permute-done.6.s3
  20.7 0.0 copy-done
  20.7 0.5 project.1
  21.1 15.9 %all_to_all.15.parts = f32[8,16,256]{2,1,0:T(8,128)S(1)} all-to-all(f32[8,16,256]{2,1,0:T(8,128)S(1)} %project.1), channel_id=1, replica_groups=mesh['ctx'=32,'tp'=8] {'tp'}, dimensions={0} | all-to-all | bytes 262144 | tf_op jit(solution)/shard_map/all_to_all | solution.py:417
  37.1 1.3 %head_other.1 = (f32[16,16,512]{2,1,0:T(8,128)S(1)}, bf16[16,256]{1,0:T(8,128)(2,1)S(1)}, f32[16,128]{1,0:T(8,128)S(1)}) custom-call(f32[8,16,256]{2,1,0:T(8,128)S(1)} %all_to_all.15.parts, bf16[16,256]{1,0:T(8,128)(2,1)S(1)} %get-tuple-element.19.residual, f32[1,256]{1,0:T(1,128)S(1)} %get-tuple-element.20.gain, bf16[16032,256]{1,0:T(8,128)(2,1)S(1)} %bitcast.14), custom_call_target="tpu_custom_call" | custom-call | bytes 4194304 | tf_op jit(solution)/shard_map/head_other/pallas_call | solution.py:317
  38.4 5.1 %collective-permute-start.7 = (f32[16,16,512]{2,1,0:T(8,128)S(1)}, f32[16,16,512]{2,1,0:T(8,128)S(1)}, u32[]{:S(2)}, u32[]{:S(2)}) collective-permute-start(f32[16,16,512]{2,1,0:T(8,128)S(1)} %get-tuple-element.23), channel_id=1, source_target_pairs={{0,8},{8,0},{16,24},{24,16},{32,40},{40,32},{48,56},{56,48},{64,72... | collective-permute-start | bytes 1572872 | tf_op jit(solution)/shard_map/ppermute | solution.py:426
  43.5 1.3 %head_same.1.one = f32[16,16,512]{2,1,0:T(8,128)S(1)} custom-call(bf16[16,256]{1,0:T(8,128)(2,1)S(1)} %get-tuple-element.21.scaled, f32[16,128]{1,0:T(8,128)S(1)} %get-tuple-element.22.squares, bf16[16032,256]{1,0:T(8,128)(2,1)S(1)} %bitcast.15), custom_call_target="tpu_custom_call" | custom-call | bytes 4194304 | tf_op jit(solution)/shard_map/head_same/pallas_call | solution.py:317
  44.8 0.2 collective-permute-done.7.two
  45.0 0.1 add_cores.1
  45.1 13.3 %all_to_all.16.parts = f32[16,16,512]{2,1,0:T(8,128)S(1)} all-to-all(f32[16,16,512]{2,1,0:T(8,128)S(1)} %add_cores.1), channel_id=1, replica_groups={{0,16,32,48,64,80,96,112,128,144,160,176,192,208,224,240},{8,24,40,56,7..., dimensions={0} | all-to-all | bytes 1048576 | tf_op jit(solution)/shard_map/all_to_all | solution.py:437
  58.4 0.3 vocab_stats.1
  58.7 2.2 %collective-permute-start.8 = (f32[8,128]{1,0:T(8,128)S(1)}, f32[8,128]{1,0:T(8,128)S(1)}, u32[]{:S(2)}, u32[]{:S(2)}) collective-permute-start(f32[8,128]{1,0:T(8,128)S(1)} %get-tuple-element.24.one), channel_id=1, source_target_pairs={{0,8},{8,0},{16,24},{24,16},{32,40},{40,32},{48,56},{56,48},{64,72... | collective-permute-start | bytes 12296 | tf_op jit(solution)/shard_map/ppermute | solution.py:446
  60.8 0.8 %collective-permute-done.8.two = f32[8,128]{1,0:T(8,128)S(1)} collective-permute-done((f32[8,128]{1,0:T(8,128)S(1)}, f32[8,128]{1,0:T(8,128)S(1)}, u32[]{:S(2)}, u32[]{:S(2)}) %collective-permute-start.8) | collective-permute-done | bytes 4128 | tf_op jit(solution)/shard_map/ppermute | solution.py:446
  61.7 0.1 join_stats.1
  61.7 16.1 %all_to_all.17 = f32[128,1,128]{2,1,0:T(1,128)S(1)} all-to-all(f32[128,1,128]{2,1,0:T(1,128)S(1)} %bitcast.17), channel_id=1, replica_groups={{0,1,2,3,4,5,6,7,16,17,18,19,20,21,22,23,32,33,34,35,36,37,38,39,48,49,..., dimensions={0} | all-to-all | bytes 131072 | tf_op jit(solution)/shard_map/all_to_all | solution.py:454
  77.9 0.9 %scores.1 = (f32[8,501]{1,0:T(8,128)}, f32[1,8]{1,0:T(1,128)}) custom-call(f32[128,128]{1,0:T(8,128)S(1)} %bitcast.16, f32[16,512]{1,0:T(8,128)S(1)} %get-tuple-element.25.logits), custom_call_target="tpu_custom_call" | custom-call | tf_op jit(solution)/shard_map/scores/pallas_call | solution.py:317
  (7 shorter events, 0.0 us)
Async XLA Ops:
  2.9 4.2 %collective-permute-start = (f32[72,128]{1,0:T(8,128)S(1)}, f32[72,128]{1,0:T(8,128)S(1)}, u32[]{:S(2)}, u32[]{:S(2)}) collective-permute-start(f32[72,128]{1,0:T(8,128)S(1)} %long_attention.1.refs_0_), channel_id=1, source_target_pairs={{0,8},{8,0},{16,24},{24,16},{32,40},{40,32},{48,56},{56,48},{64,72... | collective-permute-start | bytes 110600 | tf_op jit(solution)/shard_map/ppermute | solution.py:373
  7.1 13.5 %copy-start = (bf16[1024,256]{1,0:T(8,128)(2,1)S(1)}, bf16[1024,256]{1,0:T(8,128)(2,1)}, u32[]{:S(2)}) copy-start(bf16[1024,256]{1,0:T(8,128)(2,1)} %weight.1) | copy-start | bytes 1572868
  7.1 3.3 %collective-permute-start.1 = (f32[72,128]{1,0:T(8,128)S(1)}, f32[72,128]{1,0:T(8,128)S(1)}, u32[]{:S(2)}, u32[]{:S(2)}) collective-permute-start(f32[72,128]{1,0:T(8,128)S(1)} %merge_cores.1.refs_0_), channel_id=1, source_target_pairs={{0,16},{8,24},{16,0},{24,8},{32,48},{40,56},{48,32},{56,40},{64,80... | collective-permute-start | bytes 110600 | tf_op jit(solution)/shard_map/ppermute | solution.py:376
  7.2 4.1 %collective-permute-start.2 = (f32[72,128]{1,0:T(8,128)S(1)}, f32[72,128]{1,0:T(8,128)S(1)}, u32[]{:S(2)}, u32[]{:S(2)}) collective-permute-start(f32[72,128]{1,0:T(8,128)S(1)} %merge_cores.1.refs_0_), channel_id=1, source_target_pairs={{0,48},{8,56},{16,32},{24,40},{32,16},{40,24},{48,0},{56,8},{64,11... | collective-permute-start | bytes 110600 | tf_op jit(solution)/shard_map/ppermute | solution.py:376
  8.7 4.3 %collective-permute-start.3 = (f32[72,128]{1,0:T(8,128)S(1)}, f32[72,128]{1,0:T(8,128)S(1)}, u32[]{:S(2)}, u32[]{:S(2)}) collective-permute-start(f32[72,128]{1,0:T(8,128)S(1)} %merge_cores.1.refs_0_), channel_id=1, source_target_pairs={{0,32},{8,40},{16,48},{24,56},{32,0},{40,8},{48,16},{56,24},{64,96... | collective-permute-start | bytes 110600 | tf_op jit(solution)/shard_map/ppermute | solution.py:376
  13.0 24.1 %slice-start = ((s8[8208384]{0:T(1024)(128)(4,1)}), s8[4194304]{0:T(1024)(128)(4,1)S(1)}, s32[]{:S(2)}) async-start(s8[8208384]{0:T(1024)(128)(4,1)} %bitcast.12), calls=%async_computation.3 | async-start | bytes 8388608
  13.0 7.2 %collective-permute-start.4 = (f32[72,128]{1,0:T(8,128)S(1)}, f32[72,128]{1,0:T(8,128)S(1)}, u32[]{:S(2)}, u32[]{:S(2)}) collective-permute-start(f32[72,128]{1,0:T(8,128)S(1)} %merge_y.1.s0), channel_id=1, source_target_pairs={{0,64},{8,72},{16,80},{24,88},{32,96},{40,104},{48,112},{56,120},{... | collective-permute-start | bytes 110600 | tf_op jit(solution)/shard_map/ppermute | solution.py:376
  14.3 5.9 %collective-permute-start.5 = (f32[72,128]{1,0:T(8,128)S(1)}, f32[72,128]{1,0:T(8,128)S(1)}, u32[]{:S(2)}, u32[]{:S(2)}) collective-permute-start(f32[72,128]{1,0:T(8,128)S(1)} %merge_y.1.s0), channel_id=1, source_target_pairs={{0,192},{8,200},{16,208},{24,216},{32,224},{40,232},{48,240},{56,2... | collective-permute-start | bytes 110600 | tf_op jit(solution)/shard_map/ppermute | solution.py:376
  16.1 4.5 %collective-permute-start.6 = (f32[72,128]{1,0:T(8,128)S(1)}, f32[72,128]{1,0:T(8,128)S(1)}, u32[]{:S(2)}, u32[]{:S(2)}) collective-permute-start(f32[72,128]{1,0:T(8,128)S(1)} %merge_y.1.s0), channel_id=1, source_target_pairs={{0,128},{8,136},{16,144},{24,152},{32,160},{40,168},{48,176},{56,1... | collective-permute-start | bytes 110600 | tf_op jit(solution)/shard_map/ppermute | solution.py:376
  16.8 20.3 %slice-start.1 = ((s8[8208384]{0:T(1024)(128)(4,1)}), s8[4014080]{0:T(1024)(128)(4,1)S(1)}, s32[]{:S(2)}) async-start(s8[8208384]{0:T(1024)(128)(4,1)} %bitcast.12), calls=%async_computation.4 | async-start | bytes 8028160
  38.4 6.6 %collective-permute-start.7 = (f32[16,16,512]{2,1,0:T(8,128)S(1)}, f32[16,16,512]{2,1,0:T(8,128)S(1)}, u32[]{:S(2)}, u32[]{:S(2)}) collective-permute-start(f32[16,16,512]{2,1,0:T(8,128)S(1)} %get-tuple-element.23), channel_id=1, source_target_pairs={{0,8},{8,0},{16,24},{24,16},{32,40},{40,32},{48,56},{56,48},{64,72... | collective-permute-start | bytes 1572872 | tf_op jit(solution)/shard_map/ppermute | solution.py:426
  58.7 3.0 %collective-permute-start.8 = (f32[8,128]{1,0:T(8,128)S(1)}, f32[8,128]{1,0:T(8,128)S(1)}, u32[]{:S(2)}, u32[]{:S(2)}) collective-permute-start(f32[8,128]{1,0:T(8,128)S(1)} %get-tuple-element.24.one), channel_id=1, source_target_pairs={{0,8},{8,0},{16,24},{24,16},{32,40},{40,32},{48,56},{56,48},{64,72... | collective-permute-start | bytes 12296 | tf_op jit(solution)/shard_map/ppermute | solution.py:446

commit v9 on v8

--- a/solution.py
+++ b/solution.py
@@ -86,9 +86,9 @@
 
 
 def short_kernel(
-    queries_far,
-    cache_far,
-    fresh_far,
+    queries,
+    cache,
+    fresh,
     targets_far,
     residual_far,
     gain_far,
@@ -97,24 +97,16 @@
     residual,
     gain,
     targets,
-    queries,
-    fresh,
-    cache,
     sems,
 ):
     copies = begin(
         [
-            (queries_far, queries),
-            (fresh_far, fresh),
-            (cache_far.at[0], cache.at[0]),
-            (cache_far.at[1], cache.at[1]),
             (targets_far, targets),
             (residual_far, residual),
             (gain_far, gain),
         ],
         sems,
     )
-    finish(copies)
     rows = cache.shape[1]
     query = [queries[0].astype(F32), queries[1].astype(F32)]
     heads = query[0].shape[0] // rows
@@ -139,6 +131,7 @@
         aux[0, where, :] = mixed / (total * older + newer)
         aux[1, where, :] = jnp.broadcast_to(own[0], (heads, HEAD_DIM))
         aux[2, where, :] = jnp.broadcast_to(value[0][b : b + 1], (heads, HEAD_DIM))
+    finish(copies)
     row = iota(wanted.shape, 0)
     aim = jnp.zeros(wanted.shape, jnp.int32)
     for b in range(rows):
@@ -393,15 +386,9 @@
             ((rows, width), BF16),
             ((1, width), F32),
         ],
-        [ANY] * 6,
+        [VMEM] * 3 + [ANY] * 3,
         "short_attention",
-        [
-            pltpu.SMEM((row_count,), jnp.int32),
-            pltpu.VMEM(flat_queries.shape, BF16),
-            pltpu.VMEM(fresh.shape, BF16),
-            pltpu.VMEM(short_rows.shape, BF16),
-            pltpu.SemaphoreType.DMA((7,)),
-        ],
+        [pltpu.SMEM((row_count,), jnp.int32), pltpu.SemaphoreType.DMA((3,))],
         moved=1024 * 1024,
     )(
         flat_queries,

time: 79 us -> 78.6 us (level)
  Pallas kernels: 10.2 us -> 8.77 us
  waiting for transfers between devices: 4.83 us -> 6.21 us
    pallas_call x11, Pallas kernels: 10.2 us -> 8.77 us  [pinned(): run(*(pltpu.with_memory_space_constraint(operand, pltpu.HBM) if spec is A...]
    ppermute x6, waiting for transfers between devices: 2.93 us -> 4.31 us  [ring(): lax.ppermute(value, 'ctx', [(i, i ^ m) for i in range(ctx_size)])]
  transfers between devices with their start and end apart: 9 -> 9, of which waited for: 6 -> 6; matrix products, arithmetic and copies ran while one was open for 0% -> 0% of each run, Pallas kernels for 6% -> 4%
where the time goes in v9:
time: 78.6 us; the launch traced here: 78.4 us
  blocking collectives  45.1 us (57%)
  starting transfers between devices  17.6 us (22%)
  Pallas kernels  8.77 us (11%)
  waiting for transfers between devices  6.21 us (8%)
    all_to_all x1, blocking collectives, per_device(): lax.all_to_all(spread.reshape(devices, 1, 128), ('ctx', 'tp'), 0, 0, tile...  16.1 us
    all_to_all x1, blocking collectives, per_device(): parts = lax.all_to_all(spread, 'tp', 0, 0, tiled=True)  15.9 us
    all_to_all x1, blocking collectives, per_device(): lax.all_to_all(blocks, 'ctx', 0, 0, tiled=True, axis_index_groups=same_core)  13.1 us
    pallas_call x11, Pallas kernels, pinned(): run(*(pltpu.with_memory_space_constraint(operand, pltpu.HBM) if spec is A...  8.77 us
    ppermute x6, starting transfers between devices, ring(): lax.ppermute(value, 'ctx', [(i, i ^ m) for i in range(ctx_size)])  7.08 us
    ppermute x1, starting transfers between devices, per_device(): arrived = lax.ppermute(theirs, 'ctx', cores)  5.08 us
    ppermute x6, waiting for transfers between devices, ring(): lax.ppermute(value, 'ctx', [(i, i ^ m) for i in range(ctx_size)])  4.31 us
    ppermute x1, starting transfers between devices, per_device(): other = lax.ppermute(state, 'ctx', cores)  3.33 us
  transfers between devices with their start and end apart: 9, of which 6 were waited for; matrix products, arithmetic and copies ran while one was open for 0% of the time, Pallas kernels for 4%

profile of v9, /device:TPU:1, one launch (start us, length us, event | category | flops | bytes accessed | tf_op | source)
XLA Modules:
  0.0 78.4 jit_solution(16881077143462846442)
XLA Ops:
  0.6 2.3 %long_attention.1.refs_0_ = f32[72,128]{1,0:T(8,128)S(1)} custom-call(s32[8]{0:T(128)} %lengths_far.1, bf16[2,64,128]{2,1,0:T(8,128)(2,1)} %bitcast.19, bf16[2,8,512,128]{3,2,1,0:T(8,128)(2,1)} %bitcast.22), custom_call_target="tpu_custom_call" | custom-call | bytes 2097152 | tf_op jit(solution)/shard_map/long_attention/pallas_call | solution.py:310
  2.9 3.3 %collective-permute-start = (f32[72,128]{1,0:T(8,128)S(1)}, f32[72,128]{1,0:T(8,128)S(1)}, u32[]{:S(2)}, u32[]{:S(2)}) collective-permute-start(f32[72,128]{1,0:T(8,128)S(1)} %long_attention.1.refs_0_), channel_id=1, source_target_pairs={{0,8},{8,0},{16,24},{24,16},{32,40},{40,32},{48,56},{56,48},{64,72... | collective-permute-start | bytes 110600 | tf_op jit(solution)/shard_map/ppermute | solution.py:366
  6.2 0.9 %collective-permute-done.refs_1_ = f32[72,128]{1,0:T(8,128)S(1)} collective-permute-done((f32[72,128]{1,0:T(8,128)S(1)}, f32[72,128]{1,0:T(8,128)S(1)}, u32[]{:S(2)}, u32[]{:S(2)}) %collective-permute-start) | collective-permute-done | bytes 36896 | tf_op jit(solution)/shard_map/ppermute | solution.py:366
  7.1 0.0 copy-start
  7.1 0.0 copy-start.1
  7.1 0.0 copy-start.2
  7.1 0.0 copy-start.3
  7.2 0.1 collective-permute-start.1
  7.3 1.4 %collective-permute-start.2 = (f32[72,128]{1,0:T(8,128)S(1)}, f32[72,128]{1,0:T(8,128)S(1)}, u32[]{:S(2)}, u32[]{:S(2)}) collective-permute-start(f32[72,128]{1,0:T(8,128)S(1)} %merge_cores.1.refs_0_), channel_id=1, source_target_pairs={{0,48},{8,56},{16,32},{24,40},{32,16},{40,24},{48,0},{56,8},{64,11... | collective-permute-start | bytes 110600 | tf_op jit(solution)/shard_map/ppermute | solution.py:369
  8.7 1.8 %collective-permute-start.3 = (f32[72,128]{1,0:T(8,128)S(1)}, f32[72,128]{1,0:T(8,128)S(1)}, u32[]{:S(2)}, u32[]{:S(2)}) collective-permute-start(f32[72,128]{1,0:T(8,128)S(1)} %merge_cores.1.refs_0_), channel_id=1, source_target_pairs={{0,32},{8,40},{16,48},{24,56},{32,0},{40,8},{48,16},{56,24},{64,96... | collective-permute-start | bytes 110600 | tf_op jit(solution)/shard_map/ppermute | solution.py:369
  10.5 0.9 %collective-permute-done.2.refs_2_ = f32[72,128]{1,0:T(8,128)S(1)} collective-permute-done((f32[72,128]{1,0:T(8,128)S(1)}, f32[72,128]{1,0:T(8,128)S(1)}, u32[]{:S(2)}, u32[]{:S(2)}) %collective-permute-start.2) | collective-permute-done | bytes 36896 | tf_op jit(solution)/shard_map/ppermute | solution.py:369
  11.4 1.7 %collective-permute-done.3.refs_3_ = f32[72,128]{1,0:T(8,128)S(1)} collective-permute-done((f32[72,128]{1,0:T(8,128)S(1)}, f32[72,128]{1,0:T(8,128)S(1)}, u32[]{:S(2)}, u32[]{:S(2)}) %collective-permute-start.3) | collective-permute-done | bytes 36896 | tf_op jit(solution)/shard_map/ppermute | solution.py:369
  13.1 1.3 %collective-permute-start.4 = (f32[72,128]{1,0:T(8,128)S(1)}, f32[72,128]{1,0:T(8,128)S(1)}, u32[]{:S(2)}, u32[]{:S(2)}) collective-permute-start(f32[72,128]{1,0:T(8,128)S(1)} %merge_y.1.s0), channel_id=1, source_target_pairs={{0,64},{8,72},{16,80},{24,88},{32,96},{40,104},{48,112},{56,120},{... | collective-permute-start | bytes 110600 | tf_op jit(solution)/shard_map/ppermute | solution.py:369
  14.4 1.8 %collective-permute-start.5 = (f32[72,128]{1,0:T(8,128)S(1)}, f32[72,128]{1,0:T(8,128)S(1)}, u32[]{:S(2)}, u32[]{:S(2)}) collective-permute-start(f32[72,128]{1,0:T(8,128)S(1)} %merge_y.1.s0), channel_id=1, source_target_pairs={{0,192},{8,200},{16,208},{24,216},{32,224},{40,232},{48,240},{56,2... | collective-permute-start | bytes 110600 | tf_op jit(solution)/shard_map/ppermute | solution.py:369
  16.2 0.6 collective-permute-start.6
  16.8 2.0 %short_attention.1 = (f32[3,64,128]{2,1,0:T(8,128)S(1)}, s32[16,128]{1,0:T(8,128)S(1)}, bf16[16,256]{1,0:T(8,128)(2,1)S(1)}, f32[1,256]{1,0:T(1,128)S(1)}) custom-call(bf16[2,64,128]{2,1,0:T(8,128)(2,1)S(1)} %bitcast.20, bf16[2,8,256,128]{3,2,1,0:T(8,128)(2,1)S(1)} %bitcast.16, bf16[2,2,8,128]{3,2,1,0:T(8,128)(2,1)S(1)} %bitcast.21, s32[8]{0:T(128)} %targets_far.1, ...), custom_call_target="tpu_custom_call" | custom-call | bytes 1048576 | tf_op jit(solution)/shard_map/short_attention/pallas_call | solution.py:310
  18.9 0.0 collective-permute-done.5.s2
  18.9 1.8 %collective-permute-done.6.s3 = f32[72,128]{1,0:T(8,128)S(1)} collective-permute-done((f32[72,128]{1,0:T(8,128)S(1)}, f32[72,128]{1,0:T(8,128)S(1)}, u32[]{:S(2)}, u32[]{:S(2)}) %collective-permute-start.6) | collective-permute-done | bytes 36896 | tf_op jit(solution)/shard_map/ppermute | solution.py:369
  20.7 0.5 project.1
  21.2 15.9 %all_to_all.15.parts = f32[8,16,256]{2,1,0:T(8,128)S(1)} all-to-all(f32[8,16,256]{2,1,0:T(8,128)S(1)} %project.1), channel_id=1, replica_groups=mesh['ctx'=32,'tp'=8] {'tp'}, dimensions={0} | all-to-all | bytes 262144 | tf_op jit(solution)/shard_map/all_to_all | solution.py:404
  37.1 1.3 %head_other.1 = (f32[16,16,512]{2,1,0:T(8,128)S(1)}, bf16[16,256]{1,0:T(8,128)(2,1)S(1)}, f32[16,128]{1,0:T(8,128)S(1)}) custom-call(f32[8,16,256]{2,1,0:T(8,128)S(1)} %all_to_all.15.parts, bf16[16,256]{1,0:T(8,128)(2,1)S(1)} %get-tuple-element.19.residual, f32[1,256]{1,0:T(1,128)S(1)} %get-tuple-element.20.gain, bf16[16032,256]{1,0:T(8,128)(2,1)S(1)} %bitcast.14), custom_call_target="tpu_custom_call" | custom-call | bytes 4194304 | tf_op jit(solution)/shard_map/head_other/pallas_call | solution.py:310
  38.4 5.1 %collective-permute-start.7 = (f32[16,16,512]{2,1,0:T(8,128)S(1)}, f32[16,16,512]{2,1,0:T(8,128)S(1)}, u32[]{:S(2)}, u32[]{:S(2)}) collective-permute-start(f32[16,16,512]{2,1,0:T(8,128)S(1)} %get-tuple-element.23), channel_id=1, source_target_pairs={{0,8},{8,0},{16,24},{24,16},{32,40},{40,32},{48,56},{56,48},{64,72... | collective-permute-start | bytes 1572872 | tf_op jit(solution)/shard_map/ppermute | solution.py:413
  43.5 1.3 %head_same.1.one = f32[16,16,512]{2,1,0:T(8,128)S(1)} custom-call(bf16[16,256]{1,0:T(8,128)(2,1)S(1)} %get-tuple-element.21.scaled, f32[16,128]{1,0:T(8,128)S(1)} %get-tuple-element.22.squares, bf16[16032,256]{1,0:T(8,128)(2,1)S(1)} %bitcast.15), custom_call_target="tpu_custom_call" | custom-call | bytes 4194304 | tf_op jit(solution)/shard_map/head_same/pallas_call | solution.py:310
  44.9 0.2 collective-permute-done.7.two
  45.1 0.1 add_cores.1
  45.1 13.1 %all_to_all.16.parts = f32[16,16,512]{2,1,0:T(8,128)S(1)} all-to-all(f32[16,16,512]{2,1,0:T(8,128)S(1)} %add_cores.1), channel_id=1, replica_groups={{0,16,32,48,64,80,96,112,128,144,160,176,192,208,224,240},{8,24,40,56,7..., dimensions={0} | all-to-all | bytes 1048576 | tf_op jit(solution)/shard_map/all_to_all | solution.py:424
  58.2 0.3 vocab_stats.1
  58.5 2.1 %collective-permute-start.8 = (f32[8,128]{1,0:T(8,128)S(1)}, f32[8,128]{1,0:T(8,128)S(1)}, u32[]{:S(2)}, u32[]{:S(2)}) collective-permute-start(f32[8,128]{1,0:T(8,128)S(1)} %get-tuple-element.24.one), channel_id=1, source_target_pairs={{0,8},{8,0},{16,24},{24,16},{32,40},{40,32},{48,56},{56,48},{64,72... | collective-permute-start | bytes 12296 | tf_op jit(solution)/shard_map/ppermute | solution.py:433
  60.5 0.8 %collective-permute-done.8.two = f32[8,128]{1,0:T(8,128)S(1)} collective-permute-done((f32[8,128]{1,0:T(8,128)S(1)}, f32[8,128]{1,0:T(8,128)S(1)}, u32[]{:S(2)}, u32[]{:S(2)}) %collective-permute-start.8) | collective-permute-done | bytes 4128 | tf_op jit(solution)/shard_map/ppermute | solution.py:433
  61.4 0.1 join_stats.1
  61.4 16.1 %all_to_all.17 = f32[128,1,128]{2,1,0:T(1,128)S(1)} all-to-all(f32[128,1,128]{2,1,0:T(1,128)S(1)} %bitcast.18), channel_id=1, replica_groups={{0,1,2,3,4,5,6,7,16,17,18,19,20,21,22,23,32,33,34,35,36,37,38,39,48,49,..., dimensions={0} | all-to-all | bytes 131072 | tf_op jit(solution)/shard_map/all_to_all | solution.py:441
  77.6 0.9 %scores.1 = (f32[8,501]{1,0:T(8,128)}, f32[1,8]{1,0:T(1,128)}) custom-call(f32[128,128]{1,0:T(8,128)S(1)} %bitcast.17, f32[16,512]{1,0:T(8,128)S(1)} %get-tuple-element.25.logits), custom_call_target="tpu_custom_call" | custom-call | tf_op jit(solution)/shard_map/scores/pallas_call | solution.py:310
  (13 shorter events, 0.1 us)
Async XLA Ops:
  2.9 4.2 %collective-permute-start = (f32[72,128]{1,0:T(8,128)S(1)}, f32[72,128]{1,0:T(8,128)S(1)}, u32[]{:S(2)}, u32[]{:S(2)}) collective-permute-start(f32[72,128]{1,0:T(8,128)S(1)} %long_attention.1.refs_0_), channel_id=1, source_target_pairs={{0,8},{8,0},{16,24},{24,16},{32,40},{40,32},{48,56},{56,48},{64,72... | collective-permute-start | bytes 110600 | tf_op jit(solution)/shard_map/ppermute | solution.py:366
  7.1 9.7 %copy-start = (bf16[2,8,256,1,128]{4,2,3,1,0:T(8,128)(2,1)S(1)}, bf16[2,8,256,1,128]{4,2,3,1,0:T(8,128)(2,1)}, u32[]{:S(2)}) copy-start(bf16[2,8,256,1,128]{4,2,3,1,0:T(8,128)(2,1)} %param.13) | copy-start | bytes 3145732
  7.1 9.7 %copy-start.1 = (bf16[2,8,8,128]{3,2,1,0:T(8,128)(2,1)S(1)}, bf16[2,8,8,128]{3,2,1,0:T(8,128)(2,1)}, u32[]{:S(2)}) copy-start(bf16[2,8,8,128]{3,2,1,0:T(8,128)(2,1)} %param.10) | copy-start | bytes 98308
  7.1 9.7 %copy-start.2 = (bf16[2,2,8,1,128]{4,2,3,1,0:T(8,128)(2,1)S(1)}, bf16[2,2,8,1,128]{4,2,3,1,0:T(8,128)(2,1)}, u32[]{:S(2)}) copy-start(bf16[2,2,8,1,128]{4,2,3,1,0:T(8,128)(2,1)} %param.11) | copy-start | bytes 24580
  7.1 13.5 %copy-start.3 = (bf16[1024,256]{1,0:T(8,128)(2,1)S(1)}, bf16[1024,256]{1,0:T(8,128)(2,1)}, u32[]{:S(2)}) copy-start(bf16[1024,256]{1,0:T(8,128)(2,1)} %weight.1) | copy-start | bytes 1572868
  7.2 3.3 %collective-permute-start.1 = (f32[72,128]{1,0:T(8,128)S(1)}, f32[72,128]{1,0:T(8,128)S(1)}, u32[]{:S(2)}, u32[]{:S(2)}) collective-permute-start(f32[72,128]{1,0:T(8,128)S(1)} %merge_cores.1.refs_0_), channel_id=1, source_target_pairs={{0,16},{8,24},{16,0},{24,8},{32,48},{40,56},{48,32},{56,40},{64,80... | collective-permute-start | bytes 110600 | tf_op jit(solution)/shard_map/ppermute | solution.py:369
  7.3 4.1 %collective-permute-start.2 = (f32[72,128]{1,0:T(8,128)S(1)}, f32[72,128]{1,0:T(8,128)S(1)}, u32[]{:S(2)}, u32[]{:S(2)}) collective-permute-start(f32[72,128]{1,0:T(8,128)S(1)} %merge_cores.1.refs_0_), channel_id=1, source_target_pairs={{0,48},{8,56},{16,32},{24,40},{32,16},{40,24},{48,0},{56,8},{64,11... | collective-permute-start | bytes 110600 | tf_op jit(solution)/shard_map/ppermute | solution.py:369
  8.7 4.3 %collective-permute-start.3 = (f32[72,128]{1,0:T(8,128)S(1)}, f32[72,128]{1,0:T(8,128)S(1)}, u32[]{:S(2)}, u32[]{:S(2)}) collective-permute-start(f32[72,128]{1,0:T(8,128)S(1)} %merge_cores.1.refs_0_), channel_id=1, source_target_pairs={{0,32},{8,40},{16,48},{24,56},{32,0},{40,8},{48,16},{56,24},{64,96... | collective-permute-start | bytes 110600 | tf_op jit(solution)/shard_map/ppermute | solution.py:369
  13.0 24.1 %slice-start = ((s8[8208384]{0:T(1024)(128)(4,1)}), s8[4194304]{0:T(1024)(128)(4,1)S(1)}, s32[]{:S(2)}) async-start(s8[8208384]{0:T(1024)(128)(4,1)} %bitcast.12), calls=%async_computation.3 | async-start | bytes 8388608
  13.1 5.8 %collective-permute-start.4 = (f32[72,128]{1,0:T(8,128)S(1)}, f32[72,128]{1,0:T(8,128)S(1)}, u32[]{:S(2)}, u32[]{:S(2)}) collective-permute-start(f32[72,128]{1,0:T(8,128)S(1)} %merge_y.1.s0), channel_id=1, source_target_pairs={{0,64},{8,72},{16,80},{24,88},{32,96},{40,104},{48,112},{56,120},{... | collective-permute-start | bytes 110600 | tf_op jit(solution)/shard_map/ppermute | solution.py:369
  14.4 4.5 %collective-permute-start.5 = (f32[72,128]{1,0:T(8,128)S(1)}, f32[72,128]{1,0:T(8,128)S(1)}, u32[]{:S(2)}, u32[]{:S(2)}) collective-permute-start(f32[72,128]{1,0:T(8,128)S(1)} %merge_y.1.s0), channel_id=1, source_target_pairs={{0,192},{8,200},{16,208},{24,216},{32,224},{40,232},{48,240},{56,2... | collective-permute-start | bytes 110600 | tf_op jit(solution)/shard_map/ppermute | solution.py:369
  16.2 4.5 %collective-permute-start.6 = (f32[72,128]{1,0:T(8,128)S(1)}, f32[72,128]{1,0:T(8,128)S(1)}, u32[]{:S(2)}, u32[]{:S(2)}) collective-permute-start(f32[72,128]{1,0:T(8,128)S(1)} %merge_y.1.s0), channel_id=1, source_target_pairs={{0,128},{8,136},{16,144},{24,152},{32,160},{40,168},{48,176},{56,1... | collective-permute-start | bytes 110600 | tf_op jit(solution)/shard_map/ppermute | solution.py:369
  16.8 20.3 %slice-start.1 = ((s8[8208384]{0:T(1024)(128)(4,1)}), s8[4014080]{0:T(1024)(128)(4,1)S(1)}, s32[]{:S(2)}) async-start(s8[8208384]{0:T(1024)(128)(4,1)} %bitcast.12), calls=%async_computation.4 | async-start | bytes 8028160
  38.4 6.6 %collective-permute-start.7 = (f32[16,16,512]{2,1,0:T(8,128)S(1)}, f32[16,16,512]{2,1,0:T(8,128)S(1)}, u32[]{:S(2)}, u32[]{:S(2)}) collective-permute-start(f32[16,16,512]{2,1,0:T(8,128)S(1)} %get-tuple-element.23), channel_id=1, source_target_pairs={{0,8},{8,0},{16,24},{24,16},{32,40},{40,32},{48,56},{56,48},{64,72... | collective-permute-start | bytes 1572872 | tf_op jit(solution)/shard_map/ppermute | solution.py:413
  58.5 2.9 %collective-permute-start.8 = (f32[8,128]{1,0:T(8,128)S(1)}, f32[8,128]{1,0:T(8,128)S(1)}, u32[]{:S(2)}, u32[]{:S(2)}) collective-permute-start(f32[8,128]{1,0:T(8,128)S(1)} %get-tuple-element.24.one), channel_id=1, source_target_pairs={{0,8},{8,0},{16,24},{24,16},{32,40},{40,32},{48,56},{56,48},{64,72... | collective-permute-start | bytes 12296 | tf_op jit(solution)/shard_map/ppermute | solution.py:433
